TPU v7x, 512 devices: a whole 4x8x8 slice. The times are simulated.
512 devices in a mesh: tm: 8 (over y), acct: 64 (over z, x, core).
Axes of the slice: x: 4, y: 8, z: 8, core: 2. Of those that a mesh axis runs over, the one named last changes fastest.
Arguments:
- features: bfloat16 [8, 8192, 256], P('tm', 'acct'), may hold values from -6 to 6
- nbr_owner: int32 [8, 65536, 1], P('tm', 'acct'), may hold values from 0 to 63; in each aligned block of 1024 rows (0 to 1023, 1024 to 2047, ..., all dimensions but the last counted through in order) at most 20 rows name the same one
- nbr_row: int32 [8, 65536], P('tm', 'acct'), may hold values from 0 to 127
- counts: int32 [8, 8192], P('tm', 'acct'), may hold values from 1 to 8
- weight_one: bfloat16 [256, 256], replicated, may hold values from -0.375 to 0.375
- weight_two: bfloat16 [256, 256], replicated, may hold values from -0.375 to 0.375
- w_in: bfloat16 [256, 1024], replicated, may hold values from -0.375 to 0.375
- w_rec: bfloat16 [256, 1024], replicated, may hold values from -0.375 to 0.375
- gate_bias: float32 [1024], replicated, may hold values from -1 to 3
- cotangent: bfloat16 [8, 8192, 256], P('tm', 'acct'), may hold values from -6 to 6
Outputs:
- hidden: bfloat16 [8, 8192, 256], P('tm', 'acct')
- grad_gates: bfloat16 [8, 8192, 1024], P('tm', 'acct')
Inputs may be any that keep to these rules, and one draw needn't show every extreme that they name: `nbr_owner`: in each aligned block of 1024 rows of one snapshot, no shard is named more than 20 times, a bound that some block reaches.
All inputs are finite; a program needn't handle non-finite values.
Results may differ from a plain program's by a relative error of at most 0.014.
Values may be sent and summed in bfloat16 or wider, within the bound.
No kernel may reach another device: no remote copies, remote signals or barrier semaphores. Data moves between devices by JAX's collectives and lax.ppermute only.
A program may use at most 64 MiB of HBM per device.

v0:
```python
import jax
import jax.numpy as jnp
from jax import lax
from jax.sharding import PartitionSpec as P

H = 256
KNB = 8


def for_sending(array):
    return jax.tree.map(lambda a: a.astype(jnp.bfloat16) if a.dtype == jnp.float32 else a, array)


def from_behind(array, axis, by):
    size = lax.axis_size(axis)
    pairs = [(i, i + by) for i in range(size) if 0 <= i + by < size]
    return lax.ppermute(array, axis, pairs)


def cell(z, h_prev, c_prev, w_rec):
    gates = z.astype(jnp.float32) + jnp.dot(h_prev, w_rec, preferred_element_type=jnp.float32)
    gate_i = jax.nn.sigmoid(gates[:, :H])
    gate_f = jax.nn.sigmoid(gates[:, H : 2 * H])
    gate_g = jnp.tanh(gates[:, 2 * H : 3 * H])
    gate_o = jax.nn.sigmoid(gates[:, 3 * H :])
    cell_new = gate_f * c_prev + gate_i * gate_g
    return ((gate_o * jnp.tanh(cell_new)).astype(jnp.bfloat16), cell_new)


def backstep(z, h_prev, c_prev, grad_h, grad_c, w_rec):
    gates = z.astype(jnp.float32) + jnp.dot(h_prev, w_rec, preferred_element_type=jnp.float32)
    gate_i = jax.nn.sigmoid(gates[:, :H])
    gate_f = jax.nn.sigmoid(gates[:, H : 2 * H])
    gate_g = jnp.tanh(gates[:, 2 * H : 3 * H])
    gate_o = jax.nn.sigmoid(gates[:, 3 * H :])
    cell_new = gate_f * c_prev + gate_i * gate_g
    tanh_c = jnp.tanh(cell_new)
    grad_o = grad_h * tanh_c
    total_c = grad_c + grad_h * gate_o * (1.0 - tanh_c * tanh_c)
    pieces = [
        total_c * gate_g * gate_i * (1.0 - gate_i),
        total_c * c_prev * gate_f * (1.0 - gate_f),
        total_c * gate_i * (1.0 - gate_g * gate_g),
        grad_o * gate_o * (1.0 - gate_o),
    ]
    grad_g = jnp.concatenate(pieces, 1).astype(jnp.bfloat16)
    grad_hp = jnp.einsum("ng,hg->nh", grad_g, w_rec, preferred_element_type=jnp.float32)
    return (grad_g, grad_hp, total_c * gate_f)


def convolve(x, asked, slots, mask, scale, weight):
    n_local = x.shape[0]
    outgoing = x[asked]
    arrived = lax.all_to_all(outgoing, "acct", split_axis=0, concat_axis=0, tiled=True)
    picked = arrived.reshape(-1, H)[slots].reshape(n_local, KNB, H).astype(jnp.float32)
    summed = x.astype(jnp.float32) + jnp.sum(picked * mask[:, :, None], 1)
    agg = (summed * scale[:, None]).astype(jnp.bfloat16)
    return jax.nn.relu(jnp.dot(agg, weight, preferred_element_type=jnp.float32)).astype(
        jnp.bfloat16
    )


def shards(
    features, nbr_owner, nbr_row, counts, weight_one, weight_two, w_in, w_rec, gate_bias, cotangent
):
    x_local = features[0]
    n_local = x_local.shape[0]
    n_shards = lax.axis_size("acct")
    n_snaps = lax.axis_size("tm")
    capacity = max(2, n_local * KNB * 5 // (4 * n_shards))
    owners = nbr_owner[0, :, 0]
    onehot = (owners[:, None] == jnp.arange(n_shards, dtype=jnp.int32)[None, :]).astype(jnp.int32)
    ranks = jnp.sum((jnp.cumsum(onehot, 0) - 1) * onehot, 1)
    slots = owners * capacity + ranks
    wanted = (
        jnp.zeros((n_shards * capacity,), jnp.int32)
        .at[slots]
        .set(nbr_row[0])
        .reshape(n_shards, capacity)
    )
    asked = lax.all_to_all(wanted, "acct", split_axis=0, concat_axis=0, tiled=True)
    cnt = counts[0]
    mask = (jnp.arange(KNB, dtype=jnp.int32)[None, :] < cnt[:, None]).astype(jnp.float32)
    scale = 1.0 / (cnt.astype(jnp.float32) + 1.0)
    current = x_local
    for weight in (weight_one, weight_two):
        current = convolve(current, asked, slots, mask, scale, weight)
    z_mine = (jnp.dot(current, w_in, preferred_element_type=jnp.float32) + gate_bias).astype(
        jnp.bfloat16
    )
    cot_mine = cotangent[0]
    zero_state = jnp.zeros((n_local, H), jnp.float32)
    h_prev = zero_state.astype(jnp.bfloat16)
    c_prev = zero_state
    h_out, c_out = cell(z_mine, h_prev, c_prev, w_rec)
    for turn in range(n_snaps - 1):
        incoming = from_behind(for_sending(jnp.stack([h_out.astype(jnp.float32), c_out])), "tm", 1)
        h_prev = incoming[0].astype(jnp.bfloat16)
        c_prev = incoming[1]
        h_out, c_out = cell(z_mine, h_prev, c_prev, w_rec)
    cot_f = cot_mine.astype(jnp.float32)
    grad_g, grad_hp, grad_cp = backstep(z_mine, h_prev, c_prev, cot_f, zero_state, w_rec)
    for turn in range(n_snaps - 1):
        returned = from_behind(for_sending(jnp.stack([grad_hp, grad_cp])), "tm", -1)
        grad_g, grad_hp, grad_cp = backstep(
            z_mine, h_prev, c_prev, cot_f + returned[0], returned[1], w_rec
        )
    return (h_out[None], grad_g[None])


def solution(mesh):
    return jax.shard_map(
        shards,
        mesh=mesh,
        in_specs=(
            P("tm", "acct", None),
            P("tm", "acct", None),
            P("tm", "acct"),
            P("tm", "acct"),
            P(),
            P(),
            P(),
            P(),
            P(),
            P("tm", "acct", None),
        ),
        out_specs=(P("tm", "acct", None), P("tm", "acct", None)),
        check_vma=False,
    )
```

profile of v0, /device:TPU:26, one launch (start us, length us, event | category | flops | bytes accessed | tf_op | source)
XLA Modules:
  0.0 255.5 jit_solution(15059055480149700301)
XLA Ops:
  0.6 0.8 fusion.63
  1.4 18.0 %reduce-window.6 = s32[64,8,128]{2,1,0:T(8,128)S(1)} reduce-window(s32[64,8,128]{2,1,0:T(8,128)S(1)} %fusion.63, s32[]{:T(128)} %constant.9.clone.1), window={size=1x1x128 pad=0_0x0_0x127_0}, to_apply=%region_0.0 | reduce-window | flops 8323072 | bytes 524292 | tf_op jit(solution)/shard_map/reduce-window
  20.0 0.5 copy-done.8
  20.6 4.5 %scatter_custom_fusion = s32[1280]{0:T(1024)S(1)} fusion(s32[1024]{0:T(1024)S(1)} %bitcast.357, s32[1024]{0:T(1024)} %bitcast.360, s32[]{:T(128)} %constant.9.clone.1), kind=kCustom, calls=%fused_computation.401 | custom fusion | bytes 5632 | tf_op jit(solution)/shard_map/scatter | solution.py:78
  25.2 22.3 %all_to_all.22 = s32[64,1,20]{2,1,0:T(1,128)S(1)} all-to-all(s32[64,1,20]{2,1,0:T(1,128)S(1)} %bitcast.351), channel_id=1, replica_groups=mesh['tm'=8,'acct'=64] {'acct'}, dimensions={0} | all-to-all | bytes 10240 | tf_op jit(solution)/shard_map/all_to_all | solution.py:81
  47.6 0.7 copy-done.1
  48.3 4.0 %gather_fusion = bf16[1280,256]{1,0:T(8,128)(2,1)S(1)} fusion(bf16[128,256]{1,0:T(8,128)(2,1)S(1)} %bitcast.342, s32[2048]{0:T(1024)S(1)} %pad_clamp_fusion), kind=kCustom, calls=%fused_computation | custom fusion | bytes 1315840 | tf_op jit(solution)/shard_map/gather | solution.py:53
  52.4 1.0 reshape.259
  53.4 5.7 %all-to-all-start.1 = ((bf16[64,20,256]{2,1,0:T(8,128)(2,1)}), bf16[64,20,256]{2,1,0:T(8,128)(2,1)S(1)}, u32[]{:S(2)}, u32[]{:S(2)}) async-start(bf16[64,20,256]{2,1,0:T(8,128)(2,1)} %reshape.259), calls=%async_computation.1 | async-start | bytes 1572864 | tf_op jit(solution)/shard_map/all_to_all | solution.py:54
  59.2 23.2 %all-to-all-done.1 = bf16[64,20,256]{2,1,0:T(8,128)(2,1)S(1)} async-done(((bf16[64,20,256]{2,1,0:T(8,128)(2,1)}), bf16[64,20,256]{2,1,0:T(8,128)(2,1)S(1)}, u32[]{:S(2)}, u32[]{:S(2)}) %all-to-all-start.1) | async-done | bytes 655392 | tf_op jit(solution)/shard_map/all_to_all | solution.py:54
  82.5 3.9 %gather_fusion.1 = bf16[1024,256]{1,0:T(8,128)(2,1)S(1)} fusion(bf16[1280,256]{1,0:T(8,128)(2,1)S(1)} %reshape.232, s32[1024]{0:T(1024)S(1)} %broadcast_clamp_fusion), kind=kCustom, calls=%fused_computation.1 | custom fusion | bytes 1052672 | tf_op jit(solution)/shard_map/gather | solution.py:55
  86.5 0.4 fusion.11
  86.8 0.5 copy-done.6
  87.6 4.1 %gather_fusion.2 = bf16[1280,256]{1,0:T(8,128)(2,1)S(1)} fusion(bf16[128,256]{1,0:T(8,128)(2,1)S(1)} %fusion.1, s32[2048]{0:T(1024)S(1)} %pad_clamp_fusion), kind=kCustom, calls=%fused_computation.2 | custom fusion | bytes 1315840 | tf_op jit(solution)/shard_map/gather | solution.py:53
  91.8 28.8 %all_to_all.23 = bf16[64,20,256]{2,1,0:T(8,128)(2,1)S(1)} all-to-all(bf16[64,20,256]{2,1,0:T(8,128)(2,1)S(1)} %reshape.275), channel_id=1, replica_groups=mesh['tm'=8,'acct'=64] {'acct'}, dimensions={0} | all-to-all | bytes 1310720 | tf_op jit(solution)/shard_map/all_to_all | solution.py:54
  120.7 3.9 %gather_fusion.3 = bf16[1024,256]{1,0:T(8,128)(2,1)S(1)} fusion(bf16[1280,256]{1,0:T(8,128)(2,1)S(1)} %reshape.233, s32[1024]{0:T(1024)S(1)} %broadcast_clamp_fusion), kind=kCustom, calls=%fused_computation.3 | custom fusion | bytes 1052672 | tf_op jit(solution)/shard_map/gather | solution.py:55
  124.7 0.4 fusion.10
  125.1 0.6 copy-done.5
  125.7 0.4 fusion
  126.1 0.2 convert_add_fusion.7
  126.5 4.7 %collective-permute-start = (bf16[2,128,256]{2,1,0:T(8,128)(2,1)S(1)}, bf16[2,128,256]{2,1,0:T(8,128)(2,1)S(1)}, u32[]{:S(2)}, u32[]{:S(2)}) collective-permute-start(bf16[2,128,256]{2,1,0:T(8,128)(2,1)S(1)} %pad_maximum_fusion.1), channel_id=1, source_target_pairs={{0,64},{64,128},{128,192},{192,256},{256,320},{320,384},{384,448},... | collective-permute-start | bytes 393224 | tf_op jit(solution)/shard_map/ppermute | solution.py:17
  131.3 2.5 collective-permute-done
  134.2 5.6 %collective-permute-start.1 = (bf16[2,128,256]{2,1,0:T(8,128)(2,1)S(1)}, bf16[2,128,256]{2,1,0:T(8,128)(2,1)S(1)}, u32[]{:S(2)}, u32[]{:S(2)}) collective-permute-start(bf16[2,128,256]{2,1,0:T(8,128)(2,1)S(1)} %pad_maximum_fusion.2), channel_id=1, source_target_pairs={{0,64},{64,128},{128,192},{192,256},{256,320},{320,384},{384,448},... | collective-permute-start | bytes 393224 | tf_op jit(solution)/shard_map/ppermute | solution.py:17
  139.7 2.5 collective-permute-done.1
  142.7 5.6 %collective-permute-start.2 = (bf16[2,128,256]{2,1,0:T(8,128)(2,1)S(1)}, bf16[2,128,256]{2,1,0:T(8,128)(2,1)S(1)}, u32[]{:S(2)}, u32[]{:S(2)}) collective-permute-start(bf16[2,128,256]{2,1,0:T(8,128)(2,1)S(1)} %pad_maximum_fusion.3), channel_id=1, source_target_pairs={{0,64},{64,128},{128,192},{192,256},{256,320},{320,384},{384,448},... | collective-permute-start | bytes 393224 | tf_op jit(solution)/shard_map/ppermute | solution.py:17
  148.2 2.5 collective-permute-done.2
  150.7 0.2 convert_add_fusion.4
  151.2 5.6 %collective-permute-start.3 = (bf16[2,128,256]{2,1,0:T(8,128)(2,1)S(1)}, bf16[2,128,256]{2,1,0:T(8,128)(2,1)S(1)}, u32[]{:S(2)}, u32[]{:S(2)}) collective-permute-start(bf16[2,128,256]{2,1,0:T(8,128)(2,1)S(1)} %pad_maximum_fusion.4), channel_id=1, source_target_pairs={{0,64},{64,128},{128,192},{192,256},{256,320},{320,384},{384,448},... | collective-permute-start | bytes 393224 | tf_op jit(solution)/shard_map/ppermute | solution.py:17
  156.7 2.5 collective-permute-done.3
  159.7 5.6 %collective-permute-start.4 = (bf16[2,128,256]{2,1,0:T(8,128)(2,1)S(1)}, bf16[2,128,256]{2,1,0:T(8,128)(2,1)S(1)}, u32[]{:S(2)}, u32[]{:S(2)}) collective-permute-start(bf16[2,128,256]{2,1,0:T(8,128)(2,1)S(1)} %pad_maximum_fusion.5), channel_id=1, source_target_pairs={{0,64},{64,128},{128,192},{192,256},{256,320},{320,384},{384,448},... | collective-permute-start | bytes 393224 | tf_op jit(solution)/shard_map/ppermute | solution.py:17
  165.2 2.8 %collective-permute-done.4 = bf16[2,128,256]{2,1,0:T(8,128)(2,1)S(1)} collective-permute-done((bf16[2,128,256]{2,1,0:T(8,128)(2,1)S(1)}, bf16[2,128,256]{2,1,0:T(8,128)(2,1)S(1)}, u32[]{:S(2)}, u32[]{:S(2)}) %collective-permute-start.4) | collective-permute-done | bytes 131104 | tf_op jit(solution)/shard_map/ppermute | solution.py:17
  168.5 5.6 %collective-permute-start.5 = (bf16[2,128,256]{2,1,0:T(8,128)(2,1)S(1)}, bf16[2,128,256]{2,1,0:T(8,128)(2,1)S(1)}, u32[]{:S(2)}, u32[]{:S(2)}) collective-permute-start(bf16[2,128,256]{2,1,0:T(8,128)(2,1)S(1)} %pad_maximum_fusion.6), channel_id=1, source_target_pairs={{0,64},{64,128},{128,192},{192,256},{256,320},{320,384},{384,448},... | collective-permute-start | bytes 393224 | tf_op jit(solution)/shard_map/ppermute | solution.py:17
  174.1 3.8 %collective-permute-done.5 = bf16[2,128,256]{2,1,0:T(8,128)(2,1)S(1)} collective-permute-done((bf16[2,128,256]{2,1,0:T(8,128)(2,1)S(1)}, bf16[2,128,256]{2,1,0:T(8,128)(2,1)S(1)}, u32[]{:S(2)}, u32[]{:S(2)}) %collective-permute-start.5) | collective-permute-done | bytes 131104 | tf_op jit(solution)/shard_map/ppermute | solution.py:17
  178.4 5.9 %collective-permute-start.6 = (bf16[2,128,256]{2,1,0:T(8,128)(2,1)S(1)}, bf16[2,128,256]{2,1,0:T(8,128)(2,1)S(1)}, u32[]{:S(2)}, u32[]{:S(2)}) collective-permute-start(bf16[2,128,256]{2,1,0:T(8,128)(2,1)S(1)} %pad_maximum_fusion.7), channel_id=1, source_target_pairs={{0,64},{64,128},{128,192},{192,256},{256,320},{320,384},{384,448},... | collective-permute-start | bytes 393224 | tf_op jit(solution)/shard_map/ppermute | solution.py:17
  184.3 2.3 collective-permute-done.6
  187.5 0.3 fusion.3
  187.8 1.9 collective-permute-start.7
  189.7 7.1 %collective-permute-done.7 = bf16[2,128,256]{2,1,0:T(8,128)(2,1)S(1)} collective-permute-done((bf16[2,128,256]{2,1,0:T(8,128)(2,1)S(1)}, bf16[2,128,256]{2,1,0:T(8,128)(2,1)S(1)}, u32[]{:S(2)}, u32[]{:S(2)}) %collective-permute-start.7) | collective-permute-done | bytes 131104 | tf_op jit(solution)/shard_map/ppermute | solution.py:17
  197.0 0.9 fusion.71
  197.9 0.3 fusion.4
  198.2 1.9 collective-permute-start.8
  200.2 6.1 %collective-permute-done.8 = bf16[2,128,256]{2,1,0:T(8,128)(2,1)S(1)} collective-permute-done((bf16[2,128,256]{2,1,0:T(8,128)(2,1)S(1)}, bf16[2,128,256]{2,1,0:T(8,128)(2,1)S(1)}, u32[]{:S(2)}, u32[]{:S(2)}) %collective-permute-start.8) | collective-permute-done | bytes 131104 | tf_op jit(solution)/shard_map/ppermute | solution.py:17
  206.5 0.9 fusion.74
  207.4 0.3 fusion.5
  207.7 1.9 collective-permute-start.9
  209.7 6.1 %collective-permute-done.9 = bf16[2,128,256]{2,1,0:T(8,128)(2,1)S(1)} collective-permute-done((bf16[2,128,256]{2,1,0:T(8,128)(2,1)S(1)}, bf16[2,128,256]{2,1,0:T(8,128)(2,1)S(1)}, u32[]{:S(2)}, u32[]{:S(2)}) %collective-permute-start.9) | collective-permute-done | bytes 131104 | tf_op jit(solution)/shard_map/ppermute | solution.py:17
  215.9 0.9 fusion.77
  216.9 0.3 fusion.6
  217.2 1.9 collective-permute-start.10
  219.2 6.1 %collective-permute-done.10 = bf16[2,128,256]{2,1,0:T(8,128)(2,1)S(1)} collective-permute-done((bf16[2,128,256]{2,1,0:T(8,128)(2,1)S(1)}, bf16[2,128,256]{2,1,0:T(8,128)(2,1)S(1)}, u32[]{:S(2)}, u32[]{:S(2)}) %collective-permute-start.10) | collective-permute-done | bytes 131104 | tf_op jit(solution)/shard_map/ppermute | solution.py:17
  225.4 0.9 fusion.80
  226.4 0.3 fusion.7
  226.7 1.9 collective-permute-start.11
  228.7 6.1 %collective-permute-done.11 = bf16[2,128,256]{2,1,0:T(8,128)(2,1)S(1)} collective-permute-done((bf16[2,128,256]{2,1,0:T(8,128)(2,1)S(1)}, bf16[2,128,256]{2,1,0:T(8,128)(2,1)S(1)}, u32[]{:S(2)}, u32[]{:S(2)}) %collective-permute-start.11) | collective-permute-done | bytes 131104 | tf_op jit(solution)/shard_map/ppermute | solution.py:17
  234.9 0.9 fusion.83
  235.9 0.3 fusion.8
  236.2 1.9 collective-permute-start.12
  238.1 6.1 %collective-permute-done.12 = bf16[2,128,256]{2,1,0:T(8,128)(2,1)S(1)} collective-permute-done((bf16[2,128,256]{2,1,0:T(8,128)(2,1)S(1)}, bf16[2,128,256]{2,1,0:T(8,128)(2,1)S(1)}, u32[]{:S(2)}, u32[]{:S(2)}) %collective-permute-start.12) | collective-permute-done | bytes 131104 | tf_op jit(solution)/shard_map/ppermute | solution.py:17
  244.4 0.9 fusion.86
  245.4 0.3 fusion.9
  245.7 2.1 collective-permute-start.13
  247.8 6.1 %collective-permute-done.13 = bf16[2,128,256]{2,1,0:T(8,128)(2,1)S(1)} collective-permute-done((bf16[2,128,256]{2,1,0:T(8,128)(2,1)S(1)}, bf16[2,128,256]{2,1,0:T(8,128)(2,1)S(1)}, u32[]{:S(2)}, u32[]{:S(2)}) %collective-permute-start.13) | collective-permute-done | bytes 131104 | tf_op jit(solution)/shard_map/ppermute | solution.py:17
  253.9 0.8 fusion.209
  254.8 0.7 pad_maximum_fusion
  (73 shorter events, 5.7 us)
Async XLA Ops:
  0.6 125.5 %copy-start = (bf16[256,1024]{1,0:T(8,128)(2,1)S(1)}, bf16[256,1024]{1,0:T(8,128)(2,1)}, u32[]{:S(2)}) copy-start(bf16[256,1024]{1,0:T(8,128)(2,1)} %param.17) | copy-start | bytes 1572868
  19.8 0.7 copy-start.8
  47.5 0.8 copy-start.1
  53.4 5.7 %copy-start.10 = (s32[1,128]{1,0:T(1,128)S(1)}, s32[1,128]{1,0:T(1,128)}, u32[]{:S(2)}) copy-start(s32[1,128]{1,0:T(1,128)} %param.13) | copy-start | bytes 1540
  53.4 29.0 %all-to-all-start.1 = ((bf16[64,20,256]{2,1,0:T(8,128)(2,1)}), bf16[64,20,256]{2,1,0:T(8,128)(2,1)S(1)}, u32[]{:S(2)}, u32[]{:S(2)}) async-start(bf16[64,20,256]{2,1,0:T(8,128)(2,1)} %reshape.259), calls=%async_computation.1 | async-start | bytes 1572864 | tf_op jit(solution)/shard_map/all_to_all | solution.py:54
  86.4 0.9 copy-start.6
  124.6 1.0 copy-start.5
  124.7 1.1 copy-start.7
  124.7 1.0 copy-start.9
  126.5 7.2 %collective-permute-start = (bf16[2,128,256]{2,1,0:T(8,128)(2,1)S(1)}, bf16[2,128,256]{2,1,0:T(8,128)(2,1)S(1)}, u32[]{:S(2)}, u32[]{:S(2)}) collective-permute-start(bf16[2,128,256]{2,1,0:T(8,128)(2,1)S(1)} %pad_maximum_fusion.1), channel_id=1, source_target_pairs={{0,64},{64,128},{128,192},{192,256},{256,320},{320,384},{384,448},... | collective-permute-start | bytes 393224 | tf_op jit(solution)/shard_map/ppermute | solution.py:17
  134.2 8.1 %collective-permute-start.1 = (bf16[2,128,256]{2,1,0:T(8,128)(2,1)S(1)}, bf16[2,128,256]{2,1,0:T(8,128)(2,1)S(1)}, u32[]{:S(2)}, u32[]{:S(2)}) collective-permute-start(bf16[2,128,256]{2,1,0:T(8,128)(2,1)S(1)} %pad_maximum_fusion.2), channel_id=1, source_target_pairs={{0,64},{64,128},{128,192},{192,256},{256,320},{320,384},{384,448},... | collective-permute-start | bytes 393224 | tf_op jit(solution)/shard_map/ppermute | solution.py:17
  142.7 8.1 %collective-permute-start.2 = (bf16[2,128,256]{2,1,0:T(8,128)(2,1)S(1)}, bf16[2,128,256]{2,1,0:T(8,128)(2,1)S(1)}, u32[]{:S(2)}, u32[]{:S(2)}) collective-permute-start(bf16[2,128,256]{2,1,0:T(8,128)(2,1)S(1)} %pad_maximum_fusion.3), channel_id=1, source_target_pairs={{0,64},{64,128},{128,192},{192,256},{256,320},{320,384},{384,448},... | collective-permute-start | bytes 393224 | tf_op jit(solution)/shard_map/ppermute | solution.py:17
  151.2 8.1 %collective-permute-start.3 = (bf16[2,128,256]{2,1,0:T(8,128)(2,1)S(1)}, bf16[2,128,256]{2,1,0:T(8,128)(2,1)S(1)}, u32[]{:S(2)}, u32[]{:S(2)}) collective-permute-start(bf16[2,128,256]{2,1,0:T(8,128)(2,1)S(1)} %pad_maximum_fusion.4), channel_id=1, source_target_pairs={{0,64},{64,128},{128,192},{192,256},{256,320},{320,384},{384,448},... | collective-permute-start | bytes 393224 | tf_op jit(solution)/shard_map/ppermute | solution.py:17
  159.7 8.4 %collective-permute-start.4 = (bf16[2,128,256]{2,1,0:T(8,128)(2,1)S(1)}, bf16[2,128,256]{2,1,0:T(8,128)(2,1)S(1)}, u32[]{:S(2)}, u32[]{:S(2)}) collective-permute-start(bf16[2,128,256]{2,1,0:T(8,128)(2,1)S(1)} %pad_maximum_fusion.5), channel_id=1, source_target_pairs={{0,64},{64,128},{128,192},{192,256},{256,320},{320,384},{384,448},... | collective-permute-start | bytes 393224 | tf_op jit(solution)/shard_map/ppermute | solution.py:17
  168.5 9.4 %collective-permute-start.5 = (bf16[2,128,256]{2,1,0:T(8,128)(2,1)S(1)}, bf16[2,128,256]{2,1,0:T(8,128)(2,1)S(1)}, u32[]{:S(2)}, u32[]{:S(2)}) collective-permute-start(bf16[2,128,256]{2,1,0:T(8,128)(2,1)S(1)} %pad_maximum_fusion.6), channel_id=1, source_target_pairs={{0,64},{64,128},{128,192},{192,256},{256,320},{320,384},{384,448},... | collective-permute-start | bytes 393224 | tf_op jit(solution)/shard_map/ppermute | solution.py:17
  178.4 8.5 %copy-start.2 = (bf16[1,128,256]{2,1,0:T(8,128)(2,1)S(1)}, bf16[1,128,256]{2,1,0:T(8,128)(2,1)}, u32[]{:S(2)}) copy-start(bf16[1,128,256]{2,1,0:T(8,128)(2,1)} %param.19) | copy-start | bytes 196612
  178.4 8.2 %collective-permute-start.6 = (bf16[2,128,256]{2,1,0:T(8,128)(2,1)S(1)}, bf16[2,128,256]{2,1,0:T(8,128)(2,1)S(1)}, u32[]{:S(2)}, u32[]{:S(2)}) collective-permute-start(bf16[2,128,256]{2,1,0:T(8,128)(2,1)S(1)} %pad_maximum_fusion.7), channel_id=1, source_target_pairs={{0,64},{64,128},{128,192},{192,256},{256,320},{320,384},{384,448},... | collective-permute-start | bytes 393224 | tf_op jit(solution)/shard_map/ppermute | solution.py:17
  186.6 0.7 copy-start.3
  187.8 9.0 %collective-permute-start.7 = (bf16[2,128,256]{2,1,0:T(8,128)(2,1)S(1)}, bf16[2,128,256]{2,1,0:T(8,128)(2,1)S(1)}, u32[]{:S(2)}, u32[]{:S(2)}) collective-permute-start(bf16[2,128,256]{2,1,0:T(8,128)(2,1)S(1)} %pad_maximum_fusion.8), channel_id=1, source_target_pairs={{64,0},{128,64},{192,128},{256,192},{320,256},{384,320},{448,384},... | collective-permute-start | bytes 393224 | tf_op jit(solution)/shard_map/ppermute | solution.py:17
  198.2 8.1 %collective-permute-start.8 = (bf16[2,128,256]{2,1,0:T(8,128)(2,1)S(1)}, bf16[2,128,256]{2,1,0:T(8,128)(2,1)S(1)}, u32[]{:S(2)}, u32[]{:S(2)}) collective-permute-start(bf16[2,128,256]{2,1,0:T(8,128)(2,1)S(1)} %pad_maximum_fusion.9), channel_id=1, source_target_pairs={{64,0},{128,64},{192,128},{256,192},{320,256},{384,320},{448,384},... | collective-permute-start | bytes 393224 | tf_op jit(solution)/shard_map/ppermute | solution.py:17
  207.7 8.1 %collective-permute-start.9 = (bf16[2,128,256]{2,1,0:T(8,128)(2,1)S(1)}, bf16[2,128,256]{2,1,0:T(8,128)(2,1)S(1)}, u32[]{:S(2)}, u32[]{:S(2)}) collective-permute-start(bf16[2,128,256]{2,1,0:T(8,128)(2,1)S(1)} %pad_maximum_fusion.10), channel_id=1, source_target_pairs={{64,0},{128,64},{192,128},{256,192},{320,256},{384,320},{448,384},... | collective-permute-start | bytes 393224 | tf_op jit(solution)/shard_map/ppermute | solution.py:17
  217.2 8.1 %collective-permute-start.10 = (bf16[2,128,256]{2,1,0:T(8,128)(2,1)S(1)}, bf16[2,128,256]{2,1,0:T(8,128)(2,1)S(1)}, u32[]{:S(2)}, u32[]{:S(2)}) collective-permute-start(bf16[2,128,256]{2,1,0:T(8,128)(2,1)S(1)} %pad_maximum_fusion.11), channel_id=1, source_target_pairs={{64,0},{128,64},{192,128},{256,192},{320,256},{384,320},{448,384},... | collective-permute-start | bytes 393224 | tf_op jit(solution)/shard_map/ppermute | solution.py:17
  226.7 8.1 %collective-permute-start.11 = (bf16[2,128,256]{2,1,0:T(8,128)(2,1)S(1)}, bf16[2,128,256]{2,1,0:T(8,128)(2,1)S(1)}, u32[]{:S(2)}, u32[]{:S(2)}) collective-permute-start(bf16[2,128,256]{2,1,0:T(8,128)(2,1)S(1)} %pad_maximum_fusion.12), channel_id=1, source_target_pairs={{64,0},{128,64},{192,128},{256,192},{320,256},{384,320},{448,384},... | collective-permute-start | bytes 393224 | tf_op jit(solution)/shard_map/ppermute | solution.py:17
  236.2 8.1 %collective-permute-start.12 = (bf16[2,128,256]{2,1,0:T(8,128)(2,1)S(1)}, bf16[2,128,256]{2,1,0:T(8,128)(2,1)S(1)}, u32[]{:S(2)}, u32[]{:S(2)}) collective-permute-start(bf16[2,128,256]{2,1,0:T(8,128)(2,1)S(1)} %pad_maximum_fusion.13), channel_id=1, source_target_pairs={{64,0},{128,64},{192,128},{256,192},{320,256},{384,320},{448,384},... | collective-permute-start | bytes 393224 | tf_op jit(solution)/shard_map/ppermute | solution.py:17
  245.7 9.0 %copy-start.4 = (bf16[2,128,256]{2,1,0:T(8,128)(2,1)S(1)}, bf16[2,128,256]{2,1,0:T(8,128)(2,1)}, u32[]{:S(2)}) copy-start(bf16[2,128,256]{2,1,0:T(8,128)(2,1)} %copy-done.3) | copy-start | bytes 393220
  245.7 8.2 %collective-permute-start.13 = (bf16[2,128,256]{2,1,0:T(8,128)(2,1)S(1)}, bf16[2,128,256]{2,1,0:T(8,128)(2,1)S(1)}, u32[]{:S(2)}, u32[]{:S(2)}) collective-permute-start(bf16[2,128,256]{2,1,0:T(8,128)(2,1)S(1)} %pad_maximum_fusion.14), channel_id=1, source_target_pairs={{64,0},{128,64},{192,128},{256,192},{320,256},{384,320},{448,384},... | collective-permute-start | bytes 393224 | tf_op jit(solution)/shard_map/ppermute | solution.py:17
where the time goes:
time: 257 us; the launch traced here: 256 us
  waiting for transfers between devices  86.1 us (34%)
  starting transfers between devices  57.7 us (22%)
  blocking collectives  51.1 us (20%)
  other arithmetic  29.5 us (11%)
  local copies, waits for them, and re-layouts  25.2 us (10%)
  matrix products  4.63 us (2%)
    ppermute x14, waiting for transfers between devices, from_behind(): return lax.ppermute(array, axis, pairs)  63 us
    ppermute x14, starting transfers between devices, from_behind(): return lax.ppermute(array, axis, pairs)  52 us
    all_to_all x1, blocking collectives, convolve(): lax.all_to_all(outgoing, 'acct', split_axis=0, concat_axis=0, tiled=True)  28.8 us
    another operation x16, other arithmetic  24.8 us
    all_to_all x1, waiting for transfers between devices, convolve(): lax.all_to_all(outgoing, 'acct', split_axis=0, concat_axis=0, tiled=True)  23.2 us
    all_to_all x1, blocking collectives, shards(): lax.all_to_all(wanted, 'acct', split_axis=0, concat_axis=0, tiled=True)  22.3 us
    gather x4, local copies, waits for them, and re-layouts, convolve(): outgoing = x[asked]  9.28 us
    gather x2, local copies, waits for them, and re-layouts, convolve(): arrived.reshape(-1, H)[slots].reshape(n_local, KNB, H).astype(jnp.float32)  7.88 us
  transfers between devices with their start and end apart: 15, of which 15 were waited for; matrix products, arithmetic and copies ran while one was open for 0% of the time, Pallas kernels for 0%

commit v1 on v0

v1 whole, which is shorter than its diff:
```python
import jax
import jax.numpy as jnp
from jax import lax
from jax.experimental import pallas as pl
from jax.experimental.pallas import tpu as pltpu
from jax.sharding import Mesh
from jax.sharding import PartitionSpec as P

H = 256
KNB = 8
NODE = 128
SNAPS = 8
CHIPS = 32
CAP = 40
LANES = 128
PART = NODE // SNAPS
SLOTS = CHIPS * CAP
VMEM = pltpu.CompilerParams(vmem_limit_bytes=32 * 1024 * 1024)
BF16 = jnp.bfloat16
F32 = jnp.float32


def iota(shape, dim):
    return lax.broadcasted_iota(jnp.int32, shape, dim)


def matmul(a, b, dims=((1,), (0,))):
    return lax.dot_general(a, b, (dims, ((), ())), preferred_element_type=F32)


NT = ((1,), (1,))


def plan_kernel(owner_ref, row_ref, cnt_ref, wanted_ref, comb_ref):
    owner = owner_ref[...]
    value = ((owner % 2) * NODE + row_ref[...]).astype(F32)
    chip = owner // 2
    upper = jnp.where(iota((LANES, LANES), 0) < iota((LANES, LANES), 1), 1.0, 0.0).astype(BF16)
    base = jnp.zeros((CHIPS, 1), F32)
    wanted = jnp.zeros((CHIPS, LANES), F32)
    where = jnp.zeros((NODE, 2 * KNB), F32)
    lane = iota((1, LANES), 1)
    for i in range(KNB):
        chip_i = chip[i : i + 1, :]
        onehot = jnp.where(iota((CHIPS, LANES), 0) == chip_i, 1.0, 0.0)
        before = matmul(onehot.astype(BF16), upper) + base
        base = base + jnp.sum(onehot, 1, keepdims=True)
        rank = jnp.sum(onehot * before, 0, keepdims=True)
        ranks = jnp.where(iota((LANES, LANES), 0).astype(F32) == rank, 1.0, 0.0).astype(BF16)
        wanted = wanted + matmul((onehot * value[i : i + 1, :]).astype(BF16), ranks, NT)
        group = jnp.where(iota((NODE, LANES), 0) == i * (LANES // KNB) + lane // KNB, 1.0, 0.0)
        sub = iota((2 * KNB, LANES), 0)
        coded = jnp.where(
            sub % KNB == lane % KNB, jnp.where(sub < KNB, chip_i.astype(F32), rank), 0.0
        )
        where = where + matmul(group.astype(BF16), coded.astype(BF16), NT)
    wanted_ref[...] = wanted
    eye = iota((NODE, NODE), 0) == iota((NODE, NODE), 1)
    count = jnp.sum(jnp.where(eye, cnt_ref[...].astype(F32), 0.0), 1, keepdims=True)
    place = where[:, :KNB] * CAP + where[:, KNB:]
    place = jnp.where(iota((NODE, KNB), 1).astype(F32) < count, place, -1.0)
    spot = iota((NODE, SLOTS), 1).astype(F32)
    comb = jnp.zeros((NODE, SLOTS), F32)
    for k in range(KNB):
        comb = comb + jnp.where(spot == place[:, k : k + 1], 1.0, 0.0)
    comb_ref[...] = comb.astype(BF16)


def pick_kernel(asked_ref, x_ref, pick_ref, out_ref):
    eye = jnp.where(iota((LANES, LANES), 0) == iota((LANES, LANES), 1), 1.0, 0.0).astype(BF16)
    turned = matmul(eye, asked_ref[...].astype(BF16), NT)
    col = iota((CAP, H), 1).astype(F32)
    x = x_ref[...]
    for d in range(0, CHIPS, 2):
        both = [jnp.where(turned[:CAP, e : e + 1] == col, 1.0, 0.0) for e in (d, d + 1)]
        pick = jnp.concatenate(both, 0).astype(BF16)
        pick_ref[d * CAP : (d + 2) * CAP, :] = pick
        out_ref[d * CAP : (d + 2) * CAP, :] = matmul(pick, x).astype(BF16)


def again_kernel(pick_ref, x_ref, out_ref):
    out_ref[...] = matmul(pick_ref[...], x_ref[...]).astype(BF16)


def conv_kernel(comb_ref, arrived_ref, x_ref, cnt_ref, weight_ref, out_ref):
    eye = iota((NODE, NODE), 0) == iota((NODE, NODE), 1)
    count = jnp.sum(jnp.where(eye, cnt_ref[...].astype(F32), 0.0), 1, keepdims=True)
    summed = x_ref[...].astype(F32) + matmul(comb_ref[...], arrived_ref[...])
    agg = (summed * (1.0 / (count + 1.0))).astype(BF16)
    out_ref[...] = jnp.maximum(matmul(agg, weight_ref[...]), 0.0).astype(BF16)


def lstm_kernel(xc_ref, w_in_ref, w_rec_ref, bias_ref, out_ref, z_ref, saved_ref):
    x = xc_ref[:, :, :H].reshape(NODE, H)
    z = matmul(x, w_in_ref[...]) + bias_ref[...]
    z_ref[...] = z.astype(BF16).astype(F32)
    h = None
    c = jnp.zeros((PART, H), F32)
    for t in range(SNAPS):
        gates = z_ref[t * PART : (t + 1) * PART, :]
        if t > 0:
            gates = gates + matmul(h, w_rec_ref[...])
        i = jax.nn.sigmoid(gates[:, :H])
        f = jax.nn.sigmoid(gates[:, H : 2 * H])
        g = jnp.tanh(gates[:, 2 * H : 3 * H])
        o = jax.nn.sigmoid(gates[:, 3 * H :])
        c_new = f * c + i * g
        tc = jnp.tanh(c_new)
        h = (o * tc).astype(BF16)
        out_ref[t, :, :H] = h
        saved_ref[t, 0] = f
        saved_ref[t, 1] = o * (1.0 - tc * tc)
        saved_ref[t, 2] = g * i * (1.0 - i)
        saved_ref[t, 3] = c * f * (1.0 - f)
        saved_ref[t, 4] = i * (1.0 - g * g)
        saved_ref[t, 5] = tc * o * (1.0 - o)
        c = c_new
    dh = jnp.zeros((PART, H), F32)
    dc = jnp.zeros((PART, H), F32)
    for t in range(SNAPS - 1, -1, -1):
        dh = dh + xc_ref[t, :, H:].astype(F32)
        dc = dc + dh * saved_ref[t, 1]
        grad = jnp.concatenate(
            [dc * saved_ref[t, 2], dc * saved_ref[t, 3], dc * saved_ref[t, 4], dh * saved_ref[t, 5]],
            1,
        ).astype(BF16)
        out_ref[t, :, H:] = grad
        if t > 0:
            dh = matmul(grad, w_rec_ref[...], NT)
            dc = dc * saved_ref[t, 0]


def call(kernel, out, *args, scratch=()):
    return pl.pallas_call(
        kernel, out_shape=out, scratch_shapes=list(scratch), compiler_params=VMEM
    )(*args)


def shaped(shape, dtype=BF16):
    return jax.ShapeDtypeStruct(shape, dtype)


def shards(
    features, nbr_owner, nbr_row, counts, weight_one, weight_two, w_in, w_rec, gate_bias, cotangent
):
    x = features[0]
    chips = ("z", "x")
    wanted, comb = call(
        plan_kernel,
        (shaped((CHIPS, LANES), F32), shaped((NODE, SLOTS))),
        nbr_owner.reshape(KNB, LANES),
        nbr_row.reshape(KNB, LANES),
        counts,
    )
    asked = lax.all_to_all(wanted, chips, 0, 0, tiled=True)
    pair = lax.all_gather(x, "core", tiled=True)
    pick, outgoing = call(
        pick_kernel, (shaped((SLOTS, H)), shaped((SLOTS, H))), asked, pair
    )
    arrived = lax.all_to_all(outgoing, chips, 0, 0, tiled=True)
    x = call(conv_kernel, shaped((NODE, H)), comb, arrived, x, counts, weight_one)
    pair = lax.all_gather(x, "core", tiled=True)
    outgoing = call(again_kernel, shaped((SLOTS, H)), pick, pair)
    arrived = lax.all_to_all(outgoing, chips, 0, 0, tiled=True)
    x = call(conv_kernel, shaped((NODE, H)), comb, arrived, x, counts, weight_two)
    both = jnp.concatenate([x, cotangent[0]], 1).reshape(SNAPS, PART, 2 * H)
    both = lax.all_to_all(both, "tm", 0, 0, tiled=True)
    result = call(
        lstm_kernel,
        shaped((SNAPS, PART, 5 * H)),
        both,
        w_in,
        w_rec,
        gate_bias.reshape(1, 4 * H),
        scratch=(pltpu.VMEM((NODE, 4 * H), F32), pltpu.VMEM((SNAPS, 6, PART, H), F32)),
    )
    result = lax.all_to_all(result, "tm", 0, 0, tiled=True).reshape(1, NODE, 5 * H)
    return result[:, :, :H], result[:, :, H:]


def solution(mesh):
    mesh = Mesh(mesh.devices.reshape(8, 8, 4, 2), ("tm", "z", "x", "core"))
    acct = ("z", "x", "core")
    return jax.shard_map(
        shards,
        mesh=mesh,
        in_specs=(
            P("tm", acct, None),
            P("tm", acct, None),
            P("tm", acct),
            P("tm", acct),
            P(),
            P(),
            P(),
            P(),
            P(),
            P("tm", acct, None),
        ),
        out_specs=(P("tm", acct, None), P("tm", acct, None)),
        check_vma=False,
    )
```

time: 257 us -> 114 us (0.44)
  the two profiles are of different devices: /device:TPU:26 before, /device:TPU:6 now
where the time goes in v1:
time: 114 us
  blocking collectives  82.9 us (73%)
  starting transfers between devices  13.4 us (12%)
  Pallas kernels  7.14 us (6%)
  waiting for transfers between devices  5.77 us (5%)
  local copies, waits for them, and re-layouts  3.84 us (3%)
    all_to_all x2, blocking collectives, shards(): arrived = lax.all_to_all(outgoing, chips, 0, 0, tiled=True)  49.4 us
    all_to_all x1, blocking collectives, shards(): both = lax.all_to_all(both, 'tm', 0, 0, tiled=True)  16 us
    all_to_all x1, blocking collectives, shards(): lax.all_to_all(result, 'tm', 0, 0, tiled=True).reshape(1, NODE, 5 * H)  13.6 us
    all_to_all x1, starting transfers between devices, shards(): asked = lax.all_to_all(wanted, chips, 0, 0, tiled=True)  13.4 us
    pallas_call x6, Pallas kernels, call(): pl.pallas_call(kernel, out_shape=out, scratch_shapes=list(scratch), compi...  7.14 us
    all_to_all x1, waiting for transfers between devices, shards(): asked = lax.all_to_all(wanted, chips, 0, 0, tiled=True)  5.77 us
    all_gather x2, blocking collectives, shards(): pair = lax.all_gather(x, 'core', tiled=True)  4.01 us
    unnamed x20, local copies, waits for them, and re-layouts  2.48 us
  transfers between devices with their start and end apart: 1, of which 1 were waited for; matrix products, arithmetic and copies ran while one was open for 0% of the time, Pallas kernels for 0%

profile of v1, /device:TPU:6, one launch (start us, length us, event | category | flops | bytes accessed | tf_op | source)
XLA Modules:
  0.0 113.8 jit_solution(10763974350872911213)
XLA Ops:
  0.6 0.0 copy-start.5
  0.6 0.6 copy-done.5
  1.3 0.0 copy-start.7
  1.3 0.7 copy-done.7
  2.0 0.0 copy-start.8
  2.0 0.7 copy-done.8
  2.7 1.9 %shard_map.113 = (f32[32,128]{1,0:T(8,128)}, bf16[128,1280]{1,0:T(8,128)(2,1)S(1)}) custom-call(s32[8,128]{1,0:T(8,128)S(1)} %bitcast.25, s32[8,128]{1,0:T(8,128)S(1)} %bitcast.26, s32[1,128]{1,0:T(1,128)S(1)} %copy-done.5), custom_call_target="tpu_custom_call" | custom-call | tf_op jit(solution)/shard_map/pallas_call | solution.py:134
  4.5 13.4 %all-to-all-start = ((f32[32,1,128]{2,1,0:T(1,128)}), f32[32,1,128]{2,1,0:T(1,128)S(1)}, u32[]{:S(2)}, u32[]{:S(2)}) async-start(f32[32,1,128]{2,1,0:T(1,128)} %bitcast.3), calls=%async_computation | async-start | bytes 32768 | tf_op jit(solution)/shard_map/all_to_all | solution.py:155
  18.0 2.1 %all-gather = bf16[1,256,256]{2,1,0:T(8,128)(2,1)S(1)} all-gather(bf16[1,128,256]{2,1,0:T(8,128)(2,1)} %param.10), channel_id=2, replica_groups=mesh['tm'=8,'z'=8,'x'=4,'core'=2] {'core'}, dimensions={1}, use_global_device_ids=true | all-gather | bytes 196608 | tf_op jit(solution)/shard_map/all_gather | solution.py:156
  20.1 5.8 %all-to-all-done = f32[32,1,128]{2,1,0:T(1,128)S(1)} async-done(((f32[32,1,128]{2,1,0:T(1,128)}), f32[32,1,128]{2,1,0:T(1,128)S(1)}, u32[]{:S(2)}, u32[]{:S(2)}) %all-to-all-start) | async-done | bytes 16416 | tf_op jit(solution)/shard_map/all_to_all | solution.py:155
  25.9 0.6 shard_map.114
  26.5 0.0 copy-start.2
  26.5 0.0 copy-start.3
  26.5 23.9 %all_to_all.43 = bf16[32,40,256]{2,1,0:T(8,128)(2,1)S(1)} all-to-all(bf16[32,40,256]{2,1,0:T(8,128)(2,1)S(1)} %bitcast.19), channel_id=1, replica_groups=mesh['tm'=8,'z'=8,'x'=4,'core'=2] {'z','x'}, dimensions={0} | all-to-all | bytes 1310720 | tf_op jit(solution)/shard_map/all_to_all | solution.py:160
  50.4 0.0 copy-done.2
  50.4 0.0 copy-done.3
  50.4 0.4 shard_map.115.x_ref
  50.8 1.9 %all_gather.7.x_ref = bf16[256,256]{1,0:T(8,128)(2,1)S(1)} all-gather(bf16[128,256]{1,0:T(8,128)(2,1)S(1)} %shard_map.115.x_ref), channel_id=1, replica_groups=mesh['tm'=8,'z'=8,'x'=4,'core'=2] {'core'}, dimensions={0}, use_global_device_ids=true | all-gather | bytes 196608 | tf_op jit(solution)/shard_map/all_gather | solution.py:162
  52.7 0.3 shard_map.116
  53.1 0.0 copy-start.4
  53.1 25.5 %all_to_all.44 = bf16[32,40,256]{2,1,0:T(8,128)(2,1)S(1)} all-to-all(bf16[32,40,256]{2,1,0:T(8,128)(2,1)S(1)} %bitcast.18), channel_id=1, replica_groups=mesh['tm'=8,'z'=8,'x'=4,'core'=2] {'z','x'}, dimensions={0} | all-to-all | bytes 1310720 | tf_op jit(solution)/shard_map/all_to_all | solution.py:164
  78.5 0.0 copy-done.4
  78.5 0.0 copy-start.9
  78.5 0.0 copy-start.1
  78.5 0.4 shard_map.117
  78.9 0.0 copy-start
  79.0 0.4 copy-done.9
  79.4 0.0 copy-start.6
  79.4 16.0 %all_to_all.45.xc_ref = bf16[8,16,512]{2,1,0:T(8,128)(2,1)S(1)} all-to-all(bf16[8,16,512]{2,1,0:T(8,128)(2,1)S(1)} %pad_maximum_fusion), channel_id=1, replica_groups=mesh['tm'=8,'z'=8,'x'=4,'core'=2] {'tm'}, dimensions={0} | all-to-all | bytes 262144 | tf_op jit(solution)/shard_map/all_to_all | solution.py:167
  95.4 0.0 copy-done.1
  95.4 0.0 copy-done
  95.4 0.0 copy-done.6
  95.4 3.5 %shard_map.118 = bf16[8,16,1280]{2,1,0:T(8,128)(2,1)S(1)} custom-call(bf16[8,16,512]{2,1,0:T(8,128)(2,1)S(1)} %all_to_all.45.xc_ref, bf16[256,1024]{1,0:T(8,128)(2,1)S(1)} %copy-done, bf16[256,1024]{1,0:T(8,128)(2,1)S(1)} %copy-done.1, f32[1,1024]{1,0:T(1,128)S(1)} %bitcast.24), custom_call_target="tpu_custom_call" | custom-call | tf_op jit(solution)/shard_map/pallas_call | solution.py:134
  98.9 13.6 %all_to_all.46 = bf16[8,16,1280]{2,1,0:T(8,128)(2,1)S(1)} all-to-all(bf16[8,16,1280]{2,1,0:T(8,128)(2,1)S(1)} %shard_map.118), channel_id=1, replica_groups=mesh['tm'=8,'z'=8,'x'=4,'core'=2] {'tm'}, dimensions={0} | all-to-all | bytes 655360 | tf_op jit(solution)/shard_map/all_to_all | solution.py:177
  112.5 0.6 slice.8
  113.1 0.7 slice.9
  (1 shorter events, 0.0 us)
Async XLA Ops:
  0.6 0.7 copy-start.5
  1.3 0.7 copy-start.7
  2.0 0.7 copy-start.8
  4.5 21.3 %all-to-all-start = ((f32[32,1,128]{2,1,0:T(1,128)}), f32[32,1,128]{2,1,0:T(1,128)S(1)}, u32[]{:S(2)}, u32[]{:S(2)}) async-start(f32[32,1,128]{2,1,0:T(1,128)} %bitcast.3), calls=%async_computation | async-start | bytes 32768 | tf_op jit(solution)/shard_map/all_to_all | solution.py:155
  26.5 23.9 %copy-start.2 = (bf16[1,128,256]{2,1,0:T(8,128)(2,1)S(1)}, bf16[1,128,256]{2,1,0:T(8,128)(2,1)}, u32[]{:S(2)}) copy-start(bf16[1,128,256]{2,1,0:T(8,128)(2,1)} %param.10) | copy-start | bytes 196612
  26.5 23.9 %copy-start.3 = (bf16[256,256]{1,0:T(8,128)(2,1)S(1)}, bf16[256,256]{1,0:T(8,128)(2,1)}, u32[]{:S(2)}) copy-start(bf16[256,256]{1,0:T(8,128)(2,1)} %weight_ref.2) | copy-start | bytes 393220
  53.1 25.5 %copy-start.4 = (bf16[256,256]{1,0:T(8,128)(2,1)S(1)}, bf16[256,256]{1,0:T(8,128)(2,1)}, u32[]{:S(2)}) copy-start(bf16[256,256]{1,0:T(8,128)(2,1)} %weight_ref.3) | copy-start | bytes 393220
  78.5 0.8 copy-start.9
  78.5 16.8 %copy-start.1 = (bf16[256,1024]{1,0:T(8,128)(2,1)S(1)}, bf16[256,1024]{1,0:T(8,128)(2,1)}, u32[]{:S(2)}) copy-start(bf16[256,1024]{1,0:T(8,128)(2,1)} %w_rec_ref.1) | copy-start | bytes 1572868
  78.9 16.4 %copy-start = (bf16[256,1024]{1,0:T(8,128)(2,1)S(1)}, bf16[256,1024]{1,0:T(8,128)(2,1)}, u32[]{:S(2)}) copy-start(bf16[256,1024]{1,0:T(8,128)(2,1)} %w_in_ref.1) | copy-start | bytes 1572868
  79.4 16.0 %copy-start.6 = (f32[1024]{0:T(1024)S(1)}, f32[1024]{0:T(1024)}, u32[]{:S(2)}) copy-start(f32[1024]{0:T(1024)} %param.18) | copy-start | bytes 12292

commit v2 on v1

v2 whole, which is shorter than its diff:
```python
import jax
import jax.numpy as jnp
from jax import lax
from jax.experimental import pallas as pl
from jax.experimental.pallas import tpu as pltpu
from jax.sharding import Mesh
from jax.sharding import PartitionSpec as P

H = 256
KNB = 8
NODE = 128
SNAPS = 8
GROUP = 8
ROWS = GROUP * NODE
LANES = 128
PART = NODE // SNAPS
UNUSED = -1000000.0
VMEM = pltpu.CompilerParams(vmem_limit_bytes=40 * 1024 * 1024)
BF16 = jnp.bfloat16
F32 = jnp.float32
NT = ((1,), (1,))


def iota(shape, dim):
    return lax.broadcasted_iota(jnp.int32, shape, dim)


def matmul(a, b, dims=((1,), (0,))):
    return lax.dot_general(a, b, (dims, ((), ())), preferred_element_type=F32)


def list_kernel(owner_ref, row_ref, cnt_ref, out_ref):
    owner = owner_ref[...].astype(F32)
    row = row_ref[...].astype(F32)
    lane = iota((1, LANES), 1)
    sub = iota((2 * KNB, LANES), 0)
    listed = jnp.zeros((2 * KNB, NODE), F32)
    for i in range(KNB):
        group = jnp.where(iota((NODE, LANES), 0) == i * (LANES // KNB) + lane // KNB, 1.0, 0.0)
        coded = jnp.where(
            sub % KNB == lane % KNB,
            jnp.where(sub < KNB, owner[i : i + 1, :], row[i : i + 1, :]),
            0.0,
        )
        listed = listed + matmul(coded.astype(BF16), group.astype(BF16), NT)
    code = listed[:KNB] * NODE + listed[KNB:]
    code = jnp.where(iota((KNB, NODE), 0) < cnt_ref[...], code, UNUSED)
    for z in range(GROUP):
        out_ref[z] = code - z * ROWS


def adjacency_kernel(code_ref, place_ref, adj_ref, scale_ref):
    code = code_ref[...].reshape(GROUP * KNB, NODE)
    code = jnp.concatenate([code, jnp.full((NODE - GROUP * KNB, NODE), UNUSED, F32)], 0).T
    spot = iota((NODE, ROWS), 1).astype(F32)
    used = jnp.where(code > UNUSED / 2, 1.0, 0.0)
    for z in range(GROUP):
        adj = jnp.zeros((NODE, ROWS), F32)
        for k in range(KNB):
            at = z * KNB + k
            adj = adj + jnp.where(spot == code[:, at : at + 1], 1.0, 0.0)
        adj_ref[z * NODE : (z + 1) * NODE, :] = adj.astype(BF16)
        count = jnp.sum(used[:, z * KNB : (z + 1) * KNB], 1, keepdims=True)
        scale_ref[z * NODE : (z + 1) * NODE, :] = jnp.broadcast_to(
            1.0 / (count + 1.0), (NODE, LANES)
        )
    mine = pl.ds(pl.multiple_of(place_ref[0] * NODE, NODE), NODE)
    here = pl.ds(pl.multiple_of(place_ref[1] * NODE, NODE), NODE)
    eye = jnp.where(iota((NODE, NODE), 0) == iota((NODE, NODE), 1), 1.0, 0.0)
    adj_ref[mine, here] = (adj_ref[mine, here].astype(F32) + eye).astype(BF16)


def partial_kernel(adj_ref, plane_ref, scale_ref, out_ref):
    plane = plane_ref[...]
    for z in range(GROUP):
        rows = slice(z * NODE, (z + 1) * NODE)
        out_ref[rows, :] = (
            matmul(adj_ref[rows, :], plane) * scale_ref[rows, :1]
        ).astype(BF16)


def first_kernel(part_ref, weight_ref, out_ref):
    total = part_ref[0].astype(F32)
    for z in range(1, GROUP):
        total = total + part_ref[z].astype(F32)
    x = jnp.maximum(matmul(total.astype(BF16), weight_ref[...]), 0.0).astype(BF16)
    for z in range(GROUP):
        out_ref[z] = x


def lstm_kernel(
    part_ref, cot_ref, weight_ref, w_in_ref, w_rec_ref, bias_ref, out_ref, z_ref, saved_ref
):
    total = part_ref[0].astype(F32)
    for z in range(1, GROUP):
        total = total + part_ref[z].astype(F32)
    x = jnp.maximum(matmul(total.astype(BF16), weight_ref[...]), 0.0).astype(BF16)
    z_ref[...] = (matmul(x, w_in_ref[...]) + bias_ref[...]).astype(BF16).astype(F32)
    h = None
    c = jnp.zeros((PART, H), F32)
    for t in range(SNAPS):
        gates = z_ref[t * PART : (t + 1) * PART, :]
        if t > 0:
            gates = gates + matmul(h, w_rec_ref[...])
        i = jax.nn.sigmoid(gates[:, :H])
        f = jax.nn.sigmoid(gates[:, H : 2 * H])
        g = jnp.tanh(gates[:, 2 * H : 3 * H])
        o = jax.nn.sigmoid(gates[:, 3 * H :])
        c_new = f * c + i * g
        tc = jnp.tanh(c_new)
        h = (o * tc).astype(BF16)
        out_ref[t, :, :H] = h
        saved_ref[t, 0] = f
        saved_ref[t, 1] = o * (1.0 - tc * tc)
        saved_ref[t, 2] = g * i * (1.0 - i)
        saved_ref[t, 3] = c * f * (1.0 - f)
        saved_ref[t, 4] = i * (1.0 - g * g)
        saved_ref[t, 5] = tc * o * (1.0 - o)
        c = c_new
    dh = jnp.zeros((PART, H), F32)
    dc = jnp.zeros((PART, H), F32)
    for t in range(SNAPS - 1, -1, -1):
        dh = dh + cot_ref[t].astype(F32)
        dc = dc + dh * saved_ref[t, 1]
        grad = jnp.concatenate(
            [dc * saved_ref[t, 2], dc * saved_ref[t, 3], dc * saved_ref[t, 4], dh * saved_ref[t, 5]],
            1,
        ).astype(BF16)
        out_ref[t, :, H:] = grad
        if t > 0:
            dh = matmul(grad, w_rec_ref[...], NT)
            dc = dc * saved_ref[t, 0]


def call(kernel, out, *args, scratch=(), in_specs=None):
    more = {} if in_specs is None else {"in_specs": in_specs}
    return pl.pallas_call(
        kernel, out_shape=out, scratch_shapes=list(scratch), compiler_params=VMEM, **more
    )(*args)


def shaped(shape, dtype=BF16):
    return jax.ShapeDtypeStruct(shape, dtype)


def exchange(array, axes):
    return lax.all_to_all(array, axes, 0, 0, tiled=True)


def shards(
    features, nbr_owner, nbr_row, counts, weight_one, weight_two, w_in, w_rec, gate_bias, cotangent
):
    plane_axes = ("x", "core")
    place = jnp.stack([lax.axis_index("z"), lax.axis_index(plane_axes)]).astype(jnp.int32)
    copies = jnp.broadcast_to(features, (GROUP, NODE, H))
    plane = exchange(copies, plane_axes).reshape(ROWS, H)
    listed = call(
        list_kernel,
        shaped((GROUP, KNB, NODE), F32),
        nbr_owner.reshape(KNB, LANES),
        nbr_row.reshape(KNB, LANES),
        counts,
    )
    code = exchange(listed, "z")
    vmem = pl.BlockSpec(memory_space=pltpu.VMEM)
    adj, scale = call(
        adjacency_kernel,
        (shaped((ROWS, ROWS)), shaped((ROWS, LANES), F32)),
        code,
        place,
        in_specs=[vmem, pl.BlockSpec(memory_space=pltpu.SMEM)],
    )
    part = call(partial_kernel, shaped((ROWS, H)), adj, plane, scale)
    part = exchange(part.reshape(GROUP, NODE, H), "z")
    copies = call(first_kernel, shaped((GROUP, NODE, H)), part, weight_one)
    plane = exchange(copies, plane_axes).reshape(ROWS, H)
    part = call(partial_kernel, shaped((ROWS, H)), adj, plane, scale)
    part = exchange(part.reshape(GROUP * SNAPS, PART, H), ("z", "tm")).reshape(GROUP, NODE, H)
    cot = exchange(cotangent.reshape(SNAPS, PART, H), "tm")
    result = call(
        lstm_kernel,
        shaped((SNAPS, PART, 5 * H)),
        part,
        cot,
        weight_two,
        w_in,
        w_rec,
        gate_bias.reshape(1, 4 * H),
        scratch=(pltpu.VMEM((NODE, 4 * H), F32), pltpu.VMEM((SNAPS, 6, PART, H), F32)),
    )
    result = exchange(result, "tm").reshape(1, NODE, 5 * H)
    return result[:, :, :H], result[:, :, H:]


def solution(mesh):
    mesh = Mesh(mesh.devices.reshape(8, 8, 4, 2), ("tm", "z", "x", "core"))
    acct = ("z", "x", "core")
    return jax.shard_map(
        shards,
        mesh=mesh,
        in_specs=(
            P("tm", acct, None),
            P("tm", acct, None),
            P("tm", acct),
            P("tm", acct),
            P(),
            P(),
            P(),
            P(),
            P(),
            P("tm", acct, None),
        ),
        out_specs=(P("tm", acct, None), P("tm", acct, None)),
        check_vma=False,
    )
```

time: 114 us -> 131 us (1.15)
  blocking collectives: 82.9 us -> 88.4 us
  waiting for transfers between devices: 5.77 us -> 10.3 us
  local copies, waits for them, and re-layouts: 3.84 us -> 7.94 us
  Pallas kernels: 7.14 us -> 10.3 us
  starting transfers between devices: 13.4 us -> 11.9 us
    all_to_all x4 -> x5, blocking collectives: 78.9 us -> 88.4 us  [exchange(): return lax.all_to_all(array, axes, 0, 0, tiled=True)]
    all_to_all x1 -> x2, waiting for transfers between devices: 5.77 us -> 10.3 us  [exchange(): return lax.all_to_all(array, axes, 0, 0, tiled=True)]
    all_gather x2 -> x0, blocking collectives: 4.01 us -> none  [shards(): pair = lax.all_gather(x, 'core', tiled=True)]
    pallas_call x6, Pallas kernels: 7.14 us -> 10.3 us  [call(): pl.pallas_call(kernel, out_shape=out, scratch_shapes=list(scratch), compi...]
    unnamed x20 -> x18, local copies, waits for them, and re-layouts: 2.48 us -> 4.91 us
    broadcast_in_dim x0 -> x1, local copies, waits for them, and re-layouts: none -> 1.67 us  [shards(): copies = jnp.broadcast_to(features, (GROUP, NODE, H))]
    all_to_all x1 -> x2, starting transfers between devices: 13.4 us -> 11.9 us  [exchange(): return lax.all_to_all(array, axes, 0, 0, tiled=True)]
  transfers between devices with their start and end apart: 1 -> 2, of which waited for: 1 -> 2; matrix products, arithmetic and copies ran while one was open for 0% -> 0% of each run, Pallas kernels for 0% -> 4%
where the time goes in v2:
time: 131 us; the launch traced here: 130 us
  blocking collectives  88.4 us (67%)
  starting transfers between devices  11.9 us (9%)
  Pallas kernels  10.3 us (8%)
  waiting for transfers between devices  10.3 us (8%)
  local copies, waits for them, and re-layouts  7.94 us (6%)
    all_to_all x5, blocking collectives, exchange(): return lax.all_to_all(array, axes, 0, 0, tiled=True)  88.4 us
    all_to_all x2, starting transfers between devices, exchange(): return lax.all_to_all(array, axes, 0, 0, tiled=True)  11.9 us
    pallas_call x6, Pallas kernels, call(): pl.pallas_call(kernel, out_shape=out, scratch_shapes=list(scratch), compi...  10.3 us
    all_to_all x2, waiting for transfers between devices, exchange(): return lax.all_to_all(array, axes, 0, 0, tiled=True)  10.3 us
    unnamed x18, local copies, waits for them, and re-layouts  4.91 us
  transfers between devices with their start and end apart: 2, of which 2 were waited for; matrix products, arithmetic and copies ran while one was open for 0% of the time, Pallas kernels for 4%

profile of v2, /device:TPU:6, one launch (start us, length us, event | category | flops | bytes accessed | tf_op | source)
XLA Modules:
  0.0 129.7 jit_solution(6614955542211964316)
XLA Ops:
  0.6 0.0 copy-start.6
  0.6 0.7 copy-done.6
  1.3 0.0 copy-start.7
  1.3 0.7 copy-done.7
  2.0 0.0 copy-start.8
  2.0 0.7 copy-done.8
  2.7 0.2 shard_map.113
  2.9 18.2 %all_to_all.35.code_ref = f32[8,8,128]{2,1,0:T(8,128)S(1)} all-to-all(f32[8,8,128]{2,1,0:T(8,128)S(1)} %shard_map.113), channel_id=1, replica_groups=mesh['tm'=8,'z'=8,'x'=4,'core'=2] {'z'}, dimensions={0} | all-to-all | bytes 65536 | tf_op jit(solution)/shard_map/all_to_all | solution.py:147
  21.1 1.7 %broadcast_in_dim.8 = bf16[8,128,256]{2,1,0:T(8,128)(2,1)} broadcast(bf16[128,256]{1,0:T(8,128)(2,1)} %bitcast.23), dimensions={1,2} | broadcast | bytes 589824 | tf_op jit(solution)/shard_map/broadcast_in_dim | solution.py:155
  22.7 4.8 %all-to-all-start.1 = ((bf16[8,128,256]{2,1,0:T(8,128)(2,1)}), bf16[8,128,256]{2,1,0:T(8,128)(2,1)S(1)}, u32[]{:S(2)}, u32[]{:S(2)}) async-start(bf16[8,128,256]{2,1,0:T(8,128)(2,1)} %broadcast_in_dim.8), calls=%async_computation.1 | async-start | bytes 1048576 | tf_op jit(solution)/shard_map/all_to_all | solution.py:147
  27.5 0.1 pad_add_fusion.place_ref
  27.6 4.7 %shard_map.114 = (bf16[1024,1024]{1,0:T(8,128)(2,1)S(1)}, f32[1024,128]{1,0:T(8,128)S(1)}) custom-call(f32[8,8,128]{2,1,0:T(8,128)S(1)} %all_to_all.35.code_ref, s32[2]{0:T(128)S(1)} %pad_add_fusion.place_ref), custom_call_target="tpu_custom_call" | custom-call | tf_op jit(solution)/shard_map/pallas_call | solution.py:137
  32.3 3.5 %all-to-all-done.1 = bf16[8,128,256]{2,1,0:T(8,128)(2,1)S(1)} async-done(((bf16[8,128,256]{2,1,0:T(8,128)(2,1)}), bf16[8,128,256]{2,1,0:T(8,128)(2,1)S(1)}, u32[]{:S(2)}, u32[]{:S(2)}) %all-to-all-start.1) | async-done | bytes 524320 | tf_op jit(solution)/shard_map/all_to_all | solution.py:147
  35.8 0.0 copy-start.3
  35.8 0.7 shard_map.115
  36.5 20.0 %all_to_all.36.part_ref = bf16[8,128,256]{2,1,0:T(8,128)(2,1)S(1)} all-to-all(bf16[8,128,256]{2,1,0:T(8,128)(2,1)S(1)} %bitcast.16), channel_id=1, replica_groups=mesh['tm'=8,'z'=8,'x'=4,'core'=2] {'z'}, dimensions={0} | all-to-all | bytes 1048576 | tf_op jit(solution)/shard_map/all_to_all | solution.py:147
  56.5 0.0 copy-done.3
  56.5 0.2 shard_map.116
  56.7 12.8 %all_to_all.37 = bf16[8,128,256]{2,1,0:T(8,128)(2,1)S(1)} all-to-all(bf16[8,128,256]{2,1,0:T(8,128)(2,1)S(1)} %shard_map.116), channel_id=1, replica_groups=mesh['tm'=8,'z'=8,'x'=4,'core'=2] {'x','core'}, dimensions={0} | all-to-all | bytes 1048576 | tf_op jit(solution)/shard_map/all_to_all | solution.py:147
  69.5 7.1 %all-to-all-start.5 = ((bf16[8,16,256]{2,1,0:T(8,128)(2,1)}), bf16[8,16,256]{2,1,0:T(8,128)(2,1)S(1)}, u32[]{:S(2)}, u32[]{:S(2)}) async-start(bf16[8,16,256]{2,1,0:T(8,128)(2,1)} %bitcast.10), calls=%async_computation.5 | async-start | bytes 131072 | tf_op jit(solution)/shard_map/all_to_all | solution.py:147
  76.6 0.0 copy-start.4
  76.6 0.0 copy-start.5
  76.6 0.7 shard_map.117
  77.4 0.0 copy-start
  77.4 0.8 copy-done
  78.1 6.8 %all-to-all-done.5.cot_ref = bf16[8,16,256]{2,1,0:T(8,128)(2,1)S(1)} async-done(((bf16[8,16,256]{2,1,0:T(8,128)(2,1)}), bf16[8,16,256]{2,1,0:T(8,128)(2,1)S(1)}, u32[]{:S(2)}, u32[]{:S(2)}) %all-to-all-start.5) | async-done | bytes 65568 | tf_op jit(solution)/shard_map/all_to_all | solution.py:147
  85.0 22.9 %all_to_all.38 = bf16[64,16,256]{2,1,0:T(8,128)(2,1)S(1)} all-to-all(bf16[64,16,256]{2,1,0:T(8,128)(2,1)} %bitcast.15), channel_id=1, replica_groups=mesh['tm'=8,'z'=8,'x'=4,'core'=2] {'z','tm'}, dimensions={0} | all-to-all | bytes 1048576 | tf_op jit(solution)/shard_map/all_to_all | solution.py:147
  107.8 0.0 copy-done.4
  107.8 0.0 copy-done.5
  107.9 0.0 copy-start.1
  107.9 1.0 copy-done.1
  108.9 0.0 copy-start.2
  108.9 1.0 copy-done.2
  109.9 3.7 %shard_map.118 = bf16[8,16,1280]{2,1,0:T(8,128)(2,1)S(1)} custom-call(bf16[8,128,256]{2,1,0:T(8,128)(2,1)S(1)} %bitcast.17, bf16[8,16,256]{2,1,0:T(8,128)(2,1)S(1)} %all-to-all-done.5.cot_ref, bf16[256,256]{1,0:T(8,128)(2,1)S(1)} %copy-done.4, bf16[256,1024]{1,0:T(8,128)(2,1)S(1)} %copy-done.1, bf16[256,1024]{1,0:T(8,128)(2,1)S(1)} %copy-done.2, ...), custom_call_target="tpu_custom_call" | custom-call | tf_op jit(solution)/shard_map/pallas_call | solution.py:137
  113.7 14.6 %all_to_all.39 = bf16[8,16,1280]{2,1,0:T(8,128)(2,1)S(1)} all-to-all(bf16[8,16,1280]{2,1,0:T(8,128)(2,1)S(1)} %shard_map.118), channel_id=1, replica_groups=mesh['tm'=8,'z'=8,'x'=4,'core'=2] {'tm'}, dimensions={0} | all-to-all | bytes 655360 | tf_op jit(solution)/shard_map/all_to_all | solution.py:147
  128.3 0.7 slice.9
  129.0 0.6 slice.8
Async XLA Ops:
  0.6 0.7 copy-start.6
  1.3 0.7 copy-start.7
  2.0 0.7 copy-start.8
  22.7 13.1 %all-to-all-start.1 = ((bf16[8,128,256]{2,1,0:T(8,128)(2,1)}), bf16[8,128,256]{2,1,0:T(8,128)(2,1)S(1)}, u32[]{:S(2)}, u32[]{:S(2)}) async-start(bf16[8,128,256]{2,1,0:T(8,128)(2,1)} %broadcast_in_dim.8), calls=%async_computation.1 | async-start | bytes 1048576 | tf_op jit(solution)/shard_map/all_to_all | solution.py:147
  35.8 20.7 %copy-start.3 = (bf16[256,256]{1,0:T(8,128)(2,1)S(1)}, bf16[256,256]{1,0:T(8,128)(2,1)}, u32[]{:S(2)}) copy-start(bf16[256,256]{1,0:T(8,128)(2,1)} %weight_ref.2) | copy-start | bytes 393220
  69.5 15.5 %all-to-all-start.5 = ((bf16[8,16,256]{2,1,0:T(8,128)(2,1)}), bf16[8,16,256]{2,1,0:T(8,128)(2,1)S(1)}, u32[]{:S(2)}, u32[]{:S(2)}) async-start(bf16[8,16,256]{2,1,0:T(8,128)(2,1)} %bitcast.10), calls=%async_computation.5 | async-start | bytes 131072 | tf_op jit(solution)/shard_map/all_to_all | solution.py:147
  76.6 31.2 %copy-start.4 = (bf16[256,256]{1,0:T(8,128)(2,1)S(1)}, bf16[256,256]{1,0:T(8,128)(2,1)}, u32[]{:S(2)}) copy-start(bf16[256,256]{1,0:T(8,128)(2,1)} %weight_ref.3) | copy-start | bytes 393220
  76.6 31.2 %copy-start.5 = (f32[1024]{0:T(1024)S(1)}, f32[1024]{0:T(1024)}, u32[]{:S(2)}) copy-start(f32[1024]{0:T(1024)} %param.18) | copy-start | bytes 12292
  77.4 0.8 copy-start
  107.9 1.0 copy-start.1
  108.9 1.0 copy-start.2

commit v3 on v1

v3 whole, which is shorter than its diff:
```python
import jax
import jax.numpy as jnp
from jax import lax
from jax.experimental import pallas as pl
from jax.experimental.pallas import tpu as pltpu
from jax.sharding import Mesh
from jax.sharding import PartitionSpec as P

H = 256
KNB = 8
NODE = 128
SNAPS = 8
GROUP = 8
ROWS = GROUP * NODE
LANES = 128
PART = NODE // SNAPS
CHIPS = 32
CAP = 40
SLOTS = CHIPS * CAP
BITS = 11
NONE = 2047
ASKED, COUNT = 4, 5
VMEM = pltpu.CompilerParams(vmem_limit_bytes=16 * 1024 * 1024)
BF16 = jnp.bfloat16
F32 = jnp.float32
NT = ((1,), (1,))


def iota(shape, dim):
    return lax.broadcasted_iota(jnp.int32, shape, dim)


def matmul(a, b, dims=((1,), (0,))):
    return lax.dot_general(a, b, (dims, ((), ())), preferred_element_type=F32)


def plan_kernel(owner_hbm, row_hbm, cnt_hbm, msg_ref, place_ref, owner_ref, row_ref, cnt_ref, sems):
    pairs = ((owner_hbm, owner_ref), (row_hbm, row_ref), (cnt_hbm, cnt_ref))
    copies = [
        pltpu.make_async_copy(a, b, sems.at[i]) for i, (a, b) in enumerate(pairs)
    ]
    for copy in copies:
        copy.start()
    for copy in copies:
        copy.wait()
    owner = owner_ref[...]
    value = ((owner % 2) * NODE + row_ref[...]).astype(F32)
    chip = owner // 2
    upper = jnp.where(iota((LANES, LANES), 0) < iota((LANES, LANES), 1), 1.0, 0.0).astype(BF16)
    base = jnp.zeros((CHIPS, 1), F32)
    wanted = jnp.zeros((CHIPS, LANES), F32)
    place = jnp.zeros((NODE, 2 * KNB), F32)
    listed = jnp.zeros((2 * KNB, NODE), F32)
    lane = iota((1, LANES), 1)
    sub = iota((2 * KNB, LANES), 0)
    for i in range(KNB):
        chip_i = chip[i : i + 1, :]
        value_i = value[i : i + 1, :]
        onehot = jnp.where(iota((CHIPS, LANES), 0) == chip_i, 1.0, 0.0)
        before = matmul(onehot.astype(BF16), upper) + base
        base = base + jnp.sum(onehot, 1, keepdims=True)
        rank = jnp.sum(onehot * before, 0, keepdims=True)
        ranks = jnp.where(iota((LANES, LANES), 0).astype(F32) == rank, 1.0, 0.0).astype(BF16)
        wanted = wanted + matmul((onehot * value_i).astype(BF16), ranks, NT)
        group = jnp.where(iota((NODE, LANES), 0) == i * (LANES // KNB) + lane // KNB, 1.0, 0.0)
        group = group.astype(BF16)
        mine = sub % KNB == lane % KNB
        coded = jnp.where(mine, jnp.where(sub < KNB, chip_i.astype(F32), rank), 0.0)
        place = place + matmul(group, coded.astype(BF16), NT)
        coded = jnp.where(mine, jnp.where(sub < KNB, chip_i.astype(F32), value_i), 0.0)
        listed = listed + matmul(coded.astype(BF16), group, NT)
    place_ref[...] = place
    wanted = wanted.astype(jnp.int32)
    count = cnt_ref[...]
    chip = listed[:KNB].astype(jnp.int32)
    code = (chip % 4) * (2 * NODE) + listed[KNB:].astype(jnp.int32)
    plane = jnp.where(iota((KNB, NODE), 0) < count, chip // 4, -1)
    blank = jnp.zeros((KNB - COUNT - 1, LANES), jnp.int32)
    for z in range(GROUP):
        here = jnp.where(plane == z, code, NONE)
        packed = here[: KNB // 2] * (1 << BITS) + here[KNB // 2 :]
        for x in range(4):
            at = z * 4 + x
            msg_ref[at] = jnp.concatenate([packed, wanted[at : at + 1], count, blank], 0)


def column(row):
    eye = iota((NODE, NODE), 0) == iota((NODE, NODE), 1)
    return jnp.sum(jnp.where(eye, row, 0.0), 1, keepdims=True)


def comb_kernel(place_ref, cnt_ref, comb_ref):
    count = column(cnt_ref[...].astype(F32))
    place = place_ref[:, :KNB] * CAP + place_ref[:, KNB:]
    place = jnp.where(iota((NODE, KNB), 1).astype(F32) < count, place, -1.0)
    spot = iota((NODE, SLOTS), 1).astype(F32)
    comb = jnp.zeros((NODE, SLOTS), F32)
    for k in range(KNB):
        comb = comb + jnp.where(spot == place[:, k : k + 1], 1.0, 0.0)
    comb_ref[...] = comb.astype(BF16)


def pick_kernel(msg_ref, x_ref, out_ref):
    eye = jnp.where(iota((LANES, LANES), 0) == iota((LANES, LANES), 1), 1.0, 0.0).astype(BF16)
    turned = matmul(eye, msg_ref[:, ASKED, :].astype(F32).astype(BF16), NT)
    col = iota((CAP, H), 1).astype(F32)
    x = x_ref[...]
    for d in range(0, CHIPS, 2):
        both = [jnp.where(turned[:CAP, e : e + 1] == col, 1.0, 0.0) for e in (d, d + 1)]
        pick = jnp.concatenate(both, 0).astype(BF16)
        out_ref[d * CAP : (d + 2) * CAP, :] = matmul(pick, x).astype(BF16)


def conv_kernel(comb_ref, arrived_ref, x_ref, cnt_ref, weight_ref, out_ref):
    count = column(cnt_ref[...].astype(F32))
    summed = x_ref[...].astype(F32) + matmul(comb_ref[...], arrived_ref[...])
    agg = (summed * (1.0 / (count + 1.0))).astype(BF16)
    x = jnp.maximum(matmul(agg, weight_ref[...]), 0.0).astype(BF16)
    for d in range(GROUP):
        out_ref[d] = x


def adjacency_kernel(msg_ref, where_ref, adj_ref, scale_ref):
    z_me, x_me, core_me = where_ref[0], where_ref[1], where_ref[2]
    lists, counts = [], []
    for z in range(GROUP):
        message = msg_ref[z * 4 + x_me]
        packed = message[: KNB // 2]
        lists += [packed // (1 << BITS), packed % (1 << BITS)]
        counts.append(message[COUNT : COUNT + 1])
    blank = jnp.zeros((NODE - GROUP * (KNB + 1), NODE), jnp.int32)
    turned = jnp.concatenate(lists + counts + [blank], 0).astype(F32).T
    spot = iota((NODE, ROWS), 1).astype(F32)
    for z in range(GROUP):
        adj = jnp.zeros((NODE, ROWS), F32)
        for k in range(KNB):
            at = z * KNB + k
            adj = adj + jnp.where(spot == turned[:, at : at + 1], 1.0, 0.0)
        rows = slice(z * NODE, (z + 1) * NODE)
        adj_ref[rows, :] = adj.astype(BF16)
        at = GROUP * KNB + z
        scale = 1.0 / (turned[:, at : at + 1] + 1.0)
        scale_ref[rows, :] = jnp.broadcast_to(scale, (NODE, LANES))
    mine = pl.ds(pl.multiple_of(z_me * NODE, NODE), NODE)
    here = pl.ds(pl.multiple_of((x_me * 2 + core_me) * NODE, NODE), NODE)
    eye = jnp.where(iota((NODE, NODE), 0) == iota((NODE, NODE), 1), 1.0, 0.0)
    adj_ref[mine, here] = (adj_ref[mine, here].astype(F32) + eye).astype(BF16)


def partial_kernel(adj_ref, plane_ref, scale_ref, out_ref):
    plane = plane_ref[...]
    for z in range(GROUP):
        rows = slice(z * NODE, (z + 1) * NODE)
        part = (matmul(adj_ref[rows, :], plane) * scale_ref[rows, :1]).astype(BF16)
        out_ref[:, z] = part.reshape(SNAPS, PART, H)


def lstm_kernel(
    part_ref,
    weight_ref,
    bias_ref,
    w_in_hbm,
    w_rec_hbm,
    cot_hbm,
    out_ref,
    z_ref,
    saved_ref,
    w_in_ref,
    w_rec_ref,
    cot_ref,
    sems,
):
    pairs = ((w_in_hbm, w_in_ref), (w_rec_hbm, w_rec_ref), (cot_hbm, cot_ref))
    copies = [
        pltpu.make_async_copy(a, b, sems.at[i]) for i, (a, b) in enumerate(pairs)
    ]
    for copy in copies:
        copy.start()
    total = part_ref[:, 0].astype(F32)
    for z in range(1, GROUP):
        total = total + part_ref[:, z].astype(F32)
    agg = total.reshape(NODE, H).astype(BF16)
    x = jnp.maximum(matmul(agg, weight_ref[...]), 0.0).astype(BF16)
    copies[0].wait()
    z_ref[...] = (matmul(x, w_in_ref[...]) + bias_ref[...]).astype(BF16).astype(F32)
    copies[1].wait()
    h = None
    c = jnp.zeros((PART, H), F32)
    for t in range(SNAPS):
        gates = z_ref[t * PART : (t + 1) * PART, :]
        if t > 0:
            gates = gates + matmul(h, w_rec_ref[...])
        i = jax.nn.sigmoid(gates[:, :H])
        f = jax.nn.sigmoid(gates[:, H : 2 * H])
        g = jnp.tanh(gates[:, 2 * H : 3 * H])
        o = jax.nn.sigmoid(gates[:, 3 * H :])
        c_new = f * c + i * g
        tc = jnp.tanh(c_new)
        h = (o * tc).astype(BF16)
        out_ref[t, :, :H] = h
        saved_ref[t, 0] = f
        saved_ref[t, 1] = o * (1.0 - tc * tc)
        saved_ref[t, 2] = g * i * (1.0 - i)
        saved_ref[t, 3] = c * f * (1.0 - f)
        saved_ref[t, 4] = i * (1.0 - g * g)
        saved_ref[t, 5] = tc * o * (1.0 - o)
        c = c_new
    copies[2].wait()
    dh = jnp.zeros((PART, H), F32)
    dc = jnp.zeros((PART, H), F32)
    for t in range(SNAPS - 1, -1, -1):
        dh = dh + cot_ref[t].astype(F32)
        dc = dc + dh * saved_ref[t, 1]
        grad = jnp.concatenate(
            [dc * saved_ref[t, 2], dc * saved_ref[t, 3], dc * saved_ref[t, 4], dh * saved_ref[t, 5]],
            1,
        ).astype(BF16)
        out_ref[t, :, H:] = grad
        if t > 0:
            dh = matmul(grad, w_rec_ref[...], NT)
            dc = dc * saved_ref[t, 0]


def call(kernel, out, *args, scratch=(), in_specs=None):
    more = {} if in_specs is None else {"in_specs": in_specs}
    return pl.pallas_call(
        kernel, out_shape=out, scratch_shapes=list(scratch), compiler_params=VMEM, **more
    )(*args)


def shaped(shape, dtype=BF16):
    return jax.ShapeDtypeStruct(shape, dtype)


def exchange(array, axes):
    return lax.all_to_all(array, axes, 0, 0, tiled=True)


def turned_cotangent(cotangent):
    mine = lax.axis_index("tm") == jnp.arange(SNAPS, dtype=jnp.int32)
    spread = jnp.where(
        mine[None, :, None, None], cotangent.reshape(SNAPS, 1, PART, H), jnp.zeros((), BF16)
    )
    total = lax.psum_scatter(spread.reshape(SNAPS * NODE, H), "tm", tiled=True)
    return total.reshape(SNAPS, PART, H)


def shards(
    features, nbr_owner, nbr_row, counts, weight_one, weight_two, w_in, w_rec, gate_bias, cotangent
):
    hbm = pl.BlockSpec(memory_space=pltpu.HBM)
    vmem = pl.BlockSpec(memory_space=pltpu.VMEM)
    chips = ("z", "x")
    x = features[0]
    cot = turned_cotangent(cotangent)
    msg, place = call(
        plan_kernel,
        (shaped((CHIPS, KNB, LANES), jnp.int32), shaped((NODE, 2 * KNB), F32)),
        nbr_owner.reshape(KNB, LANES),
        nbr_row.reshape(KNB, LANES),
        counts,
        in_specs=[hbm] * 3,
        scratch=(
            pltpu.VMEM((KNB, LANES), jnp.int32),
            pltpu.VMEM((KNB, LANES), jnp.int32),
            pltpu.VMEM((1, LANES), jnp.int32),
            pltpu.SemaphoreType.DMA((3,)),
        ),
    )
    msg = exchange(msg, chips)
    pair = lax.all_gather(x, "core", tiled=True)
    comb = call(comb_kernel, shaped((NODE, SLOTS)), place, counts)
    outgoing = call(pick_kernel, shaped((SLOTS, H)), msg, pair)
    arrived = exchange(outgoing.reshape(CHIPS, CAP, H), chips).reshape(SLOTS, H)
    where = jnp.stack([lax.axis_index(a) for a in ("z", "x", "core")]).astype(jnp.int32)
    adj, scale = call(
        adjacency_kernel,
        (shaped((ROWS, ROWS)), shaped((ROWS, LANES), F32)),
        msg,
        where,
        in_specs=[vmem, pl.BlockSpec(memory_space=pltpu.SMEM)],
    )
    copies = call(conv_kernel, shaped((GROUP, NODE, H)), comb, arrived, x, counts, weight_one)
    plane = exchange(copies, ("x", "core")).reshape(ROWS, H)
    part = call(partial_kernel, shaped((SNAPS, GROUP, PART, H)), adj, plane, scale)
    part = exchange(part.reshape(SNAPS * GROUP, PART, H), ("tm", "z"))
    result = call(
        lstm_kernel,
        shaped((SNAPS, PART, 5 * H)),
        part.reshape(SNAPS, GROUP, PART, H),
        weight_two,
        gate_bias.reshape(1, 4 * H),
        w_in,
        w_rec,
        cot,
        in_specs=[vmem] * 3 + [hbm] * 3,
        scratch=(
            pltpu.VMEM((NODE, 4 * H), F32),
            pltpu.VMEM((SNAPS, 6, PART, H), F32),
            pltpu.VMEM((H, 4 * H), BF16),
            pltpu.VMEM((H, 4 * H), BF16),
            pltpu.VMEM((SNAPS, PART, H), BF16),
            pltpu.SemaphoreType.DMA((3,)),
        ),
    )
    result = exchange(result, "tm").reshape(1, NODE, 5 * H)
    return result[:, :, :H], result[:, :, H:]


def solution(mesh):
    mesh = Mesh(mesh.devices.reshape(8, 8, 4, 2), ("tm", "z", "x", "core"))
    acct = ("z", "x", "core")
    return jax.shard_map(
        shards,
        mesh=mesh,
        in_specs=(
            P("tm", acct, None),
            P("tm", acct, None),
            P("tm", acct),
            P("tm", acct),
            P(),
            P(),
            P(),
            P(),
            P(),
            P("tm", acct, None),
        ),
        out_specs=(P("tm", acct, None), P("tm", acct, None)),
        check_vma=False,
    )
```

time: 114 us -> 141 us (1.24)
  blocking collectives: 82.9 us -> 18.5 us
  waiting for transfers between devices: 5.77 us -> 51.8 us
  starting transfers between devices: 13.4 us -> 32.9 us
  between operations: 0.73 us -> 14.1 us
  Pallas kernels: 7.14 us -> 15.3 us
  local copies, waits for them, and re-layouts: 3.84 us -> 6.53 us
    all_to_all x4 -> x1, blocking collectives: 78.9 us -> 16.4 us  [exchange(): return lax.all_to_all(array, axes, 0, 0, tiled=True)]
    reduce_scatter x0 -> x1, waiting for transfers between devices: none -> 24.2 us  [turned_cotangent(): total = lax.psum_scatter(spread.reshape(SNAPS * NODE, H), 'tm', tiled=True)]
    all_to_all x1 -> x4, waiting for transfers between devices: 5.77 us -> 27.6 us  [exchange(): return lax.all_to_all(array, axes, 0, 0, tiled=True)]
    all_to_all x1 -> x4, starting transfers between devices: 13.4 us -> 32.9 us  [exchange(): return lax.all_to_all(array, axes, 0, 0, tiled=True)]
    pallas_call x6 -> x7, Pallas kernels: 7.14 us -> 15.3 us  [call(): pl.pallas_call(kernel, out_shape=out, scratch_shapes=list(scratch), compi...]
    unnamed x20 -> x24, local copies, waits for them, and re-layouts: 2.48 us -> 5 us
    all_gather x2 -> x1, blocking collectives: 4.01 us -> 2.11 us  [shards(): pair = lax.all_gather(x, 'core', tiled=True)]
  transfers between devices with their start and end apart: 1 -> 5, of which waited for: 1 -> 4; matrix products, arithmetic and copies ran while one was open for 0% -> 1% of each run, Pallas kernels for 0% -> 4%
where the time goes in v3:
time: 141 us; the launch traced here: 140 us
  waiting for transfers between devices  51.8 us (37%)
  starting transfers between devices  32.9 us (23%)
  blocking collectives  18.5 us (13%)
  Pallas kernels  15.3 us (11%)
  between operations  14.1 us (10%)
  local copies, waits for them, and re-layouts  6.53 us (5%)
    all_to_all x4, starting transfers between devices, exchange(): return lax.all_to_all(array, axes, 0, 0, tiled=True)  32.9 us
    all_to_all x4, waiting for transfers between devices, exchange(): return lax.all_to_all(array, axes, 0, 0, tiled=True)  27.6 us
    reduce_scatter x1, waiting for transfers between devices, turned_cotangent(): total = lax.psum_scatter(spread.reshape(SNAPS * NODE, H), 'tm', tiled=True)  24.2 us
    all_to_all x1, blocking collectives, exchange(): return lax.all_to_all(array, axes, 0, 0, tiled=True)  16.4 us
    pallas_call x7, Pallas kernels, call(): pl.pallas_call(kernel, out_shape=out, scratch_shapes=list(scratch), compi...  15.3 us
    unnamed x24, local copies, waits for them, and re-layouts  5 us
  transfers between devices with their start and end apart: 5, of which 4 were waited for; matrix products, arithmetic and copies ran while one was open for 1% of the time, Pallas kernels for 4%

profile of v3, /device:TPU:6, one launch (start us, length us, event | category | flops | bytes accessed | tf_op | source)
XLA Modules:
  0.0 140.3 jit_solution(1972678211777578570)
XLA Ops:
  7.2 0.0 copy-start.2
  7.2 0.0 copy-start.3
  7.2 0.0 copy-start.6
  7.2 0.7 copy-done.6
  7.9 0.0 copy-start.9
  7.9 0.7 copy-done.9
  8.6 0.0 copy-start.10
  8.6 0.7 copy-done.10
  9.3 0.0 copy-start.7
  9.3 2.1 %shard_map.113 = (s32[32,8,128]{2,1,0:T(8,128)}, f32[128,16]{1,0:T(8,128)S(1)}) custom-call(s32[8,128]{1,0:T(8,128)S(1)} %bitcast.25, s32[8,128]{1,0:T(8,128)S(1)} %bitcast.26, s32[1,128]{1,0:T(1,128)S(1)} %copy-done.6), custom_call_target="tpu_custom_call" | custom-call | tf_op jit(solution)/shard_map/pallas_call | solution.py:226
  11.4 13.4 %all-to-all-start = ((s32[32,8,128]{2,1,0:T(8,128)}), s32[32,8,128]{2,1,0:T(8,128)S(1)}, u32[]{:S(2)}, u32[]{:S(2)}) async-start(s32[32,8,128]{2,1,0:T(8,128)} %get-tuple-element.6), calls=%async_computation | async-start | bytes 262144 | tf_op jit(solution)/shard_map/all_to_all | solution.py:236
  24.8 2.1 %all-gather = bf16[1,256,256]{2,1,0:T(8,128)(2,1)S(1)} all-gather(bf16[1,128,256]{2,1,0:T(8,128)(2,1)} %param.10), channel_id=2, replica_groups=mesh['tm'=8,'z'=8,'x'=4,'core'=2] {'core'}, dimensions={1}, use_global_device_ids=true | all-gather | bytes 196608 | tf_op jit(solution)/shard_map/all_gather | solution.py:271
  26.9 6.8 %all-to-all-done.msg_ref = s32[32,8,128]{2,1,0:T(8,128)S(1)} async-done(((s32[32,8,128]{2,1,0:T(8,128)}), s32[32,8,128]{2,1,0:T(8,128)S(1)}, u32[]{:S(2)}, u32[]{:S(2)}) %all-to-all-start) | async-done | bytes 131104 | tf_op jit(solution)/shard_map/all_to_all | solution.py:236
  33.7 1.5 %shard_map.116 = bf16[1280,256]{1,0:T(8,128)(2,1)} custom-call(s32[32,8,128]{2,1,0:T(8,128)S(1)} %all-to-all-done.msg_ref, bf16[256,256]{1,0:T(8,128)(2,1)S(1)} %bitcast.21), custom_call_target="tpu_custom_call" | custom-call | tf_op jit(solution)/shard_map/pallas_call | solution.py:226
  35.3 0.0 copy-start.11
  35.3 5.5 %all-to-all-start.1 = ((bf16[32,40,256]{2,1,0:T(8,128)(2,1)}), bf16[32,40,256]{2,1,0:T(8,128)(2,1)S(1)}, u32[]{:S(2)}, u32[]{:S(2)}) async-start(bf16[32,40,256]{2,1,0:T(8,128)(2,1)} %bitcast.6), calls=%async_computation.1 | async-start | bytes 1310720 | tf_op jit(solution)/shard_map/all_to_all | solution.py:236
  40.8 0.0 copy-done.7
  40.8 0.7 shard_map.115.comb_ref
  41.5 17.9 %all-to-all-done.1 = bf16[32,40,256]{2,1,0:T(8,128)(2,1)S(1)} async-done(((bf16[32,40,256]{2,1,0:T(8,128)(2,1)}), bf16[32,40,256]{2,1,0:T(8,128)(2,1)S(1)}, u32[]{:S(2)}, u32[]{:S(2)}) %all-to-all-start.1) | async-done | bytes 655392 | tf_op jit(solution)/shard_map/all_to_all | solution.py:236
  59.4 0.0 copy-done.2
  59.4 0.0 copy-done.3
  59.4 1.2 shard_map.117
  60.6 4.8 %all-to-all-start.2 = ((bf16[8,128,256]{2,1,0:T(8,128)(2,1)}), bf16[8,128,256]{2,1,0:T(8,128)(2,1)S(1)}, u32[]{:S(2)}, u32[]{:S(2)}) async-start(bf16[8,128,256]{2,1,0:T(8,128)(2,1)} %shard_map.117), calls=%async_computation.2 | async-start | bytes 1048576 | tf_op jit(solution)/shard_map/all_to_all | solution.py:236
  65.4 0.0 reduce-scatter.2.cloned.1.call-start
  65.4 0.1 broadcast_in_dim.29
  65.5 0.1 broadcast_in_dim.30
  65.6 0.0 copy-done.11
  65.6 1.0 bitcast_select_fusion
  66.6 0.0 reduce-scatter.2.cloned.1.call-update
  66.6 0.1 pad_add_fusion.where_ref
  66.7 4.1 %shard_map.114 = (bf16[1024,1024]{1,0:T(8,128)(2,1)S(1)}, f32[1024,128]{1,0:T(8,128)S(1)}) custom-call(s32[32,8,128]{2,1,0:T(8,128)S(1)} %all-to-all-done.msg_ref, s32[3]{0:T(128)S(1)} %pad_add_fusion.where_ref), custom_call_target="tpu_custom_call" | custom-call | tf_op jit(solution)/shard_map/pallas_call | solution.py:226
  70.8 2.9 %all-to-all-done.2 = bf16[8,128,256]{2,1,0:T(8,128)(2,1)S(1)} async-done(((bf16[8,128,256]{2,1,0:T(8,128)(2,1)}), bf16[8,128,256]{2,1,0:T(8,128)(2,1)S(1)}, u32[]{:S(2)}, u32[]{:S(2)}) %all-to-all-start.2) | async-done | bytes 524320 | tf_op jit(solution)/shard_map/all_to_all | solution.py:236
  73.7 0.0 copy-start.4
  73.7 0.0 copy-start.8
  73.7 1.5 %shard_map.118 = bf16[8,8,16,256]{3,2,1,0:T(8,128)(2,1)} custom-call(bf16[1024,1024]{1,0:T(8,128)(2,1)S(1)} %get-tuple-element.7.adj_ref, bf16[1024,256]{1,0:T(8,128)(2,1)S(1)} %bitcast.19, f32[1024,128]{1,0:T(8,128)S(1)} %get-tuple-element.9.scale_ref), custom_call_target="tpu_custom_call" | custom-call | tf_op jit(solution)/shard_map/pallas_call | solution.py:226
  75.2 9.2 %all-to-all-start.3 = ((bf16[64,16,256]{2,1,0:T(8,128)(2,1)}), bf16[64,16,256]{2,1,0:T(8,128)(2,1)S(1)}, u32[]{:S(2)}, u32[]{:S(2)}) async-start(bf16[64,16,256]{2,1,0:T(8,128)(2,1)} %bitcast.10), calls=%async_computation.3 | async-start | bytes 1048576 | tf_op jit(solution)/shard_map/all_to_all | solution.py:236
  84.4 24.2 %reduce-scatter.2.cloned.1.call-done = bf16[128,256]{1,0:T(8,128)(2,1)} async-done(((bf16[1024,256]{1,0:T(8,128)(2,1)}), bf16[128,256]{1,0:T(8,128)(2,1)}) %reduce-scatter.2.cloned.1.call-update) | async-done | bytes 65552 | tf_op jit(solution)/shard_map/reduce_scatter | solution.py:244
  108.6 0.0 all-to-all-done.3
  108.6 0.0 copy-done.4
  108.6 0.0 copy-done.8
  108.6 0.0 copy-start
  108.6 1.0 copy-done
  109.7 0.0 copy-start.1
  109.7 1.0 copy-done.1
  110.7 0.0 copy-start.5
  110.7 0.8 copy-done.5
  111.5 4.1 %shard_map.119 = bf16[8,16,1280]{2,1,0:T(8,128)(2,1)S(1)} custom-call(bf16[8,8,16,256]{3,2,1,0:T(8,128)(2,1)S(1)} %bitcast.20, bf16[256,256]{1,0:T(8,128)(2,1)S(1)} %copy-done.4, f32[1,1024]{1,0:T(1,128)S(1)} %bitcast.24, bf16[256,1024]{1,0:T(8,128)(2,1)S(1)} %copy-done, bf16[256,1024]{1,0:T(8,128)(2,1)S(1)} %copy-done.1, bf16[8,16,256]{2,1,0:T(8,128)(2,1)S(1)} %bitcast.23), custom_call_target="tpu_custom_call" | custom-call | tf_op jit(solution)/shard_map/pallas_call | solution.py:226
  115.7 16.4 %all_to_all.25 = bf16[8,16,1280]{2,1,0:T(8,128)(2,1)S(1)} all-to-all(bf16[8,16,1280]{2,1,0:T(8,128)(2,1)S(1)} %shard_map.119), channel_id=1, replica_groups=mesh['tm'=8,'z'=8,'x'=4,'core'=2] {'tm'}, dimensions={0} | all-to-all | bytes 655360 | tf_op jit(solution)/shard_map/all_to_all | solution.py:236
  132.0 0.6 slice.8
  132.7 0.7 slice.9
  (1 shorter events, 0.0 us)
Async XLA Ops:
  7.2 52.2 %copy-start.2 = (bf16[1,128,256]{2,1,0:T(8,128)(2,1)S(1)}, bf16[1,128,256]{2,1,0:T(8,128)(2,1)}, u32[]{:S(2)}) copy-start(bf16[1,128,256]{2,1,0:T(8,128)(2,1)} %param.10) | copy-start | bytes 196612
  7.2 52.2 %copy-start.3 = (bf16[256,256]{1,0:T(8,128)(2,1)S(1)}, bf16[256,256]{1,0:T(8,128)(2,1)}, u32[]{:S(2)}) copy-start(bf16[256,256]{1,0:T(8,128)(2,1)} %weight_ref.2) | copy-start | bytes 393220
  7.2 0.7 copy-start.6
  7.9 0.7 copy-start.9
  8.6 0.7 copy-start.10
  9.3 31.5 %copy-start.7 = (s32[1,128]{1,0:T(1,128)S(1)}, s32[1,128]{1,0:T(1,128)}, u32[]{:S(2)}) copy-start(s32[1,128]{1,0:T(1,128)} %cnt_ref.3) | copy-start | bytes 1540
  11.4 22.3 %all-to-all-start = ((s32[32,8,128]{2,1,0:T(8,128)}), s32[32,8,128]{2,1,0:T(8,128)S(1)}, u32[]{:S(2)}, u32[]{:S(2)}) async-start(s32[32,8,128]{2,1,0:T(8,128)} %get-tuple-element.6), calls=%async_computation | async-start | bytes 262144 | tf_op jit(solution)/shard_map/all_to_all | solution.py:236
  35.3 30.3 %copy-start.11 = (bf16[1,128,256]{2,1,0:T(8,128)(2,1)S(1)}, bf16[1,128,256]{2,1,0:T(8,128)(2,1)}, u32[]{:S(2)}) copy-start(bf16[1,128,256]{2,1,0:T(8,128)(2,1)} %param.19) | copy-start | bytes 196612
  35.3 24.1 %all-to-all-start.1 = ((bf16[32,40,256]{2,1,0:T(8,128)(2,1)}), bf16[32,40,256]{2,1,0:T(8,128)(2,1)S(1)}, u32[]{:S(2)}, u32[]{:S(2)}) async-start(bf16[32,40,256]{2,1,0:T(8,128)(2,1)} %bitcast.6), calls=%async_computation.1 | async-start | bytes 1310720 | tf_op jit(solution)/shard_map/all_to_all | solution.py:236
  60.6 13.1 %all-to-all-start.2 = ((bf16[8,128,256]{2,1,0:T(8,128)(2,1)}), bf16[8,128,256]{2,1,0:T(8,128)(2,1)S(1)}, u32[]{:S(2)}, u32[]{:S(2)}) async-start(bf16[8,128,256]{2,1,0:T(8,128)(2,1)} %shard_map.117), calls=%async_computation.2 | async-start | bytes 1048576 | tf_op jit(solution)/shard_map/all_to_all | solution.py:236
  65.4 43.2 %reduce-scatter.2.cloned.1.call-start = ((), (), s32[]{:S(2)}) async-start(), calls=%async_computation.6 | async-start | bytes 589824 | tf_op jit(solution)/shard_map/reduce_scatter | solution.py:244
  73.7 34.9 %copy-start.4 = (bf16[256,256]{1,0:T(8,128)(2,1)S(1)}, bf16[256,256]{1,0:T(8,128)(2,1)}, u32[]{:S(2)}) copy-start(bf16[256,256]{1,0:T(8,128)(2,1)} %weight_ref.3) | copy-start | bytes 393220
  73.7 34.9 %copy-start.8 = (f32[1024]{0:T(1024)S(1)}, f32[1024]{0:T(1024)}, u32[]{:S(2)}) copy-start(f32[1024]{0:T(1024)} %param.18) | copy-start | bytes 12292
  75.2 33.4 %all-to-all-start.3 = ((bf16[64,16,256]{2,1,0:T(8,128)(2,1)}), bf16[64,16,256]{2,1,0:T(8,128)(2,1)S(1)}, u32[]{:S(2)}, u32[]{:S(2)}) async-start(bf16[64,16,256]{2,1,0:T(8,128)(2,1)} %bitcast.10), calls=%async_computation.3 | async-start | bytes 1048576 | tf_op jit(solution)/shard_map/all_to_all | solution.py:236
  108.6 1.0 copy-start
  109.7 1.0 copy-start.1
  110.7 0.8 copy-start.5
Sparse Core Ops, SparseCore 0:
  69.0 39.5 reduce-scatter.1

commit v4 on v1

v4 whole, which is shorter than its diff:
```python
import jax
import jax.numpy as jnp
from jax import lax
from jax.experimental import pallas as pl
from jax.experimental.pallas import tpu as pltpu
from jax.sharding import Mesh
from jax.sharding import PartitionSpec as P

H = 256
KNB = 8
NODE = 128
SNAPS = 8
CHIPS = 32
CAP = 40
SLOTS = CHIPS * CAP
LANES = 128
BF16 = jnp.bfloat16
F32 = jnp.float32
NT = ((1,), (1,))


def iota(shape, dim):
    return lax.broadcasted_iota(jnp.int32, shape, dim)


def matmul(a, b, dims=((1,), (0,))):
    return lax.dot_general(a, b, (dims, ((), ())), preferred_element_type=F32)


def fetch(pairs, sems):
    copies = [pltpu.make_async_copy(a, b, sems.at[i]) for i, (a, b) in enumerate(pairs)]
    for copy in copies:
        copy.start()
    return copies


def plan_kernel(owner_hbm, row_hbm, wanted_ref, place_ref, owner_ref, row_ref, sems):
    for copy in fetch(((owner_hbm, owner_ref), (row_hbm, row_ref)), sems):
        copy.wait()
    owner = owner_ref[...]
    value = ((owner % 2) * NODE + row_ref[...]).astype(F32)
    chip = owner // 2
    upper = jnp.where(iota((LANES, LANES), 0) < iota((LANES, LANES), 1), 1.0, 0.0).astype(BF16)
    base = jnp.zeros((CHIPS, 1), F32)
    wanted = jnp.zeros((CHIPS, LANES), F32)
    place = jnp.zeros((NODE, 2 * KNB), F32)
    lane = iota((1, LANES), 1)
    sub = iota((2 * KNB, LANES), 0)
    for i in range(KNB):
        chip_i = chip[i : i + 1, :]
        onehot = jnp.where(iota((CHIPS, LANES), 0) == chip_i, 1.0, 0.0)
        before = matmul(onehot.astype(BF16), upper) + base
        base = base + jnp.sum(onehot, 1, keepdims=True)
        rank = jnp.sum(onehot * before, 0, keepdims=True)
        ranks = jnp.where(iota((LANES, LANES), 0).astype(F32) == rank, 1.0, 0.0).astype(BF16)
        wanted = wanted + matmul((onehot * value[i : i + 1, :]).astype(BF16), ranks, NT)
        group = jnp.where(iota((NODE, LANES), 0) == i * (LANES // KNB) + lane // KNB, 1.0, 0.0)
        coded = jnp.where(sub < KNB, chip_i.astype(F32), rank)
        coded = jnp.where(sub % KNB == lane % KNB, coded, 0.0)
        place = place + matmul(group.astype(BF16), coded.astype(BF16), NT)
    wanted_ref[...] = wanted
    place_ref[...] = place


def column(row):
    eye = iota((NODE, NODE), 0) == iota((NODE, NODE), 1)
    return jnp.sum(jnp.where(eye, row, 0.0), 1, keepdims=True)


def comb_kernel(place_ref, cnt_ref, comb_ref):
    count = column(cnt_ref[...].astype(F32))
    place = place_ref[:, :KNB] * CAP + place_ref[:, KNB:]
    place = jnp.where(iota((NODE, KNB), 1).astype(F32) < count, place, -1.0)
    spot = iota((NODE, SLOTS), 1).astype(F32)
    comb = jnp.zeros((NODE, SLOTS), F32)
    for k in range(KNB):
        comb = comb + jnp.where(spot == place[:, k : k + 1], 1.0, 0.0)
    comb_ref[...] = comb.astype(BF16)


def pick_kernel(asked_ref, x_ref, pick_ref, out_ref):
    eye = jnp.where(iota((LANES, LANES), 0) == iota((LANES, LANES), 1), 1.0, 0.0).astype(BF16)
    turned = matmul(eye, asked_ref[...].astype(BF16), NT)
    col = iota((CAP, H), 1).astype(F32)
    x = x_ref[...]
    for d in range(0, CHIPS, 2):
        both = [jnp.where(turned[:CAP, e : e + 1] == col, 1.0, 0.0) for e in (d, d + 1)]
        pick = jnp.concatenate(both, 0).astype(BF16)
        pick_ref[d * CAP : (d + 2) * CAP, :] = pick
        out_ref[d * CAP : (d + 2) * CAP, :] = matmul(pick, x).astype(BF16)


def again_kernel(pick_ref, x_ref, out_ref):
    out_ref[...] = matmul(pick_ref[...], x_ref[...]).astype(BF16)


def convolved(comb_ref, arrived_ref, x_ref, cnt_ref, weight_ref):
    count = column(cnt_ref[...].astype(F32))
    summed = x_ref[...].astype(F32) + matmul(comb_ref[...], arrived_ref[...])
    agg = (summed * (1.0 / (count + 1.0))).astype(BF16)
    return jnp.maximum(matmul(agg, weight_ref[...]), 0.0).astype(BF16)


def first_kernel(*refs):
    refs[-1][...] = convolved(*refs[:-1])


def second_kernel(*refs):
    x = convolved(*refs[:-1])
    for t in range(SNAPS):
        refs[-1][t] = x


def lstm_kernel(
    x_ref, cot_ref, w_in_ref, w_rec_ref, bias_ref, snap_ref, hidden_ref, grads_ref, saved_ref
):
    snap = snap_ref[0]
    h = None
    c = jnp.zeros((NODE, H), F32)
    for t in range(SNAPS):
        z = (matmul(x_ref[t], w_in_ref[...]) + bias_ref[...]).astype(BF16)
        gates = z.astype(F32)
        if t > 0:
            gates = gates + matmul(h, w_rec_ref[...])
        i = jax.nn.sigmoid(gates[:, :H])
        f = jax.nn.sigmoid(gates[:, H : 2 * H])
        g = jnp.tanh(gates[:, 2 * H : 3 * H])
        o = jax.nn.sigmoid(gates[:, 3 * H :])
        c_new = f * c + i * g
        tc = jnp.tanh(c_new)
        h = (o * tc).astype(BF16)

        @pl.when(snap == t)
        def _(h=h):
            hidden_ref[...] = h

        saved_ref[t, 0] = f
        saved_ref[t, 1] = o * (1.0 - tc * tc)
        saved_ref[t, 2] = g * i * (1.0 - i)
        saved_ref[t, 3] = c * f * (1.0 - f)
        saved_ref[t, 4] = i * (1.0 - g * g)
        saved_ref[t, 5] = tc * o * (1.0 - o)
        c = c_new
    dh = jnp.zeros((NODE, H), F32)
    dc = jnp.zeros((NODE, H), F32)
    for t in range(SNAPS - 1, -1, -1):
        dh = dh + cot_ref[t].astype(F32)
        dc = dc + dh * saved_ref[t, 1]
        grad = jnp.concatenate(
            [dc * saved_ref[t, 2], dc * saved_ref[t, 3], dc * saved_ref[t, 4], dh * saved_ref[t, 5]],
            1,
        ).astype(BF16)

        @pl.when(snap == t)
        def _(grad=grad):
            grads_ref[...] = grad

        if t > 0:
            dh = matmul(grad, w_rec_ref[...], NT)
            dc = dc * saved_ref[t, 0]


def call(kernel, out, *args, scratch=(), in_specs=None, limit=16):
    more = {} if in_specs is None else {"in_specs": in_specs}
    return pl.pallas_call(
        kernel,
        out_shape=out,
        scratch_shapes=list(scratch),
        compiler_params=pltpu.CompilerParams(vmem_limit_bytes=limit * 1024 * 1024),
        **more,
    )(*args)


def shaped(shape, dtype=BF16):
    return jax.ShapeDtypeStruct(shape, dtype)


def exchange(array, axes):
    return lax.all_to_all(array, axes, 0, 0, tiled=True)


def shards(
    features, nbr_owner, nbr_row, counts, weight_one, weight_two, w_in, w_rec, gate_bias, cotangent
):
    vmem = pl.BlockSpec(memory_space=pltpu.VMEM)
    chips = ("z", "x")
    x = features[0]
    wanted, place = call(
        plan_kernel,
        (shaped((CHIPS, LANES), F32), shaped((NODE, 2 * KNB), F32)),
        nbr_owner.reshape(KNB, LANES),
        nbr_row.reshape(KNB, LANES),
        in_specs=[pl.BlockSpec(memory_space=pltpu.HBM)] * 2,
        scratch=(
            pltpu.VMEM((KNB, LANES), jnp.int32),
            pltpu.VMEM((KNB, LANES), jnp.int32),
            pltpu.SemaphoreType.DMA((2,)),
        ),
        limit=60,
    )
    asked = exchange(wanted, chips)
    pair = lax.all_gather(x, "core", tiled=True)
    pick, outgoing = call(pick_kernel, (shaped((SLOTS, H)), shaped((SLOTS, H))), asked, pair)
    outgoing, cot = lax.optimization_barrier((outgoing, cotangent))
    arrived = exchange(outgoing.reshape(CHIPS, CAP, H), chips).reshape(SLOTS, H)
    cots = lax.all_gather(cot, "tm", tiled=True)
    comb = call(comb_kernel, shaped((NODE, SLOTS)), place, counts)
    comb, cots = lax.optimization_barrier((comb, cots))
    x = call(first_kernel, shaped((NODE, H)), comb, arrived, x, counts, weight_one)
    pair = lax.all_gather(x, "core", tiled=True)
    outgoing = call(again_kernel, shaped((SLOTS, H)), pick, pair)
    arrived = exchange(outgoing.reshape(CHIPS, CAP, H), chips).reshape(SLOTS, H)
    x = call(second_kernel, shaped((SNAPS, NODE, H)), comb, arrived, x, counts, weight_two)
    xs = exchange(x, "tm")
    hidden, grads = call(
        lstm_kernel,
        (shaped((NODE, H)), shaped((NODE, 4 * H))),
        xs,
        cots,
        w_in,
        w_rec,
        gate_bias.reshape(1, 4 * H),
        lax.axis_index("tm").reshape(1).astype(jnp.int32),
        in_specs=[vmem] * 5 + [pl.BlockSpec(memory_space=pltpu.SMEM)],
        scratch=(pltpu.VMEM((SNAPS, 6, NODE, H), F32),),
    )
    return hidden[None], grads[None]


def solution(mesh):
    mesh = Mesh(mesh.devices.reshape(8, 8, 4, 2), ("tm", "z", "x", "core"))
    acct = ("z", "x", "core")
    return jax.shard_map(
        shards,
        mesh=mesh,
        in_specs=(
            P("tm", acct, None),
            P("tm", acct, None),
            P("tm", acct),
            P("tm", acct),
            P(),
            P(),
            P(),
            P(),
            P(),
            P("tm", acct, None),
        ),
        out_specs=(P("tm", acct, None), P("tm", acct, None)),
        check_vma=False,
    )
```

time: 114 us -> 124 us (1.088)
  blocking collectives: 82.9 us -> 61.1 us
  waiting for transfers between devices: 5.77 us -> 22.1 us
  starting transfers between devices: 13.4 us -> 24.6 us
  Pallas kernels: 7.14 us -> 13.9 us
  local copies, waits for them, and re-layouts: 3.84 us -> 0.8 us
    all_to_all x4 -> x1, blocking collectives: 78.9 us -> 29.7 us  [exchange(): return lax.all_to_all(array, axes, 0, 0, tiled=True)]
    all_gather x0 -> x1, blocking collectives: none -> 27.4 us  [shards(): cots = lax.all_gather(cot, 'tm', tiled=True)]
    all_to_all x1 -> x3, waiting for transfers between devices: 5.77 us -> 22.1 us  [exchange(): return lax.all_to_all(array, axes, 0, 0, tiled=True)]
    all_to_all x1 -> x3, starting transfers between devices: 13.4 us -> 24.6 us  [exchange(): return lax.all_to_all(array, axes, 0, 0, tiled=True)]
    pallas_call x6 -> x7, Pallas kernels: 7.14 us -> 13.9 us  [call(): pl.pallas_call(kernel, out_shape=out, scratch_shapes=list(scratch), compi...]
    unnamed x20 -> x18, local copies, waits for them, and re-layouts: 2.48 us -> 0.8 us
    slice x2 -> x0, local copies, waits for them, and re-layouts: 1.36 us -> none  [shards(): return (result[:, :, :H], result[:, :, H:])]
  transfers between devices with their start and end apart: 1 -> 3, of which waited for: 1 -> 2; matrix products, arithmetic and copies ran while one was open for 0% -> 0% of each run, Pallas kernels for 0% -> 1%
where the time goes in v4:
time: 124 us; the launch traced here: 123 us
  blocking collectives  61.1 us (49%)
  starting transfers between devices  24.6 us (20%)
  waiting for transfers between devices  22.1 us (18%)
  Pallas kernels  13.9 us (11%)
    all_to_all x1, blocking collectives, exchange(): return lax.all_to_all(array, axes, 0, 0, tiled=True)  29.7 us
    all_gather x1, blocking collectives, shards(): cots = lax.all_gather(cot, 'tm', tiled=True)  27.4 us
    all_to_all x3, starting transfers between devices, exchange(): return lax.all_to_all(array, axes, 0, 0, tiled=True)  24.6 us
    all_to_all x3, waiting for transfers between devices, exchange(): return lax.all_to_all(array, axes, 0, 0, tiled=True)  22.1 us
    pallas_call x7, Pallas kernels, call(): pl.pallas_call(kernel, out_shape=out, scratch_shapes=list(scratch), compi...  13.9 us
    all_gather x2, blocking collectives, shards(): pair = lax.all_gather(x, 'core', tiled=True)  4.01 us
  transfers between devices with their start and end apart: 3, of which 2 were waited for; matrix products, arithmetic and copies ran while one was open for 0% of the time, Pallas kernels for 1%

profile of v4, /device:TPU:6, one launch (start us, length us, event | category | flops | bytes accessed | tf_op | source)
XLA Modules:
  0.0 123.2 jit_solution(16360125986983580822)
XLA Ops:
  0.6 2.6 %shard_map.113 = (f32[32,128]{1,0:T(8,128)}, f32[128,16]{1,0:T(8,128)}) custom-call(s32[8,128]{1,0:T(8,128)} %bitcast.24, s32[8,128]{1,0:T(8,128)} %bitcast.25), custom_call_target="tpu_custom_call" | custom-call | tf_op jit(solution)/shard_map/pallas_call | solution.py:165
  3.2 13.4 %all-to-all-start = ((f32[32,1,128]{2,1,0:T(1,128)}), f32[32,1,128]{2,1,0:T(1,128)S(1)}, u32[]{:S(2)}, u32[]{:S(2)}) async-start(f32[32,1,128]{2,1,0:T(1,128)} %bitcast.23), calls=%async_computation | async-start | bytes 32768 | tf_op jit(solution)/shard_map/all_to_all | solution.py:179
  16.7 2.1 %all-gather = bf16[1,256,256]{2,1,0:T(8,128)(2,1)S(1)} all-gather(bf16[1,128,256]{2,1,0:T(8,128)(2,1)} %param.10), channel_id=2, replica_groups=mesh['tm'=8,'z'=8,'x'=4,'core'=2] {'core'}, dimensions={1}, use_global_device_ids=true | all-gather | bytes 196608 | tf_op jit(solution)/shard_map/all_gather | solution.py:202
  18.8 5.8 %all-to-all-done = f32[32,1,128]{2,1,0:T(1,128)S(1)} async-done(((f32[32,1,128]{2,1,0:T(1,128)}), f32[32,1,128]{2,1,0:T(1,128)S(1)}, u32[]{:S(2)}, u32[]{:S(2)}) %all-to-all-start) | async-done | bytes 16416 | tf_op jit(solution)/shard_map/all_to_all | solution.py:179
  24.5 1.5 %shard_map.115 = (bf16[1280,256]{1,0:T(8,128)(2,1)S(1)}, bf16[1280,256]{1,0:T(8,128)(2,1)}) custom-call(f32[32,128]{1,0:T(8,128)S(1)} %bitcast.21, bf16[256,256]{1,0:T(8,128)(2,1)S(1)} %bitcast.19), custom_call_target="tpu_custom_call" | custom-call | tf_op jit(solution)/shard_map/pallas_call | solution.py:165
  26.0 0.0 copy-start.5
  26.0 5.7 %all-to-all-start.1 = ((bf16[32,40,256]{2,1,0:T(8,128)(2,1)}), bf16[32,40,256]{2,1,0:T(8,128)(2,1)S(1)}, u32[]{:S(2)}, u32[]{:S(2)}) async-start(bf16[32,40,256]{2,1,0:T(8,128)(2,1)} %bitcast.6), calls=%async_computation.1 | async-start | bytes 1310720 | tf_op jit(solution)/shard_map/all_to_all | solution.py:179
  31.7 0.0 copy-start.6
  31.8 0.0 copy-done.5
  31.8 0.6 copy-done.6
  32.4 0.0 copy-start.8
  32.4 0.7 shard_map.114.refs_0_
  33.1 0.1 copy-done.8
  33.2 0.0 copy-start.2
  33.2 0.0 copy-start.3
  33.2 27.4 %all_gather.10.cot_ref = bf16[8,128,256]{2,1,0:T(8,128)(2,1)S(1)} all-gather(bf16[1,128,256]{2,1,0:T(8,128)(2,1)S(1)} %copy-done.8), channel_id=1, replica_groups=mesh['tm'=8,'z'=8,'x'=4,'core'=2] {'tm'}, dimensions={0}, use_global_device_ids=true | all-gather | bytes 589824 | tf_op jit(solution)/shard_map/all_gather | solution.py:206
  60.6 0.0 all-to-all-done.1
  60.6 0.0 copy-done.2
  60.6 0.0 copy-done.3
  60.6 0.4 shard_map.116.refs_2_
  61.0 1.9 %all_gather.11.x_ref = bf16[256,256]{1,0:T(8,128)(2,1)S(1)} all-gather(bf16[128,256]{1,0:T(8,128)(2,1)S(1)} %shard_map.116.refs_2_), channel_id=1, replica_groups=mesh['tm'=8,'z'=8,'x'=4,'core'=2] {'core'}, dimensions={0}, use_global_device_ids=true | all-gather | bytes 196608 | tf_op jit(solution)/shard_map/all_gather | solution.py:210
  62.9 0.3 shard_map.117
  63.3 0.0 copy-start.4
  63.3 29.7 %all_to_all.26 = bf16[32,40,256]{2,1,0:T(8,128)(2,1)S(1)} all-to-all(bf16[32,40,256]{2,1,0:T(8,128)(2,1)S(1)} %bitcast.18), channel_id=1, replica_groups=mesh['tm'=8,'z'=8,'x'=4,'core'=2] {'z','x'}, dimensions={0} | all-to-all | bytes 1310720 | tf_op jit(solution)/shard_map/all_to_all | solution.py:179
  92.9 0.0 copy-done.4
  93.0 1.2 shard_map.118
  94.2 0.0 copy-start
  94.2 0.0 copy-start.1
  94.2 5.5 %all-to-all-start.3 = ((bf16[8,128,256]{2,1,0:T(8,128)(2,1)}), bf16[8,128,256]{2,1,0:T(8,128)(2,1)S(1)}, u32[]{:S(2)}, u32[]{:S(2)}) async-start(bf16[8,128,256]{2,1,0:T(8,128)(2,1)} %shard_map.118), calls=%async_computation.3 | async-start | bytes 1048576 | tf_op jit(solution)/shard_map/all_to_all | solution.py:179
  99.6 0.0 copy-start.7
  99.6 16.3 %all-to-all-done.3.x_ref = bf16[8,128,256]{2,1,0:T(8,128)(2,1)S(1)} async-done(((bf16[8,128,256]{2,1,0:T(8,128)(2,1)}), bf16[8,128,256]{2,1,0:T(8,128)(2,1)S(1)}, u32[]{:S(2)}, u32[]{:S(2)}) %all-to-all-start.3) | async-done | bytes 524320 | tf_op jit(solution)/shard_map/all_to_all | solution.py:179
  116.0 0.0 copy-done
  116.0 0.0 copy-done.1
  116.0 0.0 copy-done.7
  116.0 7.2 %shard_map.119 = (bf16[128,256]{1,0:T(8,128)(2,1)}, bf16[128,1024]{1,0:T(8,128)(2,1)}) custom-call(bf16[8,128,256]{2,1,0:T(8,128)(2,1)S(1)} %all-to-all-done.3.x_ref, bf16[8,128,256]{2,1,0:T(8,128)(2,1)S(1)} %all_gather.10.cot_ref, bf16[256,1024]{1,0:T(8,128)(2,1)S(1)} %copy-done, bf16[256,1024]{1,0:T(8,128)(2,1)S(1)} %copy-done.1, f32[1,1024]{1,0:T(1,128)S(1)} %bitcast.22, ...), custom_call_target="tpu_custom_call" | custom-call | tf_op jit(solution)/shard_map/pallas_call | solution.py:165
Async XLA Ops:
  3.2 21.3 %all-to-all-start = ((f32[32,1,128]{2,1,0:T(1,128)}), f32[32,1,128]{2,1,0:T(1,128)S(1)}, u32[]{:S(2)}, u32[]{:S(2)}) async-start(f32[32,1,128]{2,1,0:T(1,128)} %bitcast.23), calls=%async_computation | async-start | bytes 32768 | tf_op jit(solution)/shard_map/all_to_all | solution.py:179
  26.0 5.7 %copy-start.5 = (f32[128,16]{1,0:T(8,128)S(1)}, f32[128,16]{1,0:T(8,128)}, u32[]{:S(2)}) copy-start(f32[128,16]{1,0:T(8,128)} %get-tuple-element.12.place_ref) | copy-start | bytes 24580
  26.0 34.6 %all-to-all-start.1 = ((bf16[32,40,256]{2,1,0:T(8,128)(2,1)}), bf16[32,40,256]{2,1,0:T(8,128)(2,1)S(1)}, u32[]{:S(2)}, u32[]{:S(2)}) async-start(bf16[32,40,256]{2,1,0:T(8,128)(2,1)} %bitcast.6), calls=%async_computation.1 | async-start | bytes 1310720 | tf_op jit(solution)/shard_map/all_to_all | solution.py:179
  31.7 0.7 copy-start.6
  32.4 0.8 copy-start.8
  33.2 27.4 %copy-start.2 = (bf16[1,128,256]{2,1,0:T(8,128)(2,1)S(1)}, bf16[1,128,256]{2,1,0:T(8,128)(2,1)}, u32[]{:S(2)}) copy-start(bf16[1,128,256]{2,1,0:T(8,128)(2,1)} %param.10) | copy-start | bytes 196612
  33.2 27.4 %copy-start.3 = (bf16[256,256]{1,0:T(8,128)(2,1)S(1)}, bf16[256,256]{1,0:T(8,128)(2,1)}, u32[]{:S(2)}) copy-start(bf16[256,256]{1,0:T(8,128)(2,1)} %refs_4_.2) | copy-start | bytes 393220
  63.3 29.7 %copy-start.4 = (bf16[256,256]{1,0:T(8,128)(2,1)S(1)}, bf16[256,256]{1,0:T(8,128)(2,1)}, u32[]{:S(2)}) copy-start(bf16[256,256]{1,0:T(8,128)(2,1)} %refs_4_.3) | copy-start | bytes 393220
  94.2 21.8 %copy-start = (bf16[256,1024]{1,0:T(8,128)(2,1)S(1)}, bf16[256,1024]{1,0:T(8,128)(2,1)}, u32[]{:S(2)}) copy-start(bf16[256,1024]{1,0:T(8,128)(2,1)} %w_in_ref.1) | copy-start | bytes 1572868
  94.2 21.8 %copy-start.1 = (bf16[256,1024]{1,0:T(8,128)(2,1)S(1)}, bf16[256,1024]{1,0:T(8,128)(2,1)}, u32[]{:S(2)}) copy-start(bf16[256,1024]{1,0:T(8,128)(2,1)} %w_rec_ref.1) | copy-start | bytes 1572868
  94.2 21.8 %all-to-all-start.3 = ((bf16[8,128,256]{2,1,0:T(8,128)(2,1)}), bf16[8,128,256]{2,1,0:T(8,128)(2,1)S(1)}, u32[]{:S(2)}, u32[]{:S(2)}) async-start(bf16[8,128,256]{2,1,0:T(8,128)(2,1)} %shard_map.118), calls=%async_computation.3 | async-start | bytes 1048576 | tf_op jit(solution)/shard_map/all_to_all | solution.py:179
  99.6 16.4 %copy-start.7 = (f32[1024]{0:T(1024)S(1)}, f32[1024]{0:T(1024)}, u32[]{:S(2)}) copy-start(f32[1024]{0:T(1024)} %param.18) | copy-start | bytes 12292

commit v5 on v4

--- a/solution.py
+++ b/solution.py
@@ -13,6 +13,7 @@
 CHIPS = 32
 CAP = 40
 SLOTS = CHIPS * CAP
+PART = NODE // SNAPS
 LANES = 128
 BF16 = jnp.bfloat16
 F32 = jnp.float32
@@ -105,59 +106,78 @@
     refs[-1][...] = convolved(*refs[:-1])
 
 
-def second_kernel(*refs):
-    x = convolved(*refs[:-1])
+def second_kernel(
+    comb_ref, arrived_ref, x_ref, cnt_ref, weight_ref, cot_ref, w_in_ref, bias_ref, out_ref, z_ref
+):
+    x = convolved(comb_ref, arrived_ref, x_ref, cnt_ref, weight_ref)
+    out_ref[:, :H] = x
+    out_ref[:, H:] = cot_ref[...]
+    z_ref[...] = (matmul(x, w_in_ref[...]) + bias_ref[...]).astype(BF16)
+
+
+def gated(gates, c):
+    i = jax.nn.sigmoid(gates[:, :H])
+    f = jax.nn.sigmoid(gates[:, H : 2 * H])
+    g = jnp.tanh(gates[:, 2 * H : 3 * H])
+    o = jax.nn.sigmoid(gates[:, 3 * H :])
+    c_new = f * c + i * g
+    return i, f, g, o, c_new, jnp.tanh(c_new)
+
+
+def chain_kernel(xc_ref, w_in_ref, w_rec_ref, bias_ref, out_ref, z_ref, saved_ref):
+    x = xc_ref[:, :, :H].reshape(NODE, H)
+    z = matmul(x, w_in_ref[...]) + bias_ref[...]
+    z_ref[...] = z.astype(BF16).astype(F32)
+    h = jnp.zeros((PART, H), BF16)
+    c = jnp.zeros((PART, H), F32)
     for t in range(SNAPS):
-        refs[-1][t] = x
-
-
-def lstm_kernel(
-    x_ref, cot_ref, w_in_ref, w_rec_ref, bias_ref, snap_ref, hidden_ref, grads_ref, saved_ref
-):
-    snap = snap_ref[0]
-    h = None
-    c = jnp.zeros((NODE, H), F32)
-    for t in range(SNAPS):
-        z = (matmul(x_ref[t], w_in_ref[...]) + bias_ref[...]).astype(BF16)
-        gates = z.astype(F32)
+        out_ref[t, :, :H] = h
+        out_ref[t, :, H : 2 * H] = c.astype(BF16)
+        gates = z_ref[t * PART : (t + 1) * PART, :]
         if t > 0:
             gates = gates + matmul(h, w_rec_ref[...])
-        i = jax.nn.sigmoid(gates[:, :H])
-        f = jax.nn.sigmoid(gates[:, H : 2 * H])
-        g = jnp.tanh(gates[:, 2 * H : 3 * H])
-        o = jax.nn.sigmoid(gates[:, 3 * H :])
-        c_new = f * c + i * g
-        tc = jnp.tanh(c_new)
+        i, f, g, o, c_new, tc = gated(gates, c)
         h = (o * tc).astype(BF16)
-
-        @pl.when(snap == t)
-        def _(h=h):
-            hidden_ref[...] = h
-
         saved_ref[t, 0] = f
         saved_ref[t, 1] = o * (1.0 - tc * tc)
-        saved_ref[t, 2] = g * i * (1.0 - i)
-        saved_ref[t, 3] = c * f * (1.0 - f)
-        saved_ref[t, 4] = i * (1.0 - g * g)
-        saved_ref[t, 5] = tc * o * (1.0 - o)
+        if t > 0:
+            saved_ref[t, 2] = g * i * (1.0 - i)
+            saved_ref[t, 3] = c * f * (1.0 - f)
+            saved_ref[t, 4] = i * (1.0 - g * g)
+            saved_ref[t, 5] = tc * o * (1.0 - o)
         c = c_new
-    dh = jnp.zeros((NODE, H), F32)
-    dc = jnp.zeros((NODE, H), F32)
+    dh = jnp.zeros((PART, H), F32)
+    dc = jnp.zeros((PART, H), F32)
     for t in range(SNAPS - 1, -1, -1):
-        dh = dh + cot_ref[t].astype(F32)
+        dh = dh + xc_ref[t, :, H:].astype(F32)
         dc = dc + dh * saved_ref[t, 1]
-        grad = jnp.concatenate(
-            [dc * saved_ref[t, 2], dc * saved_ref[t, 3], dc * saved_ref[t, 4], dh * saved_ref[t, 5]],
-            1,
-        ).astype(BF16)
-
-        @pl.when(snap == t)
-        def _(grad=grad):
-            grads_ref[...] = grad
-
+        out_ref[t, :, 2 * H : 3 * H] = dh.astype(BF16)
+        out_ref[t, :, 3 * H :] = dc.astype(BF16)
         if t > 0:
+            grad = jnp.concatenate(
+                [
+                    dc * saved_ref[t, 2],
+                    dc * saved_ref[t, 3],
+                    dc * saved_ref[t, 4],
+                    dh * saved_ref[t, 5],
+                ],
+                1,
+            ).astype(BF16)
             dh = matmul(grad, w_rec_ref[...], NT)
             dc = dc * saved_ref[t, 0]
+
+
+def last_kernel(back_ref, z_ref, w_rec_ref, hidden_ref, grads_ref):
+    c = back_ref[:, H : 2 * H].astype(F32)
+    dh = back_ref[:, 2 * H : 3 * H].astype(F32)
+    dc = back_ref[:, 3 * H :].astype(F32)
+    gates = z_ref[...].astype(F32) + matmul(back_ref[:, :H], w_rec_ref[...])
+    i, f, g, o, c_new, tc = gated(gates, c)
+    hidden_ref[...] = (o * tc).astype(BF16)
+    grads_ref[:, :H] = (dc * g * i * (1.0 - i)).astype(BF16)
+    grads_ref[:, H : 2 * H] = (dc * c * f * (1.0 - f)).astype(BF16)
+    grads_ref[:, 2 * H : 3 * H] = (dc * i * (1.0 - g * g)).astype(BF16)
+    grads_ref[:, 3 * H :] = (dh * tc * o * (1.0 - o)).astype(BF16)
 
 
 def call(kernel, out, *args, scratch=(), in_specs=None, limit=16):
@@ -182,8 +202,8 @@
 def shards(
     features, nbr_owner, nbr_row, counts, weight_one, weight_two, w_in, w_rec, gate_bias, cotangent
 ):
-    vmem = pl.BlockSpec(memory_space=pltpu.VMEM)
     chips = ("z", "x")
+    bias = gate_bias.reshape(1, 4 * H)
     x = features[0]
     wanted, place = call(
         plan_kernel,
@@ -200,30 +220,38 @@
     )
     asked = exchange(wanted, chips)
     pair = lax.all_gather(x, "core", tiled=True)
+    comb = call(comb_kernel, shaped((NODE, SLOTS)), place, counts)
+    asked, pair, comb = lax.optimization_barrier((asked, pair, comb))
     pick, outgoing = call(pick_kernel, (shaped((SLOTS, H)), shaped((SLOTS, H))), asked, pair)
-    outgoing, cot = lax.optimization_barrier((outgoing, cotangent))
     arrived = exchange(outgoing.reshape(CHIPS, CAP, H), chips).reshape(SLOTS, H)
-    cots = lax.all_gather(cot, "tm", tiled=True)
-    comb = call(comb_kernel, shaped((NODE, SLOTS)), place, counts)
-    comb, cots = lax.optimization_barrier((comb, cots))
     x = call(first_kernel, shaped((NODE, H)), comb, arrived, x, counts, weight_one)
     pair = lax.all_gather(x, "core", tiled=True)
     outgoing = call(again_kernel, shaped((SLOTS, H)), pick, pair)
     arrived = exchange(outgoing.reshape(CHIPS, CAP, H), chips).reshape(SLOTS, H)
-    x = call(second_kernel, shaped((SNAPS, NODE, H)), comb, arrived, x, counts, weight_two)
-    xs = exchange(x, "tm")
-    hidden, grads = call(
-        lstm_kernel,
-        (shaped((NODE, H)), shaped((NODE, 4 * H))),
-        xs,
-        cots,
+    both, z = call(
+        second_kernel,
+        (shaped((NODE, 2 * H)), shaped((NODE, 4 * H))),
+        comb,
+        arrived,
+        x,
+        counts,
+        weight_two,
+        cotangent[0],
+        w_in,
+        bias,
+    )
+    both = exchange(both.reshape(SNAPS, PART, 2 * H), "tm")
+    back = call(
+        chain_kernel,
+        shaped((SNAPS, PART, 4 * H)),
+        both,
         w_in,
         w_rec,
-        gate_bias.reshape(1, 4 * H),
-        lax.axis_index("tm").reshape(1).astype(jnp.int32),
-        in_specs=[vmem] * 5 + [pl.BlockSpec(memory_space=pltpu.SMEM)],
-        scratch=(pltpu.VMEM((SNAPS, 6, NODE, H), F32),),
-    )
+        bias,
+        scratch=(pltpu.VMEM((NODE, 4 * H), F32), pltpu.VMEM((SNAPS, 6, PART, H), F32)),
+    )
+    back = exchange(back, "tm").reshape(NODE, 4 * H)
+    hidden, grads = call(last_kernel, (shaped((NODE, H)), shaped((NODE, 4 * H))), back, z, w_rec)
     return hidden[None], grads[None]
 
 

time: 124 us -> 115 us (0.927)
  blocking collectives: 61.1 us -> 84.2 us
  waiting for transfers between devices: 22.1 us -> 3.66 us
  starting transfers between devices: 24.6 us -> 13.4 us
  Pallas kernels: 13.9 us -> 9.89 us
  local copies, waits for them, and re-layouts: 0.8 us -> 2.32 us
    all_to_all x1 -> x4, blocking collectives: 29.7 us -> 80.4 us  [exchange(): return lax.all_to_all(array, axes, 0, 0, tiled=True)]
    all_gather x1 -> x0, blocking collectives: 27.4 us -> none  [shards(): cots = lax.all_gather(cot, 'tm', tiled=True)]
    all_to_all x3 -> x1, waiting for transfers between devices: 22.1 us -> 3.66 us  [exchange(): return lax.all_to_all(array, axes, 0, 0, tiled=True)]
    all_to_all x3 -> x1, starting transfers between devices: 24.6 us -> 13.4 us  [exchange(): return lax.all_to_all(array, axes, 0, 0, tiled=True)]
    pallas_call x7 -> x8, Pallas kernels: 13.9 us -> 9.89 us  [call(): pl.pallas_call(kernel, out_shape=out, scratch_shapes=list(scratch), compi...]
    unnamed x18, local copies, waits for them, and re-layouts: 0.8 us -> 2.32 us
  transfers between devices with their start and end apart: 3 -> 1, of which waited for: 2 -> 1; matrix products, arithmetic and copies ran while one was open for 0% -> 0% of each run, Pallas kernels for 1% -> 1%
where the time goes in v5:
time: 115 us; the launch traced here: 114 us
  blocking collectives  84.2 us (73%)
  starting transfers between devices  13.4 us (12%)
  Pallas kernels  9.89 us (9%)
  waiting for transfers between devices  3.66 us (3%)
  local copies, waits for them, and re-layouts  2.32 us (2%)
    all_to_all x4, blocking collectives, exchange(): return lax.all_to_all(array, axes, 0, 0, tiled=True)  80.4 us
    all_to_all x1, starting transfers between devices, exchange(): return lax.all_to_all(array, axes, 0, 0, tiled=True)  13.4 us
    pallas_call x8, Pallas kernels, call(): pl.pallas_call(kernel, out_shape=out, scratch_shapes=list(scratch), compi...  9.89 us
    all_gather x2, blocking collectives, shards(): pair = lax.all_gather(x, 'core', tiled=True)  3.79 us
    all_to_all x1, waiting for transfers between devices, exchange(): return lax.all_to_all(array, axes, 0, 0, tiled=True)  3.66 us
    unnamed x18, local copies, waits for them, and re-layouts  2.32 us
  transfers between devices with their start and end apart: 1, of which 1 were waited for; matrix products, arithmetic and copies ran while one was open for 0% of the time, Pallas kernels for 1%

profile of v5, /device:TPU:6, one launch (start us, length us, event | category | flops | bytes accessed | tf_op | source)
XLA Modules:
  0.0 114.2 jit_solution(15963764483557756403)
XLA Ops:
  0.6 2.6 %shard_map.113 = (f32[32,128]{1,0:T(8,128)}, f32[128,16]{1,0:T(8,128)}) custom-call(s32[8,128]{1,0:T(8,128)} %bitcast.31, s32[8,128]{1,0:T(8,128)} %bitcast.32), custom_call_target="tpu_custom_call" | custom-call | tf_op jit(solution)/shard_map/pallas_call | solution.py:185
  3.2 13.4 %all-to-all-start = ((f32[32,1,128]{2,1,0:T(1,128)}), f32[32,1,128]{2,1,0:T(1,128)S(1)}, u32[]{:S(2)}, u32[]{:S(2)}) async-start(f32[32,1,128]{2,1,0:T(1,128)} %bitcast.30), calls=%async_computation | async-start | bytes 32768 | tf_op jit(solution)/shard_map/all_to_all | solution.py:199
  16.7 0.0 copy-start.8
  16.7 0.6 copy-done.8
  17.3 0.0 copy-start.5
  17.3 0.8 copy-done.5
  18.2 0.0 copy-start.2
  18.2 0.7 shard_map.114.refs_0_.comb_ref
  18.9 0.1 copy-done.2
  19.0 1.9 %all-gather = bf16[1,256,256]{2,1,0:T(8,128)(2,1)S(1)} all-gather(bf16[1,128,256]{2,1,0:T(8,128)(2,1)S(1)} %copy-done.2), channel_id=2, replica_groups=mesh['tm'=8,'z'=8,'x'=4,'core'=2] {'core'}, dimensions={1}, use_global_device_ids=true | all-gather | bytes 196608 | tf_op jit(solution)/shard_map/all_gather | solution.py:222
  20.9 3.7 %all-to-all-done = f32[32,1,128]{2,1,0:T(1,128)S(1)} async-done(((f32[32,1,128]{2,1,0:T(1,128)}), f32[32,1,128]{2,1,0:T(1,128)S(1)}, u32[]{:S(2)}, u32[]{:S(2)}) %all-to-all-start) | async-done | bytes 16416 | tf_op jit(solution)/shard_map/all_to_all | solution.py:199
  24.5 0.6 shard_map.115
  25.2 0.0 copy-start.3
  25.2 26.0 %all_to_all.32 = bf16[32,40,256]{2,1,0:T(8,128)(2,1)S(1)} all-to-all(bf16[32,40,256]{2,1,0:T(8,128)(2,1)S(1)} %bitcast.22), channel_id=1, replica_groups=mesh['tm'=8,'z'=8,'x'=4,'core'=2] {'z','x'}, dimensions={0} | all-to-all | bytes 1310720 | tf_op jit(solution)/shard_map/all_to_all | solution.py:199
  51.2 0.0 copy-done.3
  51.2 0.4 shard_map.116.x_ref
  51.6 1.9 %all_gather.7.x_ref = bf16[256,256]{1,0:T(8,128)(2,1)S(1)} all-gather(bf16[128,256]{1,0:T(8,128)(2,1)S(1)} %shard_map.116.x_ref), channel_id=1, replica_groups=mesh['tm'=8,'z'=8,'x'=4,'core'=2] {'core'}, dimensions={0}, use_global_device_ids=true | all-gather | bytes 196608 | tf_op jit(solution)/shard_map/all_gather | solution.py:228
  53.5 0.3 shard_map.117
  53.8 0.0 copy-start.1
  53.9 0.0 copy-start.4
  53.9 0.0 copy-start.6
  53.9 25.5 %all_to_all.33 = bf16[32,40,256]{2,1,0:T(8,128)(2,1)S(1)} all-to-all(bf16[32,40,256]{2,1,0:T(8,128)(2,1)S(1)} %bitcast.19), channel_id=1, replica_groups=mesh['tm'=8,'z'=8,'x'=4,'core'=2] {'z','x'}, dimensions={0} | all-to-all | bytes 1310720 | tf_op jit(solution)/shard_map/all_to_all | solution.py:199
  79.3 0.0 copy-start.7
  79.3 0.0 copy-done.1
  79.4 0.0 copy-done.4
  79.4 0.0 copy-done.6
  79.4 0.7 copy-done.7
  80.0 0.0 copy-start
  80.0 0.7 shard_map.118
  80.7 16.0 %all_to_all.34.xc_ref = bf16[8,16,512]{2,1,0:T(8,128)(2,1)S(1)} all-to-all(bf16[8,16,512]{2,1,0:T(8,128)(2,1)S(1)} %bitcast.25), channel_id=1, replica_groups=mesh['tm'=8,'z'=8,'x'=4,'core'=2] {'tm'}, dimensions={0} | all-to-all | bytes 262144 | tf_op jit(solution)/shard_map/all_to_all | solution.py:199
  96.7 0.0 copy-done
  96.7 3.5 %shard_map.119 = bf16[8,16,1024]{2,1,0:T(8,128)(2,1)S(1)} custom-call(bf16[8,16,512]{2,1,0:T(8,128)(2,1)S(1)} %all_to_all.34.xc_ref, bf16[256,1024]{1,0:T(8,128)(2,1)S(1)} %copy-done.1, bf16[256,1024]{1,0:T(8,128)(2,1)S(1)} %copy-done, f32[1,1024]{1,0:T(1,128)S(1)} %bitcast.29), custom_call_target="tpu_custom_call" | custom-call | tf_op jit(solution)/shard_map/pallas_call | solution.py:185
  100.2 12.9 %all_to_all.35 = bf16[8,16,1024]{2,1,0:T(8,128)(2,1)S(1)} all-to-all(bf16[8,16,1024]{2,1,0:T(8,128)(2,1)S(1)} %shard_map.119), channel_id=1, replica_groups=mesh['tm'=8,'z'=8,'x'=4,'core'=2] {'tm'}, dimensions={0} | all-to-all | bytes 524288 | tf_op jit(solution)/shard_map/all_to_all | solution.py:199
  113.1 1.1 shard_map.120
Async XLA Ops:
  3.2 21.3 %all-to-all-start = ((f32[32,1,128]{2,1,0:T(1,128)}), f32[32,1,128]{2,1,0:T(1,128)S(1)}, u32[]{:S(2)}, u32[]{:S(2)}) async-start(f32[32,1,128]{2,1,0:T(1,128)} %bitcast.30), calls=%async_computation | async-start | bytes 32768 | tf_op jit(solution)/shard_map/all_to_all | solution.py:199
  16.7 0.7 copy-start.8
  17.3 0.8 copy-start.5
  18.2 0.8 copy-start.2
  25.2 26.0 %copy-start.3 = (bf16[256,256]{1,0:T(8,128)(2,1)S(1)}, bf16[256,256]{1,0:T(8,128)(2,1)}, u32[]{:S(2)}) copy-start(bf16[256,256]{1,0:T(8,128)(2,1)} %refs_4_.1) | copy-start | bytes 393220
  53.8 25.5 %copy-start.1 = (bf16[256,1024]{1,0:T(8,128)(2,1)S(1)}, bf16[256,1024]{1,0:T(8,128)(2,1)}, u32[]{:S(2)}) copy-start(bf16[256,1024]{1,0:T(8,128)(2,1)} %w_in_ref.3) | copy-start | bytes 1572868
  53.9 25.5 %copy-start.4 = (bf16[256,256]{1,0:T(8,128)(2,1)S(1)}, bf16[256,256]{1,0:T(8,128)(2,1)}, u32[]{:S(2)}) copy-start(bf16[256,256]{1,0:T(8,128)(2,1)} %weight_ref.1) | copy-start | bytes 393220
  53.9 25.5 %copy-start.6 = (bf16[1,128,256]{2,1,0:T(8,128)(2,1)S(1)}, bf16[1,128,256]{2,1,0:T(8,128)(2,1)}, u32[]{:S(2)}) copy-start(bf16[1,128,256]{2,1,0:T(8,128)(2,1)} %param.19) | copy-start | bytes 196612
  79.3 0.7 copy-start.7
  80.0 16.6 %copy-start = (bf16[256,1024]{1,0:T(8,128)(2,1)S(1)}, bf16[256,1024]{1,0:T(8,128)(2,1)}, u32[]{:S(2)}) copy-start(bf16[256,1024]{1,0:T(8,128)(2,1)} %w_rec_ref.3) | copy-start | bytes 1572868

commit v6 on v5

--- a/solution.py
+++ b/solution.py
@@ -35,32 +35,27 @@
     return copies
 
 
-def plan_kernel(owner_hbm, row_hbm, wanted_ref, place_ref, owner_ref, row_ref, sems):
+def plan_kernel(owner_hbm, row_hbm, wanted_ref, rank_ref, owner_ref, row_ref, sems):
     for copy in fetch(((owner_hbm, owner_ref), (row_hbm, row_ref)), sems):
         copy.wait()
     owner = owner_ref[...]
     value = ((owner % 2) * NODE + row_ref[...]).astype(F32)
     chip = owner // 2
     upper = jnp.where(iota((LANES, LANES), 0) < iota((LANES, LANES), 1), 1.0, 0.0).astype(BF16)
+    named = [
+        jnp.where(iota((CHIPS, LANES), 0) == chip[i : i + 1, :], 1.0, 0.0) for i in range(KNB)
+    ]
+    before = matmul(jnp.concatenate(named, 0).astype(BF16), upper)
     base = jnp.zeros((CHIPS, 1), F32)
     wanted = jnp.zeros((CHIPS, LANES), F32)
-    place = jnp.zeros((NODE, 2 * KNB), F32)
-    lane = iota((1, LANES), 1)
-    sub = iota((2 * KNB, LANES), 0)
     for i in range(KNB):
-        chip_i = chip[i : i + 1, :]
-        onehot = jnp.where(iota((CHIPS, LANES), 0) == chip_i, 1.0, 0.0)
-        before = matmul(onehot.astype(BF16), upper) + base
-        base = base + jnp.sum(onehot, 1, keepdims=True)
-        rank = jnp.sum(onehot * before, 0, keepdims=True)
+        earlier = before[i * CHIPS : (i + 1) * CHIPS] + base
+        base = base + jnp.sum(named[i], 1, keepdims=True)
+        rank = jnp.sum(named[i] * earlier, 0, keepdims=True)
+        rank_ref[i : i + 1, :] = rank
         ranks = jnp.where(iota((LANES, LANES), 0).astype(F32) == rank, 1.0, 0.0).astype(BF16)
-        wanted = wanted + matmul((onehot * value[i : i + 1, :]).astype(BF16), ranks, NT)
-        group = jnp.where(iota((NODE, LANES), 0) == i * (LANES // KNB) + lane // KNB, 1.0, 0.0)
-        coded = jnp.where(sub < KNB, chip_i.astype(F32), rank)
-        coded = jnp.where(sub % KNB == lane % KNB, coded, 0.0)
-        place = place + matmul(group.astype(BF16), coded.astype(BF16), NT)
+        wanted = wanted + matmul((named[i] * value[i : i + 1, :]).astype(BF16), ranks, NT)
     wanted_ref[...] = wanted
-    place_ref[...] = place
 
 
 def column(row):
@@ -68,9 +63,18 @@
     return jnp.sum(jnp.where(eye, row, 0.0), 1, keepdims=True)
 
 
-def comb_kernel(place_ref, cnt_ref, comb_ref):
+def comb_kernel(rank_ref, owner_ref, cnt_ref, comb_ref):
     count = column(cnt_ref[...].astype(F32))
-    place = place_ref[:, :KNB] * CAP + place_ref[:, KNB:]
+    lane = iota((1, LANES), 1)
+    sub = iota((2 * KNB, LANES), 0)
+    chip = (owner_ref[...] // 2).astype(F32)
+    place = jnp.zeros((NODE, 2 * KNB), F32)
+    for i in range(KNB):
+        group = jnp.where(iota((NODE, LANES), 0) == i * (LANES // KNB) + lane // KNB, 1.0, 0.0)
+        coded = jnp.where(sub < KNB, chip[i : i + 1, :], rank_ref[i : i + 1, :])
+        coded = jnp.where(sub % KNB == lane % KNB, coded, 0.0)
+        place = place + matmul(group.astype(BF16), coded.astype(BF16), NT)
+    place = place[:, :KNB] * CAP + place[:, KNB:]
     place = jnp.where(iota((NODE, KNB), 1).astype(F32) < count, place, -1.0)
     spot = iota((NODE, SLOTS), 1).astype(F32)
     comb = jnp.zeros((NODE, SLOTS), F32)
@@ -106,13 +110,10 @@
     refs[-1][...] = convolved(*refs[:-1])
 
 
-def second_kernel(
-    comb_ref, arrived_ref, x_ref, cnt_ref, weight_ref, cot_ref, w_in_ref, bias_ref, out_ref, z_ref
-):
+def second_kernel(comb_ref, arrived_ref, x_ref, cnt_ref, weight_ref, cot_ref, out_ref):
     x = convolved(comb_ref, arrived_ref, x_ref, cnt_ref, weight_ref)
     out_ref[:, :H] = x
     out_ref[:, H:] = cot_ref[...]
-    z_ref[...] = (matmul(x, w_in_ref[...]) + bias_ref[...]).astype(BF16)
 
 
 def gated(gates, c):
@@ -167,11 +168,12 @@
             dc = dc * saved_ref[t, 0]
 
 
-def last_kernel(back_ref, z_ref, w_rec_ref, hidden_ref, grads_ref):
+def last_kernel(back_ref, x_ref, w_in_ref, w_rec_ref, bias_ref, hidden_ref, grads_ref):
     c = back_ref[:, H : 2 * H].astype(F32)
     dh = back_ref[:, 2 * H : 3 * H].astype(F32)
     dc = back_ref[:, 3 * H :].astype(F32)
-    gates = z_ref[...].astype(F32) + matmul(back_ref[:, :H], w_rec_ref[...])
+    z = (matmul(x_ref[:, :H], w_in_ref[...]) + bias_ref[...]).astype(BF16)
+    gates = z.astype(F32) + matmul(back_ref[:, :H], w_rec_ref[...])
     i, f, g, o, c_new, tc = gated(gates, c)
     hidden_ref[...] = (o * tc).astype(BF16)
     grads_ref[:, :H] = (dc * g * i * (1.0 - i)).astype(BF16)
@@ -205,10 +207,11 @@
     chips = ("z", "x")
     bias = gate_bias.reshape(1, 4 * H)
     x = features[0]
-    wanted, place = call(
+    owner = nbr_owner.reshape(KNB, LANES)
+    wanted, rank = call(
         plan_kernel,
-        (shaped((CHIPS, LANES), F32), shaped((NODE, 2 * KNB), F32)),
-        nbr_owner.reshape(KNB, LANES),
+        (shaped((CHIPS, LANES), F32), shaped((KNB, LANES), F32)),
+        owner,
         nbr_row.reshape(KNB, LANES),
         in_specs=[pl.BlockSpec(memory_space=pltpu.HBM)] * 2,
         scratch=(
@@ -220,27 +223,26 @@
     )
     asked = exchange(wanted, chips)
     pair = lax.all_gather(x, "core", tiled=True)
-    comb = call(comb_kernel, shaped((NODE, SLOTS)), place, counts)
-    asked, pair, comb = lax.optimization_barrier((asked, pair, comb))
+    pair, rank = lax.optimization_barrier((pair, rank))
+    comb = call(comb_kernel, shaped((NODE, SLOTS)), rank, owner, counts)
+    asked, comb = lax.optimization_barrier((asked, comb))
     pick, outgoing = call(pick_kernel, (shaped((SLOTS, H)), shaped((SLOTS, H))), asked, pair)
     arrived = exchange(outgoing.reshape(CHIPS, CAP, H), chips).reshape(SLOTS, H)
     x = call(first_kernel, shaped((NODE, H)), comb, arrived, x, counts, weight_one)
     pair = lax.all_gather(x, "core", tiled=True)
     outgoing = call(again_kernel, shaped((SLOTS, H)), pick, pair)
     arrived = exchange(outgoing.reshape(CHIPS, CAP, H), chips).reshape(SLOTS, H)
-    both, z = call(
+    mine = call(
         second_kernel,
-        (shaped((NODE, 2 * H)), shaped((NODE, 4 * H))),
+        shaped((NODE, 2 * H)),
         comb,
         arrived,
         x,
         counts,
         weight_two,
         cotangent[0],
-        w_in,
-        bias,
-    )
-    both = exchange(both.reshape(SNAPS, PART, 2 * H), "tm")
+    )
+    both = exchange(mine.reshape(SNAPS, PART, 2 * H), "tm")
     back = call(
         chain_kernel,
         shaped((SNAPS, PART, 4 * H)),
@@ -251,7 +253,15 @@
         scratch=(pltpu.VMEM((NODE, 4 * H), F32), pltpu.VMEM((SNAPS, 6, PART, H), F32)),
     )
     back = exchange(back, "tm").reshape(NODE, 4 * H)
-    hidden, grads = call(last_kernel, (shaped((NODE, H)), shaped((NODE, 4 * H))), back, z, w_rec)
+    hidden, grads = call(
+        last_kernel,
+        (shaped((NODE, H)), shaped((NODE, 4 * H))),
+        back,
+        mine,
+        w_in,
+        w_rec,
+        bias,
+    )
     return hidden[None], grads[None]
 
 

time: 115 us -> 112 us (0.974)
  local copies, waits for them, and re-layouts: 2.32 us -> 0.7 us
    unnamed x18 -> x20, local copies, waits for them, and re-layouts: 2.32 us -> 0.7 us
where the time goes in v6:
time: 112 us
  blocking collectives  83.8 us (75%)
  starting transfers between devices  13.4 us (12%)
  Pallas kernels  9.06 us (8%)
  waiting for transfers between devices  4.2 us (4%)
    all_to_all x4, blocking collectives, exchange(): return lax.all_to_all(array, axes, 0, 0, tiled=True)  79.8 us
    all_to_all x1, starting transfers between devices, exchange(): return lax.all_to_all(array, axes, 0, 0, tiled=True)  13.4 us
    pallas_call x8, Pallas kernels, call(): pl.pallas_call(kernel, out_shape=out, scratch_shapes=list(scratch), compi...  9.06 us
    all_to_all x1, waiting for transfers between devices, exchange(): return lax.all_to_all(array, axes, 0, 0, tiled=True)  4.2 us
    all_gather x2, blocking collectives, shards(): pair = lax.all_gather(x, 'core', tiled=True)  4.01 us
  transfers between devices with their start and end apart: 1, of which 1 were waited for; matrix products, arithmetic and copies ran while one was open for 0% of the time, Pallas kernels for 1%

profile of v6, /device:TPU:6, one launch (start us, length us, event | category | flops | bytes accessed | tf_op | source)
XLA Modules:
  0.0 112.0 jit_solution(10936858479683798144)
XLA Ops:
  0.6 1.8 %shard_map.113 = (f32[32,128]{1,0:T(8,128)}, f32[8,128]{1,0:T(8,128)}) custom-call(s32[8,128]{1,0:T(8,128)} %bitcast.30, s32[8,128]{1,0:T(8,128)} %bitcast.33), custom_call_target="tpu_custom_call" | custom-call | tf_op jit(solution)/shard_map/pallas_call | solution.py:187
  2.4 13.4 %all-to-all-start = ((f32[32,1,128]{2,1,0:T(1,128)}), f32[32,1,128]{2,1,0:T(1,128)S(1)}, u32[]{:S(2)}, u32[]{:S(2)}) async-start(f32[32,1,128]{2,1,0:T(1,128)} %bitcast.32), calls=%async_computation | async-start | bytes 32768 | tf_op jit(solution)/shard_map/all_to_all | solution.py:201
  15.8 0.0 copy-start.7
  15.8 0.0 copy-start.9
  15.8 2.1 %all-gather = bf16[1,256,256]{2,1,0:T(8,128)(2,1)S(1)} all-gather(bf16[1,128,256]{2,1,0:T(8,128)(2,1)} %param.10), channel_id=2, replica_groups=mesh['tm'=8,'z'=8,'x'=4,'core'=2] {'core'}, dimensions={1}, use_global_device_ids=true | all-gather | bytes 196608 | tf_op jit(solution)/shard_map/all_gather | solution.py:225
  18.0 0.0 copy-start.8
  18.0 0.0 copy-done.7
  18.0 0.0 copy-done.9
  18.0 0.6 copy-done.8
  18.6 0.9 shard_map.114.refs_0_.comb_ref
  19.5 4.2 %all-to-all-done = f32[32,1,128]{2,1,0:T(1,128)S(1)} async-done(((f32[32,1,128]{2,1,0:T(1,128)}), f32[32,1,128]{2,1,0:T(1,128)S(1)}, u32[]{:S(2)}, u32[]{:S(2)}) %all-to-all-start) | async-done | bytes 16416 | tf_op jit(solution)/shard_map/all_to_all | solution.py:201
  23.7 0.6 shard_map.115
  24.3 0.0 copy-start.2
  24.3 0.0 copy-start.3
  24.4 25.5 %all_to_all.32 = bf16[32,40,256]{2,1,0:T(8,128)(2,1)S(1)} all-to-all(bf16[32,40,256]{2,1,0:T(8,128)(2,1)S(1)} %bitcast.23), channel_id=1, replica_groups=mesh['tm'=8,'z'=8,'x'=4,'core'=2] {'z','x'}, dimensions={0} | all-to-all | bytes 1310720 | tf_op jit(solution)/shard_map/all_to_all | solution.py:201
  49.8 0.0 copy-done.2
  49.8 0.0 copy-done.3
  49.8 0.4 shard_map.116.x_ref
  50.2 1.9 %all_gather.7.x_ref = bf16[256,256]{1,0:T(8,128)(2,1)S(1)} all-gather(bf16[128,256]{1,0:T(8,128)(2,1)S(1)} %shard_map.116.x_ref), channel_id=1, replica_groups=mesh['tm'=8,'z'=8,'x'=4,'core'=2] {'core'}, dimensions={0}, use_global_device_ids=true | all-gather | bytes 196608 | tf_op jit(solution)/shard_map/all_gather | solution.py:232
  52.1 0.3 shard_map.117
  52.5 0.0 copy-start.4
  52.5 0.0 copy-start.5
  52.5 25.4 %all_to_all.33 = bf16[32,40,256]{2,1,0:T(8,128)(2,1)S(1)} all-to-all(bf16[32,40,256]{2,1,0:T(8,128)(2,1)S(1)} %bitcast.19), channel_id=1, replica_groups=mesh['tm'=8,'z'=8,'x'=4,'core'=2] {'z','x'}, dimensions={0} | all-to-all | bytes 1310720 | tf_op jit(solution)/shard_map/all_to_all | solution.py:201
  78.0 0.0 copy-done.4
  78.0 0.0 copy-done.5
  78.0 0.0 copy-start
  78.0 0.0 copy-start.1
  78.0 0.4 shard_map.118.x_ref
  78.4 0.0 copy-start.6
  78.4 16.0 %all_to_all.34.xc_ref = bf16[8,16,512]{2,1,0:T(8,128)(2,1)S(1)} all-to-all(bf16[8,16,512]{2,1,0:T(8,128)(2,1)S(1)} %bitcast.21), channel_id=1, replica_groups=mesh['tm'=8,'z'=8,'x'=4,'core'=2] {'tm'}, dimensions={0} | all-to-all | bytes 262144 | tf_op jit(solution)/shard_map/all_to_all | solution.py:201
  94.4 0.0 copy-done
  94.4 0.0 copy-done.1
  94.4 0.0 copy-done.6
  94.4 3.5 %shard_map.119 = bf16[8,16,1024]{2,1,0:T(8,128)(2,1)S(1)} custom-call(bf16[8,16,512]{2,1,0:T(8,128)(2,1)S(1)} %all_to_all.34.xc_ref, bf16[256,1024]{1,0:T(8,128)(2,1)S(1)} %copy-done, bf16[256,1024]{1,0:T(8,128)(2,1)S(1)} %copy-done.1, f32[1,1024]{1,0:T(1,128)S(1)} %bitcast.28), custom_call_target="tpu_custom_call" | custom-call | tf_op jit(solution)/shard_map/pallas_call | solution.py:187
  97.9 12.9 %all_to_all.35 = bf16[8,16,1024]{2,1,0:T(8,128)(2,1)S(1)} all-to-all(bf16[8,16,1024]{2,1,0:T(8,128)(2,1)S(1)} %shard_map.119), channel_id=1, replica_groups=mesh['tm'=8,'z'=8,'x'=4,'core'=2] {'tm'}, dimensions={0} | all-to-all | bytes 524288 | tf_op jit(solution)/shard_map/all_to_all | solution.py:201
  110.8 1.2 %shard_map.120 = (bf16[128,256]{1,0:T(8,128)(2,1)}, bf16[128,1024]{1,0:T(8,128)(2,1)}) custom-call(bf16[128,1024]{1,0:T(8,128)(2,1)S(1)} %bitcast.22, bf16[128,512]{1,0:T(8,128)(2,1)S(1)} %shard_map.118.x_ref, bf16[256,1024]{1,0:T(8,128)(2,1)S(1)} %copy-done, bf16[256,1024]{1,0:T(8,128)(2,1)S(1)} %copy-done.1, f32[1,1024]{1,0:T(1,128)S(1)} %bitcast.29), custom_call_target="tpu_custom_call" | custom-call | tf_op jit(solution)/shard_map/pallas_call | solution.py:187
Async XLA Ops:
  2.4 21.3 %all-to-all-start = ((f32[32,1,128]{2,1,0:T(1,128)}), f32[32,1,128]{2,1,0:T(1,128)S(1)}, u32[]{:S(2)}, u32[]{:S(2)}) async-start(f32[32,1,128]{2,1,0:T(1,128)} %bitcast.32), calls=%async_computation | async-start | bytes 32768 | tf_op jit(solution)/shard_map/all_to_all | solution.py:201
  15.8 2.1 %copy-start.7 = (s32[1,1024,1]{1,2,0:T(1,128)S(1)}, s32[1,1024,1]{1,2,0:T(1,128)}, u32[]{:S(2)}) copy-start(s32[1,1024,1]{1,2,0:T(1,128)} %param.11) | copy-start | bytes 12292
  15.8 2.1 %copy-start.9 = (f32[8,128]{1,0:T(8,128)S(1)}, f32[8,128]{1,0:T(8,128)}, u32[]{:S(2)}) copy-start(f32[8,128]{1,0:T(8,128)} %get-tuple-element.14.rank_ref) | copy-start | bytes 12292
  18.0 0.7 copy-start.8
  24.3 25.5 %copy-start.2 = (bf16[1,128,256]{2,1,0:T(8,128)(2,1)S(1)}, bf16[1,128,256]{2,1,0:T(8,128)(2,1)}, u32[]{:S(2)}) copy-start(bf16[1,128,256]{2,1,0:T(8,128)(2,1)} %param.10) | copy-start | bytes 196612
  24.3 25.5 %copy-start.3 = (bf16[256,256]{1,0:T(8,128)(2,1)S(1)}, bf16[256,256]{1,0:T(8,128)(2,1)}, u32[]{:S(2)}) copy-start(bf16[256,256]{1,0:T(8,128)(2,1)} %refs_4_.1) | copy-start | bytes 393220
  52.5 25.5 %copy-start.4 = (bf16[256,256]{1,0:T(8,128)(2,1)S(1)}, bf16[256,256]{1,0:T(8,128)(2,1)}, u32[]{:S(2)}) copy-start(bf16[256,256]{1,0:T(8,128)(2,1)} %weight_ref.1) | copy-start | bytes 393220
  52.5 25.5 %copy-start.5 = (bf16[1,128,256]{2,1,0:T(8,128)(2,1)S(1)}, bf16[1,128,256]{2,1,0:T(8,128)(2,1)}, u32[]{:S(2)}) copy-start(bf16[1,128,256]{2,1,0:T(8,128)(2,1)} %param.19) | copy-start | bytes 196612
  78.0 16.4 %copy-start = (bf16[256,1024]{1,0:T(8,128)(2,1)S(1)}, bf16[256,1024]{1,0:T(8,128)(2,1)}, u32[]{:S(2)}) copy-start(bf16[256,1024]{1,0:T(8,128)(2,1)} %w_in_ref.3) | copy-start | bytes 1572868
  78.0 16.4 %copy-start.1 = (bf16[256,1024]{1,0:T(8,128)(2,1)S(1)}, bf16[256,1024]{1,0:T(8,128)(2,1)}, u32[]{:S(2)}) copy-start(bf16[256,1024]{1,0:T(8,128)(2,1)} %w_rec_ref.3) | copy-start | bytes 1572868
  78.4 16.0 %copy-start.6 = (f32[1024]{0:T(1024)S(1)}, f32[1024]{0:T(1024)}, u32[]{:S(2)}) copy-start(f32[1024]{0:T(1024)} %param.18) | copy-start | bytes 12292

commit v7 on v6

--- a/solution.py
+++ b/solution.py
@@ -14,6 +14,7 @@
 CAP = 40
 SLOTS = CHIPS * CAP
 PART = NODE // SNAPS
+LAST_ROWS = 32
 LANES = 128
 BF16 = jnp.bfloat16
 F32 = jnp.float32
@@ -125,7 +126,11 @@
     return i, f, g, o, c_new, jnp.tanh(c_new)
 
 
-def chain_kernel(xc_ref, w_in_ref, w_rec_ref, bias_ref, out_ref, z_ref, saved_ref):
+def turn_kernel(w_ref, out_ref):
+    out_ref[...] = w_ref[...].T
+
+
+def chain_kernel(xc_ref, w_in_ref, w_rec_ref, turned_ref, bias_ref, out_ref, z_ref, saved_ref):
     x = xc_ref[:, :, :H].reshape(NODE, H)
     z = matmul(x, w_in_ref[...]) + bias_ref[...]
     z_ref[...] = z.astype(BF16).astype(F32)
@@ -164,26 +169,47 @@
                 ],
                 1,
             ).astype(BF16)
-            dh = matmul(grad, w_rec_ref[...], NT)
+            dh = matmul(grad, turned_ref[...])
             dc = dc * saved_ref[t, 0]
 
 
-def last_kernel(back_ref, x_ref, w_in_ref, w_rec_ref, bias_ref, hidden_ref, grads_ref):
-    c = back_ref[:, H : 2 * H].astype(F32)
-    dh = back_ref[:, 2 * H : 3 * H].astype(F32)
-    dc = back_ref[:, 3 * H :].astype(F32)
+def last_kernel(
+    back_ref,
+    x_ref,
+    w_in_ref,
+    w_rec_ref,
+    bias_ref,
+    hidden_hbm,
+    grads_hbm,
+    gates_ref,
+    hidden_ref,
+    grads_ref,
+    sems,
+):
     z = (matmul(x_ref[:, :H], w_in_ref[...]) + bias_ref[...]).astype(BF16)
-    gates = z.astype(F32) + matmul(back_ref[:, :H], w_rec_ref[...])
-    i, f, g, o, c_new, tc = gated(gates, c)
-    hidden_ref[...] = (o * tc).astype(BF16)
-    grads_ref[:, :H] = (dc * g * i * (1.0 - i)).astype(BF16)
-    grads_ref[:, H : 2 * H] = (dc * c * f * (1.0 - f)).astype(BF16)
-    grads_ref[:, 2 * H : 3 * H] = (dc * i * (1.0 - g * g)).astype(BF16)
-    grads_ref[:, 3 * H :] = (dh * tc * o * (1.0 - o)).astype(BF16)
-
-
-def call(kernel, out, *args, scratch=(), in_specs=None, limit=16):
-    more = {} if in_specs is None else {"in_specs": in_specs}
+    gates_ref[...] = z.astype(F32) + matmul(back_ref[:, :H], w_rec_ref[...])
+    copies = []
+    for part in range(NODE // LAST_ROWS):
+        rows = slice(part * LAST_ROWS, (part + 1) * LAST_ROWS)
+        c = back_ref[rows, H : 2 * H].astype(F32)
+        dh = back_ref[rows, 2 * H : 3 * H].astype(F32)
+        dc = back_ref[rows, 3 * H :].astype(F32)
+        i, f, g, o, c_new, tc = gated(gates_ref[rows, :], c)
+        hidden_ref[rows, :] = (o * tc).astype(BF16)
+        grads_ref[rows, :H] = (dc * g * i * (1.0 - i)).astype(BF16)
+        grads_ref[rows, H : 2 * H] = (dc * c * f * (1.0 - f)).astype(BF16)
+        grads_ref[rows, 2 * H : 3 * H] = (dc * i * (1.0 - g * g)).astype(BF16)
+        grads_ref[rows, 3 * H :] = (dh * tc * o * (1.0 - o)).astype(BF16)
+        pairs = (
+            (hidden_ref.at[rows, :], hidden_hbm.at[rows, :]),
+            (grads_ref.at[rows, :], grads_hbm.at[rows, :]),
+        )
+        copies += fetch(pairs, sems.at[part])
+    for copy in copies:
+        copy.wait()
+
+
+def call(kernel, out, *args, scratch=(), limit=16, **more):
     return pl.pallas_call(
         kernel,
         out_shape=out,
@@ -223,9 +249,10 @@
     )
     asked = exchange(wanted, chips)
     pair = lax.all_gather(x, "core", tiled=True)
-    pair, rank = lax.optimization_barrier((pair, rank))
+    pair, rank, w_rec = lax.optimization_barrier((pair, rank, w_rec))
+    turned = call(turn_kernel, shaped((4 * H, H)), w_rec)
     comb = call(comb_kernel, shaped((NODE, SLOTS)), rank, owner, counts)
-    asked, comb = lax.optimization_barrier((asked, comb))
+    asked, comb, turned = lax.optimization_barrier((asked, comb, turned))
     pick, outgoing = call(pick_kernel, (shaped((SLOTS, H)), shaped((SLOTS, H))), asked, pair)
     arrived = exchange(outgoing.reshape(CHIPS, CAP, H), chips).reshape(SLOTS, H)
     x = call(first_kernel, shaped((NODE, H)), comb, arrived, x, counts, weight_one)
@@ -249,6 +276,7 @@
         both,
         w_in,
         w_rec,
+        turned,
         bias,
         scratch=(pltpu.VMEM((NODE, 4 * H), F32), pltpu.VMEM((SNAPS, 6, PART, H), F32)),
     )
@@ -261,6 +289,13 @@
         w_in,
         w_rec,
         bias,
+        out_specs=[pl.BlockSpec(memory_space=pltpu.HBM)] * 2,
+        scratch=(
+            pltpu.VMEM((NODE, 4 * H), F32),
+            pltpu.VMEM((NODE, H), BF16),
+            pltpu.VMEM((NODE, 4 * H), BF16),
+            pltpu.SemaphoreType.DMA((NODE // LAST_ROWS, 2)),
+        ),
     )
     return hidden[None], grads[None]
 

time: 112 us -> 113 us (level)
    pallas_call x8 -> x9, Pallas kernels: 9.06 us -> 8.73 us  [call(): pl.pallas_call(kernel, out_shape=out, scratch_shapes=list(scratch), compi...]
where the time goes in v7:
time: 113 us
  blocking collectives  84.9 us (75%)
  starting transfers between devices  13.4 us (12%)
  Pallas kernels  8.73 us (8%)
  waiting for transfers between devices  3.12 us (3%)
  local copies, waits for them, and re-layouts  1.6 us (1%)
    all_to_all x4, blocking collectives, exchange(): return lax.all_to_all(array, axes, 0, 0, tiled=True)  80.9 us
    all_to_all x1, starting transfers between devices, exchange(): return lax.all_to_all(array, axes, 0, 0, tiled=True)  13.4 us
    pallas_call x9, Pallas kernels, call(): pl.pallas_call(kernel, out_shape=out, scratch_shapes=list(scratch), compi...  8.73 us
    all_gather x2, blocking collectives, shards(): pair = lax.all_gather(x, 'core', tiled=True)  4.01 us
    all_to_all x1, waiting for transfers between devices, exchange(): return lax.all_to_all(array, axes, 0, 0, tiled=True)  3.12 us
  transfers between devices with their start and end apart: 1, of which 1 were waited for; matrix products, arithmetic and copies ran while one was open for 0% of the time, Pallas kernels for 1%

profile of v7, /device:TPU:6, one launch (start us, length us, event | category | flops | bytes accessed | tf_op | source)
XLA Modules:
  0.0 112.5 jit_solution(9975950170488360256)
XLA Ops:
  0.6 1.8 %shard_map.113 = (f32[32,128]{1,0:T(8,128)}, f32[8,128]{1,0:T(8,128)}) custom-call(s32[8,128]{1,0:T(8,128)} %bitcast.30, s32[8,128]{1,0:T(8,128)} %bitcast.33), custom_call_target="tpu_custom_call" | custom-call | tf_op jit(solution)/shard_map/pallas_call | solution.py:213
  2.4 13.4 %all-to-all-start = ((f32[32,1,128]{2,1,0:T(1,128)}), f32[32,1,128]{2,1,0:T(1,128)S(1)}, u32[]{:S(2)}, u32[]{:S(2)}) async-start(f32[32,1,128]{2,1,0:T(1,128)} %bitcast.32), calls=%async_computation | async-start | bytes 32768 | tf_op jit(solution)/shard_map/all_to_all | solution.py:227
  15.8 2.1 %all-gather = bf16[1,256,256]{2,1,0:T(8,128)(2,1)S(1)} all-gather(bf16[1,128,256]{2,1,0:T(8,128)(2,1)} %param.10), channel_id=2, replica_groups=mesh['tm'=8,'z'=8,'x'=4,'core'=2] {'core'}, dimensions={1}, use_global_device_ids=true | all-gather | bytes 196608 | tf_op jit(solution)/shard_map/all_gather | solution.py:251
  17.9 0.0 copy-start
  17.9 1.0 copy-done
  19.0 0.0 copy-start.8
  19.0 0.0 copy-start.9
  19.0 0.0 copy-start.10
  19.0 0.2 shard_map.115.turned_ref
  19.2 0.5 copy-done.8
  19.7 0.0 copy-done.9
  19.7 0.0 copy-done.10
  19.7 0.9 shard_map.114.refs_0_.comb_ref
  20.6 3.1 %all-to-all-done = f32[32,1,128]{2,1,0:T(1,128)S(1)} async-done(((f32[32,1,128]{2,1,0:T(1,128)}), f32[32,1,128]{2,1,0:T(1,128)S(1)}, u32[]{:S(2)}, u32[]{:S(2)}) %all-to-all-start) | async-done | bytes 16416 | tf_op jit(solution)/shard_map/all_to_all | solution.py:227
  23.7 0.6 shard_map.116
  24.3 0.0 copy-start.3
  24.3 0.0 copy-start.4
  24.4 26.6 %all_to_all.32 = bf16[32,40,256]{2,1,0:T(8,128)(2,1)S(1)} all-to-all(bf16[32,40,256]{2,1,0:T(8,128)(2,1)S(1)} %bitcast.23), channel_id=1, replica_groups=mesh['tm'=8,'z'=8,'x'=4,'core'=2] {'z','x'}, dimensions={0} | all-to-all | bytes 1310720 | tf_op jit(solution)/shard_map/all_to_all | solution.py:227
  50.9 0.0 copy-done.3
  50.9 0.0 copy-done.4
  50.9 0.4 shard_map.117.x_ref
  51.3 1.9 %all_gather.7.x_ref = bf16[256,256]{1,0:T(8,128)(2,1)S(1)} all-gather(bf16[128,256]{1,0:T(8,128)(2,1)S(1)} %shard_map.117.x_ref), channel_id=1, replica_groups=mesh['tm'=8,'z'=8,'x'=4,'core'=2] {'core'}, dimensions={0}, use_global_device_ids=true | all-gather | bytes 196608 | tf_op jit(solution)/shard_map/all_gather | solution.py:259
  53.2 0.3 shard_map.118
  53.6 0.0 copy-start.5
  53.6 0.0 copy-start.6
  53.6 25.5 %all_to_all.33 = bf16[32,40,256]{2,1,0:T(8,128)(2,1)S(1)} all-to-all(bf16[32,40,256]{2,1,0:T(8,128)(2,1)S(1)} %bitcast.19), channel_id=1, replica_groups=mesh['tm'=8,'z'=8,'x'=4,'core'=2] {'z','x'}, dimensions={0} | all-to-all | bytes 1310720 | tf_op jit(solution)/shard_map/all_to_all | solution.py:227
  79.0 0.0 copy-done.5
  79.0 0.0 copy-done.6
  79.0 0.0 copy-start.1
  79.0 0.0 copy-start.2
  79.0 0.4 shard_map.119.x_ref
  79.4 0.0 copy-start.7
  79.5 16.0 %all_to_all.34.xc_ref = bf16[8,16,512]{2,1,0:T(8,128)(2,1)S(1)} all-to-all(bf16[8,16,512]{2,1,0:T(8,128)(2,1)S(1)} %bitcast.21), channel_id=1, replica_groups=mesh['tm'=8,'z'=8,'x'=4,'core'=2] {'tm'}, dimensions={0} | all-to-all | bytes 262144 | tf_op jit(solution)/shard_map/all_to_all | solution.py:227
  95.5 0.0 copy-done.1
  95.5 0.0 copy-done.2
  95.5 0.0 copy-done.7
  95.5 3.0 %shard_map.120 = bf16[8,16,1024]{2,1,0:T(8,128)(2,1)S(1)} custom-call(bf16[8,16,512]{2,1,0:T(8,128)(2,1)S(1)} %all_to_all.34.xc_ref, bf16[256,1024]{1,0:T(8,128)(2,1)S(1)} %copy-done.2, bf16[256,1024]{1,0:T(8,128)(2,1)S(1)} %copy-done.1, bf16[1024,256]{1,0:T(8,128)(2,1)S(1)} %shard_map.115.turned_ref, f32[1,1024]{1,0:T(1,128)S(1)} %bitcast.28), custom_call_target="tpu_custom_call" | custom-call | tf_op jit(solution)/shard_map/pallas_call | solution.py:213
  98.4 12.9 %all_to_all.35 = bf16[8,16,1024]{2,1,0:T(8,128)(2,1)S(1)} all-to-all(bf16[8,16,1024]{2,1,0:T(8,128)(2,1)S(1)} %shard_map.120), channel_id=1, replica_groups=mesh['tm'=8,'z'=8,'x'=4,'core'=2] {'tm'}, dimensions={0} | all-to-all | bytes 524288 | tf_op jit(solution)/shard_map/all_to_all | solution.py:227
  111.3 1.2 %shard_map.121 = (bf16[128,256]{1,0:T(8,128)(2,1)}, bf16[128,1024]{1,0:T(8,128)(2,1)}) custom-call(bf16[128,1024]{1,0:T(8,128)(2,1)S(1)} %bitcast.22, bf16[128,512]{1,0:T(8,128)(2,1)S(1)} %shard_map.119.x_ref, bf16[256,1024]{1,0:T(8,128)(2,1)S(1)} %copy-done.2, bf16[256,1024]{1,0:T(8,128)(2,1)S(1)} %copy-done.1, f32[1,1024]{1,0:T(1,128)S(1)} %bitcast.29), custom_call_target="tpu_custom_call" | custom-call | tf_op jit(solution)/shard_map/pallas_call | solution.py:213
Async XLA Ops:
  2.4 21.3 %all-to-all-start = ((f32[32,1,128]{2,1,0:T(1,128)}), f32[32,1,128]{2,1,0:T(1,128)S(1)}, u32[]{:S(2)}, u32[]{:S(2)}) async-start(f32[32,1,128]{2,1,0:T(1,128)} %bitcast.32), calls=%async_computation | async-start | bytes 32768 | tf_op jit(solution)/shard_map/all_to_all | solution.py:227
  17.9 1.0 copy-start
  19.0 0.7 copy-start.8
  19.0 0.7 copy-start.9
  19.0 0.7 copy-start.10
  24.3 26.6 %copy-start.3 = (bf16[1,128,256]{2,1,0:T(8,128)(2,1)S(1)}, bf16[1,128,256]{2,1,0:T(8,128)(2,1)}, u32[]{:S(2)}) copy-start(bf16[1,128,256]{2,1,0:T(8,128)(2,1)} %param.10) | copy-start | bytes 196612
  24.3 26.6 %copy-start.4 = (bf16[256,256]{1,0:T(8,128)(2,1)S(1)}, bf16[256,256]{1,0:T(8,128)(2,1)}, u32[]{:S(2)}) copy-start(bf16[256,256]{1,0:T(8,128)(2,1)} %refs_4_.1) | copy-start | bytes 393220
  53.6 25.5 %copy-start.5 = (bf16[256,256]{1,0:T(8,128)(2,1)S(1)}, bf16[256,256]{1,0:T(8,128)(2,1)}, u32[]{:S(2)}) copy-start(bf16[256,256]{1,0:T(8,128)(2,1)} %weight_ref.1) | copy-start | bytes 393220
  53.6 25.5 %copy-start.6 = (bf16[1,128,256]{2,1,0:T(8,128)(2,1)S(1)}, bf16[1,128,256]{2,1,0:T(8,128)(2,1)}, u32[]{:S(2)}) copy-start(bf16[1,128,256]{2,1,0:T(8,128)(2,1)} %param.19) | copy-start | bytes 196612
  79.0 16.4 %copy-start.1 = (bf16[256,1024]{1,0:T(8,128)(2,1)S(1)}, bf16[256,1024]{1,0:T(8,128)(2,1)}, u32[]{:S(2)}) copy-start(bf16[256,1024]{1,0:T(8,128)(2,1)} %w_rec_ref.1) | copy-start | bytes 1572868
  79.0 16.4 %copy-start.2 = (bf16[256,1024]{1,0:T(8,128)(2,1)S(1)}, bf16[256,1024]{1,0:T(8,128)(2,1)}, u32[]{:S(2)}) copy-start(bf16[256,1024]{1,0:T(8,128)(2,1)} %w_in_ref.3) | copy-start | bytes 1572868
  79.4 16.0 %copy-start.7 = (f32[1024]{0:T(1024)S(1)}, f32[1024]{0:T(1024)}, u32[]{:S(2)}) copy-start(f32[1024]{0:T(1024)} %param.18) | copy-start | bytes 12292

commit v8 on v6

--- a/solution.py
+++ b/solution.py
@@ -125,10 +125,13 @@
     return i, f, g, o, c_new, jnp.tanh(c_new)
 
 
-def chain_kernel(xc_ref, w_in_ref, w_rec_ref, bias_ref, out_ref, z_ref, saved_ref):
+def chain_kernel(
+    xc_ref, w_in_ref, w_rec_ref, bias_ref, out_ref, z_ref, saved_ref, turned_ref
+):
     x = xc_ref[:, :, :H].reshape(NODE, H)
     z = matmul(x, w_in_ref[...]) + bias_ref[...]
     z_ref[...] = z.astype(BF16).astype(F32)
+    turned_ref[...] = w_rec_ref[...].T
     h = jnp.zeros((PART, H), BF16)
     c = jnp.zeros((PART, H), F32)
     for t in range(SNAPS):
@@ -164,7 +167,7 @@
                 ],
                 1,
             ).astype(BF16)
-            dh = matmul(grad, w_rec_ref[...], NT)
+            dh = matmul(grad, turned_ref[...])
             dc = dc * saved_ref[t, 0]
 
 
@@ -250,7 +253,11 @@
         w_in,
         w_rec,
         bias,
-        scratch=(pltpu.VMEM((NODE, 4 * H), F32), pltpu.VMEM((SNAPS, 6, PART, H), F32)),
+        scratch=(
+            pltpu.VMEM((NODE, 4 * H), F32),
+            pltpu.VMEM((SNAPS, 6, PART, H), F32),
+            pltpu.VMEM((4 * H, H), BF16),
+        ),
     )
     back = exchange(back, "tm").reshape(NODE, 4 * H)
     hidden, grads = call(

time: 112 us -> 112 us (level)
  no operation moved by 1% of the time
where the time goes in v8:
time: 112 us; the launch traced here: 111 us
  blocking collectives  83.8 us (75%)
  starting transfers between devices  13.4 us (12%)
  Pallas kernels  8.54 us (8%)
  waiting for transfers between devices  4.2 us (4%)
    all_to_all x4, blocking collectives, exchange(): return lax.all_to_all(array, axes, 0, 0, tiled=True)  79.8 us
    all_to_all x1, starting transfers between devices, exchange(): return lax.all_to_all(array, axes, 0, 0, tiled=True)  13.4 us
    pallas_call x8, Pallas kernels, call(): pl.pallas_call(kernel, out_shape=out, scratch_shapes=list(scratch), compi...  8.54 us
    all_to_all x1, waiting for transfers between devices, exchange(): return lax.all_to_all(array, axes, 0, 0, tiled=True)  4.2 us
    all_gather x2, blocking collectives, shards(): pair = lax.all_gather(x, 'core', tiled=True)  4.01 us
  transfers between devices with their start and end apart: 1, of which 1 were waited for; matrix products, arithmetic and copies ran while one was open for 0% of the time, Pallas kernels for 1%

profile of v8, /device:TPU:6, one launch (start us, length us, event | category | flops | bytes accessed | tf_op | source)
XLA Modules:
  0.0 111.4 jit_solution(12607104356143305357)
XLA Ops:
  0.6 1.8 %shard_map.113 = (f32[32,128]{1,0:T(8,128)}, f32[8,128]{1,0:T(8,128)}) custom-call(s32[8,128]{1,0:T(8,128)} %bitcast.30, s32[8,128]{1,0:T(8,128)} %bitcast.33), custom_call_target="tpu_custom_call" | custom-call | tf_op jit(solution)/shard_map/pallas_call | solution.py:190
  2.4 13.4 %all-to-all-start = ((f32[32,1,128]{2,1,0:T(1,128)}), f32[32,1,128]{2,1,0:T(1,128)S(1)}, u32[]{:S(2)}, u32[]{:S(2)}) async-start(f32[32,1,128]{2,1,0:T(1,128)} %bitcast.32), calls=%async_computation | async-start | bytes 32768 | tf_op jit(solution)/shard_map/all_to_all | solution.py:204
  15.8 0.0 copy-start.7
  15.8 0.0 copy-start.9
  15.8 2.1 %all-gather = bf16[1,256,256]{2,1,0:T(8,128)(2,1)S(1)} all-gather(bf16[1,128,256]{2,1,0:T(8,128)(2,1)} %param.10), channel_id=2, replica_groups=mesh['tm'=8,'z'=8,'x'=4,'core'=2] {'core'}, dimensions={1}, use_global_device_ids=true | all-gather | bytes 196608 | tf_op jit(solution)/shard_map/all_gather | solution.py:228
  18.0 0.0 copy-start.8
  18.0 0.0 copy-done.7
  18.0 0.0 copy-done.9
  18.0 0.6 copy-done.8
  18.6 0.9 shard_map.114.refs_0_.comb_ref
  19.5 4.2 %all-to-all-done = f32[32,1,128]{2,1,0:T(1,128)S(1)} async-done(((f32[32,1,128]{2,1,0:T(1,128)}), f32[32,1,128]{2,1,0:T(1,128)S(1)}, u32[]{:S(2)}, u32[]{:S(2)}) %all-to-all-start) | async-done | bytes 16416 | tf_op jit(solution)/shard_map/all_to_all | solution.py:204
  23.7 0.6 shard_map.115
  24.3 0.0 copy-start.2
  24.3 0.0 copy-start.3
  24.4 25.5 %all_to_all.32 = bf16[32,40,256]{2,1,0:T(8,128)(2,1)S(1)} all-to-all(bf16[32,40,256]{2,1,0:T(8,128)(2,1)S(1)} %bitcast.23), channel_id=1, replica_groups=mesh['tm'=8,'z'=8,'x'=4,'core'=2] {'z','x'}, dimensions={0} | all-to-all | bytes 1310720 | tf_op jit(solution)/shard_map/all_to_all | solution.py:204
  49.8 0.0 copy-done.2
  49.8 0.0 copy-done.3
  49.8 0.4 shard_map.116.x_ref
  50.2 1.9 %all_gather.7.x_ref = bf16[256,256]{1,0:T(8,128)(2,1)S(1)} all-gather(bf16[128,256]{1,0:T(8,128)(2,1)S(1)} %shard_map.116.x_ref), channel_id=1, replica_groups=mesh['tm'=8,'z'=8,'x'=4,'core'=2] {'core'}, dimensions={0}, use_global_device_ids=true | all-gather | bytes 196608 | tf_op jit(solution)/shard_map/all_gather | solution.py:235
  52.1 0.3 shard_map.117
  52.5 0.0 copy-start.4
  52.5 0.0 copy-start.5
  52.5 25.4 %all_to_all.33 = bf16[32,40,256]{2,1,0:T(8,128)(2,1)S(1)} all-to-all(bf16[32,40,256]{2,1,0:T(8,128)(2,1)S(1)} %bitcast.19), channel_id=1, replica_groups=mesh['tm'=8,'z'=8,'x'=4,'core'=2] {'z','x'}, dimensions={0} | all-to-all | bytes 1310720 | tf_op jit(solution)/shard_map/all_to_all | solution.py:204
  78.0 0.0 copy-done.4
  78.0 0.0 copy-done.5
  78.0 0.0 copy-start
  78.0 0.0 copy-start.1
  78.0 0.4 shard_map.118.x_ref
  78.4 0.0 copy-start.6
  78.4 16.0 %all_to_all.34.xc_ref = bf16[8,16,512]{2,1,0:T(8,128)(2,1)S(1)} all-to-all(bf16[8,16,512]{2,1,0:T(8,128)(2,1)S(1)} %bitcast.21), channel_id=1, replica_groups=mesh['tm'=8,'z'=8,'x'=4,'core'=2] {'tm'}, dimensions={0} | all-to-all | bytes 262144 | tf_op jit(solution)/shard_map/all_to_all | solution.py:204
  94.4 0.0 copy-done
  94.4 0.0 copy-done.1
  94.4 0.0 copy-done.6
  94.4 3.0 %shard_map.119 = bf16[8,16,1024]{2,1,0:T(8,128)(2,1)S(1)} custom-call(bf16[8,16,512]{2,1,0:T(8,128)(2,1)S(1)} %all_to_all.34.xc_ref, bf16[256,1024]{1,0:T(8,128)(2,1)S(1)} %copy-done, bf16[256,1024]{1,0:T(8,128)(2,1)S(1)} %copy-done.1, f32[1,1024]{1,0:T(1,128)S(1)} %bitcast.28), custom_call_target="tpu_custom_call" | custom-call | tf_op jit(solution)/shard_map/pallas_call | solution.py:190
  97.4 12.9 %all_to_all.35 = bf16[8,16,1024]{2,1,0:T(8,128)(2,1)S(1)} all-to-all(bf16[8,16,1024]{2,1,0:T(8,128)(2,1)S(1)} %shard_map.119), channel_id=1, replica_groups=mesh['tm'=8,'z'=8,'x'=4,'core'=2] {'tm'}, dimensions={0} | all-to-all | bytes 524288 | tf_op jit(solution)/shard_map/all_to_all | solution.py:204
  110.3 1.2 %shard_map.120 = (bf16[128,256]{1,0:T(8,128)(2,1)}, bf16[128,1024]{1,0:T(8,128)(2,1)}) custom-call(bf16[128,1024]{1,0:T(8,128)(2,1)S(1)} %bitcast.22, bf16[128,512]{1,0:T(8,128)(2,1)S(1)} %shard_map.118.x_ref, bf16[256,1024]{1,0:T(8,128)(2,1)S(1)} %copy-done, bf16[256,1024]{1,0:T(8,128)(2,1)S(1)} %copy-done.1, f32[1,1024]{1,0:T(1,128)S(1)} %bitcast.29), custom_call_target="tpu_custom_call" | custom-call | tf_op jit(solution)/shard_map/pallas_call | solution.py:190
Async XLA Ops:
  2.4 21.3 %all-to-all-start = ((f32[32,1,128]{2,1,0:T(1,128)}), f32[32,1,128]{2,1,0:T(1,128)S(1)}, u32[]{:S(2)}, u32[]{:S(2)}) async-start(f32[32,1,128]{2,1,0:T(1,128)} %bitcast.32), calls=%async_computation | async-start | bytes 32768 | tf_op jit(solution)/shard_map/all_to_all | solution.py:204
  15.8 2.1 %copy-start.7 = (s32[1,1024,1]{1,2,0:T(1,128)S(1)}, s32[1,1024,1]{1,2,0:T(1,128)}, u32[]{:S(2)}) copy-start(s32[1,1024,1]{1,2,0:T(1,128)} %param.11) | copy-start | bytes 12292
  15.8 2.1 %copy-start.9 = (f32[8,128]{1,0:T(8,128)S(1)}, f32[8,128]{1,0:T(8,128)}, u32[]{:S(2)}) copy-start(f32[8,128]{1,0:T(8,128)} %get-tuple-element.14.rank_ref) | copy-start | bytes 12292
  18.0 0.7 copy-start.8
  24.3 25.5 %copy-start.2 = (bf16[1,128,256]{2,1,0:T(8,128)(2,1)S(1)}, bf16[1,128,256]{2,1,0:T(8,128)(2,1)}, u32[]{:S(2)}) copy-start(bf16[1,128,256]{2,1,0:T(8,128)(2,1)} %param.10) | copy-start | bytes 196612
  24.3 25.5 %copy-start.3 = (bf16[256,256]{1,0:T(8,128)(2,1)S(1)}, bf16[256,256]{1,0:T(8,128)(2,1)}, u32[]{:S(2)}) copy-start(bf16[256,256]{1,0:T(8,128)(2,1)} %refs_4_.1) | copy-start | bytes 393220
  52.5 25.5 %copy-start.4 = (bf16[256,256]{1,0:T(8,128)(2,1)S(1)}, bf16[256,256]{1,0:T(8,128)(2,1)}, u32[]{:S(2)}) copy-start(bf16[256,256]{1,0:T(8,128)(2,1)} %weight_ref.1) | copy-start | bytes 393220
  52.5 25.5 %copy-start.5 = (bf16[1,128,256]{2,1,0:T(8,128)(2,1)S(1)}, bf16[1,128,256]{2,1,0:T(8,128)(2,1)}, u32[]{:S(2)}) copy-start(bf16[1,128,256]{2,1,0:T(8,128)(2,1)} %param.19) | copy-start | bytes 196612
  78.0 16.4 %copy-start = (bf16[256,1024]{1,0:T(8,128)(2,1)S(1)}, bf16[256,1024]{1,0:T(8,128)(2,1)}, u32[]{:S(2)}) copy-start(bf16[256,1024]{1,0:T(8,128)(2,1)} %w_in_ref.3) | copy-start | bytes 1572868
  78.0 16.4 %copy-start.1 = (bf16[256,1024]{1,0:T(8,128)(2,1)S(1)}, bf16[256,1024]{1,0:T(8,128)(2,1)}, u32[]{:S(2)}) copy-start(bf16[256,1024]{1,0:T(8,128)(2,1)} %w_rec_ref.3) | copy-start | bytes 1572868
  78.4 16.0 %copy-start.6 = (f32[1024]{0:T(1024)S(1)}, f32[1024]{0:T(1024)}, u32[]{:S(2)}) copy-start(f32[1024]{0:T(1024)} %param.18) | copy-start | bytes 12292

commit v9 on v4

v9 whole, which is shorter than its diff:
```python
import jax
import jax.numpy as jnp
from jax import lax
from jax.experimental import pallas as pl
from jax.experimental.pallas import tpu as pltpu
from jax.sharding import Mesh
from jax.sharding import PartitionSpec as P

H = 256
KNB = 8
NODE = 128
SNAPS = 8
CHIPS = 32
CAP = 40
SLOTS = CHIPS * CAP
TM = ("t2", "t1", "t0")
LANES = 128
BF16 = jnp.bfloat16
F32 = jnp.float32
NT = ((1,), (1,))


def iota(shape, dim):
    return lax.broadcasted_iota(jnp.int32, shape, dim)


def matmul(a, b, dims=((1,), (0,))):
    return lax.dot_general(a, b, (dims, ((), ())), preferred_element_type=F32)


def fetch(pairs, sems):
    copies = [pltpu.make_async_copy(a, b, sems.at[i]) for i, (a, b) in enumerate(pairs)]
    for copy in copies:
        copy.start()
    return copies


def plan_kernel(owner_hbm, row_hbm, wanted_ref, rank_ref, owner_ref, row_ref, sems):
    for copy in fetch(((owner_hbm, owner_ref), (row_hbm, row_ref)), sems):
        copy.wait()
    owner = owner_ref[...]
    value = ((owner % 2) * NODE + row_ref[...]).astype(F32)
    chip = owner // 2
    upper = jnp.where(iota((LANES, LANES), 0) < iota((LANES, LANES), 1), 1.0, 0.0).astype(BF16)
    named = [
        jnp.where(iota((CHIPS, LANES), 0) == chip[i : i + 1, :], 1.0, 0.0) for i in range(KNB)
    ]
    before = matmul(jnp.concatenate(named, 0).astype(BF16), upper)
    base = jnp.zeros((CHIPS, 1), F32)
    wanted = jnp.zeros((CHIPS, LANES), F32)
    for i in range(KNB):
        earlier = before[i * CHIPS : (i + 1) * CHIPS] + base
        base = base + jnp.sum(named[i], 1, keepdims=True)
        rank = jnp.sum(named[i] * earlier, 0, keepdims=True)
        rank_ref[i : i + 1, :] = rank
        ranks = jnp.where(iota((LANES, LANES), 0).astype(F32) == rank, 1.0, 0.0).astype(BF16)
        wanted = wanted + matmul((named[i] * value[i : i + 1, :]).astype(BF16), ranks, NT)
    wanted_ref[...] = wanted


def column(row):
    eye = iota((NODE, NODE), 0) == iota((NODE, NODE), 1)
    return jnp.sum(jnp.where(eye, row, 0.0), 1, keepdims=True)


def comb_kernel(rank_ref, owner_ref, cnt_ref, comb_ref):
    count = column(cnt_ref[...].astype(F32))
    lane = iota((1, LANES), 1)
    sub = iota((2 * KNB, LANES), 0)
    chip = (owner_ref[...] // 2).astype(F32)
    place = jnp.zeros((NODE, 2 * KNB), F32)
    for i in range(KNB):
        group = jnp.where(iota((NODE, LANES), 0) == i * (LANES // KNB) + lane // KNB, 1.0, 0.0)
        coded = jnp.where(sub < KNB, chip[i : i + 1, :], rank_ref[i : i + 1, :])
        coded = jnp.where(sub % KNB == lane % KNB, coded, 0.0)
        place = place + matmul(group.astype(BF16), coded.astype(BF16), NT)
    place = place[:, :KNB] * CAP + place[:, KNB:]
    place = jnp.where(iota((NODE, KNB), 1).astype(F32) < count, place, -1.0)
    spot = iota((NODE, SLOTS), 1).astype(F32)
    comb = jnp.zeros((NODE, SLOTS), F32)
    for k in range(KNB):
        comb = comb + jnp.where(spot == place[:, k : k + 1], 1.0, 0.0)
    comb_ref[...] = comb.astype(BF16)


def pick_kernel(asked_ref, x_ref, pick_ref, out_ref):
    eye = jnp.where(iota((LANES, LANES), 0) == iota((LANES, LANES), 1), 1.0, 0.0).astype(BF16)
    turned = matmul(eye, asked_ref[...].astype(BF16), NT)
    col = iota((CAP, H), 1).astype(F32)
    x = x_ref[...]
    for d in range(0, CHIPS, 2):
        both = [jnp.where(turned[:CAP, e : e + 1] == col, 1.0, 0.0) for e in (d, d + 1)]
        pick = jnp.concatenate(both, 0).astype(BF16)
        pick_ref[d * CAP : (d + 2) * CAP, :] = pick
        out_ref[d * CAP : (d + 2) * CAP, :] = matmul(pick, x).astype(BF16)


def again_kernel(pick_ref, x_ref, out_ref):
    out_ref[...] = matmul(pick_ref[...], x_ref[...]).astype(BF16)


def convolved(comb_ref, arrived_ref, x_ref, cnt_ref, weight_ref):
    count = column(cnt_ref[...].astype(F32))
    summed = x_ref[...].astype(F32) + matmul(comb_ref[...], arrived_ref[...])
    agg = (summed * (1.0 / (count + 1.0))).astype(BF16)
    return jnp.maximum(matmul(agg, weight_ref[...]), 0.0).astype(BF16)


def first_kernel(*refs):
    refs[-1][...] = convolved(*refs[:-1])


def second_kernel(*refs):
    x = convolved(*refs[:-1])
    for t in range(SNAPS):
        refs[-1][t] = x


def gated(gates, c):
    i = jax.nn.sigmoid(gates[:, :H])
    f = jax.nn.sigmoid(gates[:, H : 2 * H])
    g = jnp.tanh(gates[:, 2 * H : 3 * H])
    o = jax.nn.sigmoid(gates[:, 3 * H :])
    c_new = f * c + i * g
    return i, f, g, o, c_new, jnp.tanh(c_new)


def chain_kernel(
    x_ref,
    cot_ref,
    w_in_ref,
    w_rec_ref,
    bias_ref,
    snap_ref,
    hidden_hbm,
    grads_hbm,
    saved_ref,
    turned_ref,
    hidden_ref,
    grads_ref,
    sems,
):
    snap = snap_ref[0]
    turned_ref[...] = w_rec_ref[...].T
    h = None
    c = jnp.zeros((NODE, H), F32)
    for t in range(SNAPS):
        z = (matmul(x_ref[t], w_in_ref[...]) + bias_ref[...]).astype(BF16)
        gates = z.astype(F32)
        if t > 0:
            gates = gates + matmul(h, w_rec_ref[...])
        i, f, g, o, c_new, tc = gated(gates, c)
        h = (o * tc).astype(BF16)
        hidden_ref[t] = h
        saved_ref[t, 0] = f
        saved_ref[t, 1] = o * (1.0 - tc * tc)
        saved_ref[t, 2] = g * i * (1.0 - i)
        saved_ref[t, 3] = c * f * (1.0 - f)
        saved_ref[t, 4] = i * (1.0 - g * g)
        saved_ref[t, 5] = tc * o * (1.0 - o)
        c = c_new
    copies = fetch(((hidden_ref.at[snap], hidden_hbm),), sems)
    dh = jnp.zeros((NODE, H), F32)
    dc = jnp.zeros((NODE, H), F32)
    for t in range(SNAPS - 1, -1, -1):
        at = (t & 1) * 4 + (t & 2) + (t >> 2)
        dh = dh + cot_ref[at].astype(F32)
        dc = dc + dh * saved_ref[t, 1]
        grad = jnp.concatenate(
            [dc * saved_ref[t, 2], dc * saved_ref[t, 3], dc * saved_ref[t, 4], dh * saved_ref[t, 5]],
            1,
        ).astype(BF16)
        grads_ref[t] = grad
        if t > 0:
            dh = matmul(grad, turned_ref[...])
            dc = dc * saved_ref[t, 0]
    copies += fetch(((grads_ref.at[snap], grads_hbm),), sems.at[pl.ds(1, 1)])
    for copy in copies:
        copy.wait()


def call(kernel, out, *args, scratch=(), limit=16, **more):
    return pl.pallas_call(
        kernel,
        out_shape=out,
        scratch_shapes=list(scratch),
        compiler_params=pltpu.CompilerParams(vmem_limit_bytes=limit * 1024 * 1024),
        **more,
    )(*args)


def shaped(shape, dtype=BF16):
    return jax.ShapeDtypeStruct(shape, dtype)


def exchange(array, axes):
    return lax.all_to_all(array, axes, 0, 0, tiled=True)


def shards(
    features, nbr_owner, nbr_row, counts, weight_one, weight_two, w_in, w_rec, gate_bias, cotangent
):
    chips = ("z", "x")
    hbm = pl.BlockSpec(memory_space=pltpu.HBM)
    vmem = pl.BlockSpec(memory_space=pltpu.VMEM)
    x = features[0]
    owner = nbr_owner.reshape(KNB, LANES)
    wanted, rank = call(
        plan_kernel,
        (shaped((CHIPS, LANES), F32), shaped((KNB, LANES), F32)),
        owner,
        nbr_row.reshape(KNB, LANES),
        in_specs=[hbm] * 2,
        scratch=(
            pltpu.VMEM((KNB, LANES), jnp.int32),
            pltpu.VMEM((KNB, LANES), jnp.int32),
            pltpu.SemaphoreType.DMA((2,)),
        ),
        limit=60,
    )
    asked = exchange(wanted, chips)
    pair = lax.all_gather(x, "core", tiled=True)
    asked, pair = lax.optimization_barrier((asked, pair))
    pick, outgoing = call(pick_kernel, (shaped((SLOTS, H)), shaped((SLOTS, H))), asked, pair)
    snap = lax.axis_index(TM).reshape(1).astype(jnp.int32)
    outgoing, cot, rank, snap = lax.optimization_barrier((outgoing, cotangent, rank, snap))
    arrived = exchange(outgoing.reshape(CHIPS, CAP, H), chips).reshape(SLOTS, H)
    cot = lax.all_gather(cot, "t2", tiled=True)
    cot = lax.all_gather(cot, "t1", tiled=True)
    comb = call(comb_kernel, shaped((NODE, SLOTS)), rank, owner, counts)
    comb, cot = lax.optimization_barrier((comb, cot))
    x = call(first_kernel, shaped((NODE, H)), comb, arrived, x, counts, weight_one)
    pair = lax.all_gather(x, "core", tiled=True)
    outgoing = call(again_kernel, shaped((SLOTS, H)), pick, pair)
    outgoing, cot = lax.optimization_barrier((outgoing, cot))
    arrived = exchange(outgoing.reshape(CHIPS, CAP, H), chips).reshape(SLOTS, H)
    cot = lax.all_gather(cot, "t0", tiled=True)
    comb, cot = lax.optimization_barrier((comb, cot))
    copies = call(
        second_kernel, shaped((SNAPS, NODE, H)), comb, arrived, x, counts, weight_two
    )
    xs = exchange(copies, TM)
    hidden, grads = call(
        chain_kernel,
        (shaped((NODE, H)), shaped((NODE, 4 * H))),
        xs,
        cot,
        w_in,
        w_rec,
        gate_bias.reshape(1, 4 * H),
        snap,
        in_specs=[vmem] * 5 + [pl.BlockSpec(memory_space=pltpu.SMEM)],
        out_specs=[hbm] * 2,
        scratch=(
            pltpu.VMEM((SNAPS, 6, NODE, H), F32),
            pltpu.VMEM((4 * H, H), BF16),
            pltpu.VMEM((SNAPS, NODE, H), BF16),
            pltpu.VMEM((SNAPS, NODE, 4 * H), BF16),
            pltpu.SemaphoreType.DMA((2,)),
        ),
    )
    return hidden[None], grads[None]
def solution(mesh):
    mesh = Mesh(mesh.devices.reshape(2, 2, 2, 8, 4, 2), TM + ("z", "x", "core"))
    acct = ("z", "x", "core")
    return jax.shard_map(
        shards,
        mesh=mesh,
        in_specs=(
            P(TM, acct, None),
            P(TM, acct, None),
            P(TM, acct),
            P(TM, acct),
            P(),
            P(),
            P(),
            P(),
            P(),
            P(TM, acct, None),
        ),
        out_specs=(P(TM, acct, None), P(TM, acct, None)),
        check_vma=False,
    )
```

time: 124 us -> 111 us (0.90)
  blocking collectives: 61.1 us -> 53.1 us
  waiting for transfers between devices: 22.1 us -> 17.8 us
  starting transfers between devices: 24.6 us -> 28.5 us
  Pallas kernels: 13.9 us -> 10.6 us
    all_to_all x1, blocking collectives: 29.7 us -> 23.6 us  [exchange(): return lax.all_to_all(array, axes, 0, 0, tiled=True)]
    all_to_all x3, waiting for transfers between devices: 22.1 us -> 17.8 us  [exchange(): return lax.all_to_all(array, axes, 0, 0, tiled=True)]
    all_to_all x3, starting transfers between devices: 24.6 us -> 28.5 us  [exchange(): return lax.all_to_all(array, axes, 0, 0, tiled=True)]
    pallas_call x7, Pallas kernels: 13.9 us -> 10.6 us  [call(): pl.pallas_call(kernel, out_shape=out, scratch_shapes=list(scratch), compi...]
    all_gather x1 -> x3, blocking collectives: 27.4 us -> 25.8 us  [the longest x1 8.99 us: shards(): cot = lax.all_gather(cot, 't2', tiled=True)]
  transfers between devices with their start and end apart: 3 -> 3, of which waited for: 2 -> 3; matrix products, arithmetic and copies ran while one was open for 0% -> 0% of each run, Pallas kernels for 1% -> 1%
where the time goes in v9:
time: 111 us
  blocking collectives  53.1 us (48%)
  starting transfers between devices  28.5 us (26%)
  waiting for transfers between devices  17.8 us (16%)
  Pallas kernels  10.6 us (10%)
    all_to_all x3, starting transfers between devices, exchange(): return lax.all_to_all(array, axes, 0, 0, tiled=True)  28.5 us
    all_to_all x1, blocking collectives, exchange(): return lax.all_to_all(array, axes, 0, 0, tiled=True)  23.6 us
    all_to_all x3, waiting for transfers between devices, exchange(): return lax.all_to_all(array, axes, 0, 0, tiled=True)  17.8 us
    pallas_call x7, Pallas kernels, call(): pl.pallas_call(kernel, out_shape=out, scratch_shapes=list(scratch), compi...  10.6 us
    all_gather x1, blocking collectives, shards(): cot = lax.all_gather(cot, 't2', tiled=True)  8.99 us
    all_gather x1, blocking collectives, shards(): cot = lax.all_gather(cot, 't0', tiled=True)  8.62 us
    all_gather x1, blocking collectives, shards(): cot = lax.all_gather(cot, 't1', tiled=True)  8.15 us
    all_gather x2, blocking collectives, shards(): pair = lax.all_gather(x, 'core', tiled=True)  3.8 us
  transfers between devices with their start and end apart: 3, of which 3 were waited for; matrix products, arithmetic and copies ran while one was open for 0% of the time, Pallas kernels for 1%

profile of v9, /device:TPU:6, one launch (start us, length us, event | category | flops | bytes accessed | tf_op | source)
XLA Modules:
  0.0 110.8 jit_solution(5231447903612977721)
XLA Ops:
  0.6 0.0 copy-start.2
  0.6 1.8 %shard_map.113 = (f32[32,128]{1,0:T(8,128)}, f32[8,128]{1,0:T(8,128)}) custom-call(s32[8,128]{1,0:T(8,128)} %bitcast.21, s32[8,128]{1,0:T(8,128)} %bitcast.25), custom_call_target="tpu_custom_call" | custom-call | tf_op jit(solution)/shard_map/pallas_call | solution.py:183
  2.4 13.4 %all-to-all-start = ((f32[32,1,128]{2,1,0:T(1,128)}), f32[32,1,128]{2,1,0:T(1,128)S(1)}, u32[]{:S(2)}, u32[]{:S(2)}) async-start(f32[32,1,128]{2,1,0:T(1,128)} %bitcast.24), calls=%async_computation | async-start | bytes 32768 | tf_op jit(solution)/shard_map/all_to_all | solution.py:197
  15.9 0.0 copy-done.2
  15.9 1.9 %all-gather = bf16[1,256,256]{2,1,0:T(8,128)(2,1)S(1)} all-gather(bf16[1,128,256]{2,1,0:T(8,128)(2,1)S(1)} %copy-done.2), channel_id=2, replica_groups=mesh['t2'=2,'t1'=2,'t0'=2,'z'=8,'x'=4,'core'=2] {'core'}, dimensions={1}, use_global_device_ids=true | all-gather | bytes 196608 | tf_op jit(solution)/shard_map/all_gather | solution.py:222
  17.8 6.0 %all-to-all-done = f32[32,1,128]{2,1,0:T(1,128)S(1)} async-done(((f32[32,1,128]{2,1,0:T(1,128)}), f32[32,1,128]{2,1,0:T(1,128)S(1)}, u32[]{:S(2)}, u32[]{:S(2)}) %all-to-all-start) | async-done | bytes 16416 | tf_op jit(solution)/shard_map/all_to_all | solution.py:197
  23.7 1.5 %shard_map.114 = (bf16[1280,256]{1,0:T(8,128)(2,1)S(1)}, bf16[1280,256]{1,0:T(8,128)(2,1)}) custom-call(f32[32,128]{1,0:T(8,128)S(1)} %bitcast.20, bf16[256,256]{1,0:T(8,128)(2,1)S(1)} %bitcast.18), custom_call_target="tpu_custom_call" | custom-call | tf_op jit(solution)/shard_map/pallas_call | solution.py:183
  25.2 0.0 copy-start.5
  25.2 0.0 copy-start.6
  25.2 0.0 copy-start.8
  25.2 5.7 %all-to-all-start.1 = ((bf16[32,40,256]{2,1,0:T(8,128)(2,1)}), bf16[32,40,256]{2,1,0:T(8,128)(2,1)S(1)}, u32[]{:S(2)}, u32[]{:S(2)}) async-start(bf16[32,40,256]{2,1,0:T(8,128)(2,1)} %bitcast.7), calls=%async_computation.1 | async-start | bytes 1310720 | tf_op jit(solution)/shard_map/all_to_all | solution.py:197
  30.9 0.0 copy-done.5
  31.0 0.0 copy-done.6
  31.0 0.0 copy-done.8
  31.0 0.0 copy-start.9
  31.0 0.9 shard_map.115.refs_0_
  31.9 0.0 copy-done.9
  31.9 9.0 %all_gather.16 = bf16[2,128,256]{2,1,0:T(8,128)(2,1)S(1)} all-gather(bf16[1,128,256]{2,1,0:T(8,128)(2,1)S(1)} %copy-done.9), channel_id=1, replica_groups=mesh['t2'=2,'t1'=2,'t0'=2,'z'=8,'x'=4,'core'=2] {'t2'}, dimensions={0}, use_global_device_ids=true | all-gather | bytes 196608 | tf_op jit(solution)/shard_map/all_gather | solution.py:228
  40.9 0.0 copy-start.3
  40.9 8.1 %all_gather.17 = bf16[4,128,256]{2,1,0:T(8,128)(2,1)S(1)} all-gather(bf16[2,128,256]{2,1,0:T(8,128)(2,1)S(1)} %all_gather.16), channel_id=1, replica_groups=mesh['t2'=2,'t1'=2,'t0'=2,'z'=8,'x'=4,'core'=2] {'t1'}, dimensions={0}, use_global_device_ids=true | all-gather | bytes 393216 | tf_op jit(solution)/shard_map/all_gather | solution.py:229
  49.0 0.5 all-to-all-done.1
  49.5 0.0 copy-done.3
  49.5 0.4 shard_map.116.refs_2_
  49.9 1.9 %all_gather.18.x_ref = bf16[256,256]{1,0:T(8,128)(2,1)S(1)} all-gather(bf16[128,256]{1,0:T(8,128)(2,1)S(1)} %shard_map.116.refs_2_), channel_id=1, replica_groups=mesh['t2'=2,'t1'=2,'t0'=2,'z'=8,'x'=4,'core'=2] {'core'}, dimensions={0}, use_global_device_ids=true | all-gather | bytes 196608 | tf_op jit(solution)/shard_map/all_gather | solution.py:233
  51.8 1.2 %shard_map.117 = bf16[1280,256]{1,0:T(8,128)(2,1)} custom-call(bf16[1280,256]{1,0:T(8,128)(2,1)S(1)} %get-tuple-element.28.pick_ref, bf16[256,256]{1,0:T(8,128)(2,1)S(1)} %all_gather.18.x_ref), custom_call_target="tpu_custom_call" | custom-call | tf_op jit(solution)/shard_map/pallas_call | solution.py:183
  53.0 9.4 %all-to-all-start.2 = ((bf16[32,40,256]{2,1,0:T(8,128)(2,1)}), bf16[32,40,256]{2,1,0:T(8,128)(2,1)S(1)}, u32[]{:S(2)}, u32[]{:S(2)}) async-start(bf16[32,40,256]{2,1,0:T(8,128)(2,1)} %bitcast.10), calls=%async_computation.2 | async-start | bytes 1310720 | tf_op jit(solution)/shard_map/all_to_all | solution.py:197
  62.4 0.0 copy-start.4
  62.4 8.6 %all_gather.19.cot_ref = bf16[8,128,256]{2,1,0:T(8,128)(2,1)S(1)} all-gather(bf16[4,128,256]{2,1,0:T(8,128)(2,1)S(1)} %all_gather.17), channel_id=1, replica_groups=mesh['t2'=2,'t1'=2,'t0'=2,'z'=8,'x'=4,'core'=2] {'t0'}, dimensions={0}, use_global_device_ids=true | all-gather | bytes 786432 | tf_op jit(solution)/shard_map/all_gather | solution.py:237
  71.0 11.3 %all-to-all-done.2 = bf16[32,40,256]{2,1,0:T(8,128)(2,1)S(1)} async-done(((bf16[32,40,256]{2,1,0:T(8,128)(2,1)}), bf16[32,40,256]{2,1,0:T(8,128)(2,1)S(1)}, u32[]{:S(2)}, u32[]{:S(2)}) %all-to-all-start.2) | async-done | bytes 655392 | tf_op jit(solution)/shard_map/all_to_all | solution.py:197
  82.4 0.0 copy-done.4
  82.4 0.0 copy-start.7
  82.4 0.4 shard_map.118
  82.8 0.0 copy-start
  82.8 0.0 copy-start.1
  82.8 23.6 %all_to_all.27.x_ref = bf16[8,128,256]{2,1,0:T(8,128)(2,1)S(1)} all-to-all(bf16[8,128,256]{2,1,0:T(8,128)(2,1)S(1)} %shard_map.118), channel_id=1, replica_groups=mesh['t2'=2,'t1'=2,'t0'=2,'z'=8,'x'=4,'core'=2] {'t2','t1','t0'}, dimensions={0} | all-to-all | bytes 1048576 | tf_op jit(solution)/shard_map/all_to_all | solution.py:197
  106.4 0.0 copy-done.7
  106.4 0.0 copy-done
  106.4 0.0 copy-done.1
  106.4 4.4 %shard_map.119 = (bf16[128,256]{1,0:T(8,128)(2,1)}, bf16[128,1024]{1,0:T(8,128)(2,1)}) custom-call(bf16[8,128,256]{2,1,0:T(8,128)(2,1)S(1)} %all_to_all.27.x_ref, bf16[8,128,256]{2,1,0:T(8,128)(2,1)S(1)} %all_gather.19.cot_ref, bf16[256,1024]{1,0:T(8,128)(2,1)S(1)} %copy-done, bf16[256,1024]{1,0:T(8,128)(2,1)S(1)} %copy-done.1, f32[1,1024]{1,0:T(1,128)S(1)} %bitcast.23, ...), custom_call_target="tpu_custom_call" | custom-call | tf_op jit(solution)/shard_map/pallas_call | solution.py:183
Async XLA Ops:
  0.6 15.2 %copy-start.2 = (bf16[1,128,256]{2,1,0:T(8,128)(2,1)S(1)}, bf16[1,128,256]{2,1,0:T(8,128)(2,1)}, u32[]{:S(2)}) copy-start(bf16[1,128,256]{2,1,0:T(8,128)(2,1)} %param.10) | copy-start | bytes 196612
  2.4 21.3 %all-to-all-start = ((f32[32,1,128]{2,1,0:T(1,128)}), f32[32,1,128]{2,1,0:T(1,128)S(1)}, u32[]{:S(2)}, u32[]{:S(2)}) async-start(f32[32,1,128]{2,1,0:T(1,128)} %bitcast.24), calls=%async_computation | async-start | bytes 32768 | tf_op jit(solution)/shard_map/all_to_all | solution.py:197
  25.2 5.7 %copy-start.5 = (s32[1,1024,1]{1,2,0:T(1,128)S(1)}, s32[1,1024,1]{1,2,0:T(1,128)}, u32[]{:S(2)}) copy-start(s32[1,1024,1]{1,2,0:T(1,128)} %param.11) | copy-start | bytes 12292
  25.2 5.7 %copy-start.6 = (s32[1,128]{1,0:T(1,128)S(1)}, s32[1,128]{1,0:T(1,128)}, u32[]{:S(2)}) copy-start(s32[1,128]{1,0:T(1,128)} %refs_3_.3) | copy-start | bytes 1540
  25.2 5.7 %copy-start.8 = (f32[8,128]{1,0:T(8,128)S(1)}, f32[8,128]{1,0:T(8,128)}, u32[]{:S(2)}) copy-start(f32[8,128]{1,0:T(8,128)} %get-tuple-element.25.rank_ref) | copy-start | bytes 12292
  25.2 24.3 %all-to-all-start.1 = ((bf16[32,40,256]{2,1,0:T(8,128)(2,1)}), bf16[32,40,256]{2,1,0:T(8,128)(2,1)S(1)}, u32[]{:S(2)}, u32[]{:S(2)}) async-start(bf16[32,40,256]{2,1,0:T(8,128)(2,1)} %bitcast.7), calls=%async_computation.1 | async-start | bytes 1310720 | tf_op jit(solution)/shard_map/all_to_all | solution.py:197
  31.0 0.9 copy-start.9
  40.9 8.6 %copy-start.3 = (bf16[256,256]{1,0:T(8,128)(2,1)S(1)}, bf16[256,256]{1,0:T(8,128)(2,1)}, u32[]{:S(2)}) copy-start(bf16[256,256]{1,0:T(8,128)(2,1)} %refs_4_.2) | copy-start | bytes 393220
  53.0 29.4 %all-to-all-start.2 = ((bf16[32,40,256]{2,1,0:T(8,128)(2,1)}), bf16[32,40,256]{2,1,0:T(8,128)(2,1)S(1)}, u32[]{:S(2)}, u32[]{:S(2)}) async-start(bf16[32,40,256]{2,1,0:T(8,128)(2,1)} %bitcast.10), calls=%async_computation.2 | async-start | bytes 1310720 | tf_op jit(solution)/shard_map/all_to_all | solution.py:197
  62.4 20.0 %copy-start.4 = (bf16[256,256]{1,0:T(8,128)(2,1)S(1)}, bf16[256,256]{1,0:T(8,128)(2,1)}, u32[]{:S(2)}) copy-start(bf16[256,256]{1,0:T(8,128)(2,1)} %refs_4_.3) | copy-start | bytes 393220
  82.4 24.0 %copy-start.7 = (f32[1024]{0:T(1024)S(1)}, f32[1024]{0:T(1024)}, u32[]{:S(2)}) copy-start(f32[1024]{0:T(1024)} %param.18) | copy-start | bytes 12292
  82.8 23.6 %copy-start = (bf16[256,1024]{1,0:T(8,128)(2,1)S(1)}, bf16[256,1024]{1,0:T(8,128)(2,1)}, u32[]{:S(2)}) copy-start(bf16[256,1024]{1,0:T(8,128)(2,1)} %w_in_ref.1) | copy-start | bytes 1572868
  82.8 23.6 %copy-start.1 = (bf16[256,1024]{1,0:T(8,128)(2,1)S(1)}, bf16[256,1024]{1,0:T(8,128)(2,1)}, u32[]{:S(2)}) copy-start(bf16[256,1024]{1,0:T(8,128)(2,1)} %w_rec_ref.1) | copy-start | bytes 1572868

commit v10 on v9

--- a/solution.py
+++ b/solution.py
@@ -13,6 +13,7 @@
 CHIPS = 32
 CAP = 40
 SLOTS = CHIPS * CAP
+BLOCKS = 8
 TM = ("t2", "t1", "t0")
 LANES = 128
 BF16 = jnp.bfloat16
@@ -83,20 +84,33 @@
     comb_ref[...] = comb.astype(BF16)
 
 
-def pick_kernel(asked_ref, x_ref, pick_ref, out_ref):
+def pick_kernel(asked_ref, x_ref, pick_ref, out_hbm, out_ref, sems):
     eye = jnp.where(iota((LANES, LANES), 0) == iota((LANES, LANES), 1), 1.0, 0.0).astype(BF16)
     turned = matmul(eye, asked_ref[...].astype(BF16), NT)
     col = iota((CAP, H), 1).astype(F32)
     x = x_ref[...]
-    for d in range(0, CHIPS, 2):
-        both = [jnp.where(turned[:CAP, e : e + 1] == col, 1.0, 0.0) for e in (d, d + 1)]
-        pick = jnp.concatenate(both, 0).astype(BF16)
-        pick_ref[d * CAP : (d + 2) * CAP, :] = pick
-        out_ref[d * CAP : (d + 2) * CAP, :] = matmul(pick, x).astype(BF16)
-
-
-def again_kernel(pick_ref, x_ref, out_ref):
-    out_ref[...] = matmul(pick_ref[...], x_ref[...]).astype(BF16)
+    copies = []
+    for block in range(BLOCKS):
+        rows = slice(block * SLOTS // BLOCKS, (block + 1) * SLOTS // BLOCKS)
+        chips = range(block * CHIPS // BLOCKS, (block + 1) * CHIPS // BLOCKS)
+        named = [jnp.where(turned[:CAP, d : d + 1] == col, 1.0, 0.0) for d in chips]
+        pick = jnp.concatenate(named, 0).astype(BF16)
+        pick_ref[rows, :] = pick
+        out_ref[rows, :] = matmul(pick, x).astype(BF16)
+        copies += fetch(((out_ref.at[rows, :], out_hbm.at[rows, :]),), sems.at[pl.ds(block, 1)])
+    for copy in copies:
+        copy.wait()
+
+
+def again_kernel(pick_ref, x_ref, out_hbm, out_ref, sems):
+    x = x_ref[...]
+    copies = []
+    for block in range(BLOCKS):
+        rows = slice(block * SLOTS // BLOCKS, (block + 1) * SLOTS // BLOCKS)
+        out_ref[rows, :] = matmul(pick_ref[rows, :], x).astype(BF16)
+        copies += fetch(((out_ref.at[rows, :], out_hbm.at[rows, :]),), sems.at[pl.ds(block, 1)])
+    for copy in copies:
+        copy.wait()
 
 
 def convolved(comb_ref, arrived_ref, x_ref, cnt_ref, weight_ref):
@@ -221,7 +235,15 @@
     asked = exchange(wanted, chips)
     pair = lax.all_gather(x, "core", tiled=True)
     asked, pair = lax.optimization_barrier((asked, pair))
-    pick, outgoing = call(pick_kernel, (shaped((SLOTS, H)), shaped((SLOTS, H))), asked, pair)
+    staged = (pltpu.VMEM((SLOTS, H), BF16), pltpu.SemaphoreType.DMA((BLOCKS,)))
+    pick, outgoing = call(
+        pick_kernel,
+        (shaped((SLOTS, H)), shaped((SLOTS, H))),
+        asked,
+        pair,
+        out_specs=[vmem, hbm],
+        scratch=staged,
+    )
     snap = lax.axis_index(TM).reshape(1).astype(jnp.int32)
     outgoing, cot, rank, snap = lax.optimization_barrier((outgoing, cotangent, rank, snap))
     arrived = exchange(outgoing.reshape(CHIPS, CAP, H), chips).reshape(SLOTS, H)
@@ -231,7 +253,9 @@
     comb, cot = lax.optimization_barrier((comb, cot))
     x = call(first_kernel, shaped((NODE, H)), comb, arrived, x, counts, weight_one)
     pair = lax.all_gather(x, "core", tiled=True)
-    outgoing = call(again_kernel, shaped((SLOTS, H)), pick, pair)
+    outgoing = call(
+        again_kernel, shaped((SLOTS, H)), pick, pair, out_specs=hbm, scratch=staged
+    )
     outgoing, cot = lax.optimization_barrier((outgoing, cot))
     arrived = exchange(outgoing.reshape(CHIPS, CAP, H), chips).reshape(SLOTS, H)
     cot = lax.all_gather(cot, "t0", tiled=True)

time: 111 us -> 111 us (level)
  no operation moved by 1% of the time
where the time goes in v10:
time: 111 us
  blocking collectives  53.1 us (48%)
  starting transfers between devices  28.5 us (26%)
  waiting for transfers between devices  17.8 us (16%)
  Pallas kernels  10.4 us (9%)
    all_to_all x3, starting transfers between devices, exchange(): return lax.all_to_all(array, axes, 0, 0, tiled=True)  28.5 us
    all_to_all x1, blocking collectives, exchange(): return lax.all_to_all(array, axes, 0, 0, tiled=True)  23.6 us
    all_to_all x3, waiting for transfers between devices, exchange(): return lax.all_to_all(array, axes, 0, 0, tiled=True)  17.8 us
    pallas_call x7, Pallas kernels, call(): pl.pallas_call(kernel, out_shape=out, scratch_shapes=list(scratch), compi...  10.4 us
    all_gather x1, blocking collectives, shards(): cot = lax.all_gather(cot, 't2', tiled=True)  9 us
    all_gather x1, blocking collectives, shards(): cot = lax.all_gather(cot, 't0', tiled=True)  8.62 us
    all_gather x1, blocking collectives, shards(): cot = lax.all_gather(cot, 't1', tiled=True)  8.14 us
    all_gather x2, blocking collectives, shards(): pair = lax.all_gather(x, 'core', tiled=True)  3.8 us
  transfers between devices with their start and end apart: 3, of which 3 were waited for; matrix products, arithmetic and copies ran while one was open for 0% of the time, Pallas kernels for 1%

profile of v10, /device:TPU:6, one launch (start us, length us, event | category | flops | bytes accessed | tf_op | source)
XLA Modules:
  0.0 110.7 jit_solution(1828212880528986856)
XLA Ops:
  0.6 0.0 copy-start.2
  0.6 1.8 %shard_map.113 = (f32[32,128]{1,0:T(8,128)}, f32[8,128]{1,0:T(8,128)}) custom-call(s32[8,128]{1,0:T(8,128)} %bitcast.21, s32[8,128]{1,0:T(8,128)} %bitcast.25), custom_call_target="tpu_custom_call" | custom-call | tf_op jit(solution)/shard_map/pallas_call | solution.py:197
  2.4 13.4 %all-to-all-start = ((f32[32,1,128]{2,1,0:T(1,128)}), f32[32,1,128]{2,1,0:T(1,128)S(1)}, u32[]{:S(2)}, u32[]{:S(2)}) async-start(f32[32,1,128]{2,1,0:T(1,128)} %bitcast.24), calls=%async_computation | async-start | bytes 32768 | tf_op jit(solution)/shard_map/all_to_all | solution.py:211
  15.9 0.0 copy-done.2
  15.9 1.9 %all-gather = bf16[1,256,256]{2,1,0:T(8,128)(2,1)S(1)} all-gather(bf16[1,128,256]{2,1,0:T(8,128)(2,1)S(1)} %copy-done.2), channel_id=2, replica_groups=mesh['t2'=2,'t1'=2,'t0'=2,'z'=8,'x'=4,'core'=2] {'core'}, dimensions={1}, use_global_device_ids=true | all-gather | bytes 196608 | tf_op jit(solution)/shard_map/all_gather | solution.py:236
  17.8 6.0 %all-to-all-done = f32[32,1,128]{2,1,0:T(1,128)S(1)} async-done(((f32[32,1,128]{2,1,0:T(1,128)}), f32[32,1,128]{2,1,0:T(1,128)S(1)}, u32[]{:S(2)}, u32[]{:S(2)}) %all-to-all-start) | async-done | bytes 16416 | tf_op jit(solution)/shard_map/all_to_all | solution.py:211
  23.7 1.3 %shard_map.114 = (bf16[1280,256]{1,0:T(8,128)(2,1)S(1)}, bf16[1280,256]{1,0:T(8,128)(2,1)}) custom-call(f32[32,128]{1,0:T(8,128)S(1)} %bitcast.20, bf16[256,256]{1,0:T(8,128)(2,1)S(1)} %bitcast.18), custom_call_target="tpu_custom_call" | custom-call | tf_op jit(solution)/shard_map/pallas_call | solution.py:197
  25.1 0.0 copy-start.5
  25.1 0.0 copy-start.6
  25.1 0.0 copy-start.8
  25.1 5.7 %all-to-all-start.1 = ((bf16[32,40,256]{2,1,0:T(8,128)(2,1)}), bf16[32,40,256]{2,1,0:T(8,128)(2,1)S(1)}, u32[]{:S(2)}, u32[]{:S(2)}) async-start(bf16[32,40,256]{2,1,0:T(8,128)(2,1)} %bitcast.7), calls=%async_computation.1 | async-start | bytes 1310720 | tf_op jit(solution)/shard_map/all_to_all | solution.py:211
  30.8 0.0 copy-done.5
  30.9 0.0 copy-done.6
  30.9 0.0 copy-done.8
  30.9 0.0 copy-start.9
  30.9 0.9 shard_map.115.refs_0_
  31.8 0.0 copy-done.9
  31.8 9.0 %all_gather.16 = bf16[2,128,256]{2,1,0:T(8,128)(2,1)S(1)} all-gather(bf16[1,128,256]{2,1,0:T(8,128)(2,1)S(1)} %copy-done.9), channel_id=1, replica_groups=mesh['t2'=2,'t1'=2,'t0'=2,'z'=8,'x'=4,'core'=2] {'t2'}, dimensions={0}, use_global_device_ids=true | all-gather | bytes 196608 | tf_op jit(solution)/shard_map/all_gather | solution.py:250
  40.8 0.0 copy-start.3
  40.8 8.1 %all_gather.17 = bf16[4,128,256]{2,1,0:T(8,128)(2,1)S(1)} all-gather(bf16[2,128,256]{2,1,0:T(8,128)(2,1)S(1)} %all_gather.16), channel_id=1, replica_groups=mesh['t2'=2,'t1'=2,'t0'=2,'z'=8,'x'=4,'core'=2] {'t1'}, dimensions={0}, use_global_device_ids=true | all-gather | bytes 393216 | tf_op jit(solution)/shard_map/all_gather | solution.py:251
  48.9 0.5 all-to-all-done.1
  49.4 0.0 copy-done.3
  49.4 0.4 shard_map.116.refs_2_
  49.8 1.9 %all_gather.18.x_ref = bf16[256,256]{1,0:T(8,128)(2,1)S(1)} all-gather(bf16[128,256]{1,0:T(8,128)(2,1)S(1)} %shard_map.116.refs_2_), channel_id=1, replica_groups=mesh['t2'=2,'t1'=2,'t0'=2,'z'=8,'x'=4,'core'=2] {'core'}, dimensions={0}, use_global_device_ids=true | all-gather | bytes 196608 | tf_op jit(solution)/shard_map/all_gather | solution.py:255
  51.7 1.1 %shard_map.117 = bf16[1280,256]{1,0:T(8,128)(2,1)} custom-call(bf16[1280,256]{1,0:T(8,128)(2,1)S(1)} %get-tuple-element.28.pick_ref, bf16[256,256]{1,0:T(8,128)(2,1)S(1)} %all_gather.18.x_ref), custom_call_target="tpu_custom_call" | custom-call | tf_op jit(solution)/shard_map/pallas_call | solution.py:197
  52.9 9.4 %all-to-all-start.2 = ((bf16[32,40,256]{2,1,0:T(8,128)(2,1)}), bf16[32,40,256]{2,1,0:T(8,128)(2,1)S(1)}, u32[]{:S(2)}, u32[]{:S(2)}) async-start(bf16[32,40,256]{2,1,0:T(8,128)(2,1)} %bitcast.10), calls=%async_computation.2 | async-start | bytes 1310720 | tf_op jit(solution)/shard_map/all_to_all | solution.py:211
  62.3 0.0 copy-start.4
  62.3 8.6 %all_gather.19.cot_ref = bf16[8,128,256]{2,1,0:T(8,128)(2,1)S(1)} all-gather(bf16[4,128,256]{2,1,0:T(8,128)(2,1)S(1)} %all_gather.17), channel_id=1, replica_groups=mesh['t2'=2,'t1'=2,'t0'=2,'z'=8,'x'=4,'core'=2] {'t0'}, dimensions={0}, use_global_device_ids=true | all-gather | bytes 786432 | tf_op jit(solution)/shard_map/all_gather | solution.py:261
  70.9 11.3 %all-to-all-done.2 = bf16[32,40,256]{2,1,0:T(8,128)(2,1)S(1)} async-done(((bf16[32,40,256]{2,1,0:T(8,128)(2,1)}), bf16[32,40,256]{2,1,0:T(8,128)(2,1)S(1)}, u32[]{:S(2)}, u32[]{:S(2)}) %all-to-all-start.2) | async-done | bytes 655392 | tf_op jit(solution)/shard_map/all_to_all | solution.py:211
  82.2 0.0 copy-done.4
  82.2 0.0 copy-start.7
  82.2 0.4 shard_map.118
  82.6 0.0 copy-start
  82.6 0.0 copy-start.1
  82.7 23.6 %all_to_all.27.x_ref = bf16[8,128,256]{2,1,0:T(8,128)(2,1)S(1)} all-to-all(bf16[8,128,256]{2,1,0:T(8,128)(2,1)S(1)} %shard_map.118), channel_id=1, replica_groups=mesh['t2'=2,'t1'=2,'t0'=2,'z'=8,'x'=4,'core'=2] {'t2','t1','t0'}, dimensions={0} | all-to-all | bytes 1048576 | tf_op jit(solution)/shard_map/all_to_all | solution.py:211
  106.2 0.0 copy-done.7
  106.3 0.0 copy-done
  106.3 0.0 copy-done.1
  106.3 4.4 %shard_map.119 = (bf16[128,256]{1,0:T(8,128)(2,1)}, bf16[128,1024]{1,0:T(8,128)(2,1)}) custom-call(bf16[8,128,256]{2,1,0:T(8,128)(2,1)S(1)} %all_to_all.27.x_ref, bf16[8,128,256]{2,1,0:T(8,128)(2,1)S(1)} %all_gather.19.cot_ref, bf16[256,1024]{1,0:T(8,128)(2,1)S(1)} %copy-done, bf16[256,1024]{1,0:T(8,128)(2,1)S(1)} %copy-done.1, f32[1,1024]{1,0:T(1,128)S(1)} %bitcast.23, ...), custom_call_target="tpu_custom_call" | custom-call | tf_op jit(solution)/shard_map/pallas_call | solution.py:197
Async XLA Ops:
  0.6 15.2 %copy-start.2 = (bf16[1,128,256]{2,1,0:T(8,128)(2,1)S(1)}, bf16[1,128,256]{2,1,0:T(8,128)(2,1)}, u32[]{:S(2)}) copy-start(bf16[1,128,256]{2,1,0:T(8,128)(2,1)} %param.10) | copy-start | bytes 196612
  2.4 21.3 %all-to-all-start = ((f32[32,1,128]{2,1,0:T(1,128)}), f32[32,1,128]{2,1,0:T(1,128)S(1)}, u32[]{:S(2)}, u32[]{:S(2)}) async-start(f32[32,1,128]{2,1,0:T(1,128)} %bitcast.24), calls=%async_computation | async-start | bytes 32768 | tf_op jit(solution)/shard_map/all_to_all | solution.py:211
  25.1 5.8 %copy-start.5 = (s32[1,1024,1]{1,2,0:T(1,128)S(1)}, s32[1,1024,1]{1,2,0:T(1,128)}, u32[]{:S(2)}) copy-start(s32[1,1024,1]{1,2,0:T(1,128)} %param.11) | copy-start | bytes 12292
  25.1 5.8 %copy-start.6 = (s32[1,128]{1,0:T(1,128)S(1)}, s32[1,128]{1,0:T(1,128)}, u32[]{:S(2)}) copy-start(s32[1,128]{1,0:T(1,128)} %refs_3_.3) | copy-start | bytes 1540
  25.1 5.8 %copy-start.8 = (f32[8,128]{1,0:T(8,128)S(1)}, f32[8,128]{1,0:T(8,128)}, u32[]{:S(2)}) copy-start(f32[8,128]{1,0:T(8,128)} %get-tuple-element.25.rank_ref) | copy-start | bytes 12292
  25.1 24.3 %all-to-all-start.1 = ((bf16[32,40,256]{2,1,0:T(8,128)(2,1)}), bf16[32,40,256]{2,1,0:T(8,128)(2,1)S(1)}, u32[]{:S(2)}, u32[]{:S(2)}) async-start(bf16[32,40,256]{2,1,0:T(8,128)(2,1)} %bitcast.7), calls=%async_computation.1 | async-start | bytes 1310720 | tf_op jit(solution)/shard_map/all_to_all | solution.py:211
  30.9 0.9 copy-start.9
  40.8 8.6 %copy-start.3 = (bf16[256,256]{1,0:T(8,128)(2,1)S(1)}, bf16[256,256]{1,0:T(8,128)(2,1)}, u32[]{:S(2)}) copy-start(bf16[256,256]{1,0:T(8,128)(2,1)} %refs_4_.2) | copy-start | bytes 393220
  52.9 29.4 %all-to-all-start.2 = ((bf16[32,40,256]{2,1,0:T(8,128)(2,1)}), bf16[32,40,256]{2,1,0:T(8,128)(2,1)S(1)}, u32[]{:S(2)}, u32[]{:S(2)}) async-start(bf16[32,40,256]{2,1,0:T(8,128)(2,1)} %bitcast.10), calls=%async_computation.2 | async-start | bytes 1310720 | tf_op jit(solution)/shard_map/all_to_all | solution.py:211
  62.3 20.0 %copy-start.4 = (bf16[256,256]{1,0:T(8,128)(2,1)S(1)}, bf16[256,256]{1,0:T(8,128)(2,1)}, u32[]{:S(2)}) copy-start(bf16[256,256]{1,0:T(8,128)(2,1)} %refs_4_.3) | copy-start | bytes 393220
  82.2 24.0 %copy-start.7 = (f32[1024]{0:T(1024)S(1)}, f32[1024]{0:T(1024)}, u32[]{:S(2)}) copy-start(f32[1024]{0:T(1024)} %param.18) | copy-start | bytes 12292
  82.6 23.6 %copy-start = (bf16[256,1024]{1,0:T(8,128)(2,1)S(1)}, bf16[256,1024]{1,0:T(8,128)(2,1)}, u32[]{:S(2)}) copy-start(bf16[256,1024]{1,0:T(8,128)(2,1)} %w_in_ref.1) | copy-start | bytes 1572868
  82.6 23.6 %copy-start.1 = (bf16[256,1024]{1,0:T(8,128)(2,1)S(1)}, bf16[256,1024]{1,0:T(8,128)(2,1)}, u32[]{:S(2)}) copy-start(bf16[256,1024]{1,0:T(8,128)(2,1)} %w_rec_ref.1) | copy-start | bytes 1572868

commit v11 on v10

--- a/solution.py
+++ b/solution.py
@@ -248,7 +248,6 @@
     outgoing, cot, rank, snap = lax.optimization_barrier((outgoing, cotangent, rank, snap))
     arrived = exchange(outgoing.reshape(CHIPS, CAP, H), chips).reshape(SLOTS, H)
     cot = lax.all_gather(cot, "t2", tiled=True)
-    cot = lax.all_gather(cot, "t1", tiled=True)
     comb = call(comb_kernel, shaped((NODE, SLOTS)), rank, owner, counts)
     comb, cot = lax.optimization_barrier((comb, cot))
     x = call(first_kernel, shaped((NODE, H)), comb, arrived, x, counts, weight_one)
@@ -258,6 +257,7 @@
     )
     outgoing, cot = lax.optimization_barrier((outgoing, cot))
     arrived = exchange(outgoing.reshape(CHIPS, CAP, H), chips).reshape(SLOTS, H)
+    cot = lax.all_gather(cot, "t1", tiled=True)
     cot = lax.all_gather(cot, "t0", tiled=True)
     comb, cot = lax.optimization_barrier((comb, cot))
     copies = call(

time: 111 us -> 107 us (0.964)
  starting transfers between devices: 28.5 us -> 24.7 us
    all_to_all x3, starting transfers between devices: 28.5 us -> 24.7 us  [exchange(): return lax.all_to_all(array, axes, 0, 0, tiled=True)]
    all_gather x1, blocking collectives: 8.14 us -> 9.38 us  [shards(): cot = lax.all_gather(cot, 't1', tiled=True)]
where the time goes in v11:
time: 107 us
  blocking collectives  53.7 us (50%)
  starting transfers between devices  24.7 us (23%)
  waiting for transfers between devices  17.1 us (16%)
  Pallas kernels  10.4 us (10%)
    all_to_all x3, starting transfers between devices, exchange(): return lax.all_to_all(array, axes, 0, 0, tiled=True)  24.7 us
    all_to_all x1, blocking collectives, exchange(): return lax.all_to_all(array, axes, 0, 0, tiled=True)  23.4 us
    all_to_all x3, waiting for transfers between devices, exchange(): return lax.all_to_all(array, axes, 0, 0, tiled=True)  17.1 us
    pallas_call x7, Pallas kernels, call(): pl.pallas_call(kernel, out_shape=out, scratch_shapes=list(scratch), compi...  10.4 us
    all_gather x1, blocking collectives, shards(): cot = lax.all_gather(cot, 't1', tiled=True)  9.38 us
    all_gather x1, blocking collectives, shards(): cot = lax.all_gather(cot, 't2', tiled=True)  9.13 us
    all_gather x1, blocking collectives, shards(): cot = lax.all_gather(cot, 't0', tiled=True)  7.96 us
    all_gather x2, blocking collectives, shards(): pair = lax.all_gather(x, 'core', tiled=True)  3.8 us
  transfers between devices with their start and end apart: 3, of which 3 were waited for; matrix products, arithmetic and copies ran while one was open for 0% of the time, Pallas kernels for 1%

profile of v11, /device:TPU:6, one launch (start us, length us, event | category | flops | bytes accessed | tf_op | source)
XLA Modules:
  0.0 106.7 jit_solution(16156128701639338789)
XLA Ops:
  0.6 0.0 copy-start.2
  0.6 1.8 %shard_map.113 = (f32[32,128]{1,0:T(8,128)}, f32[8,128]{1,0:T(8,128)}) custom-call(s32[8,128]{1,0:T(8,128)} %bitcast.21, s32[8,128]{1,0:T(8,128)} %bitcast.25), custom_call_target="tpu_custom_call" | custom-call | tf_op jit(solution)/shard_map/pallas_call | solution.py:197
  2.4 13.4 %all-to-all-start = ((f32[32,1,128]{2,1,0:T(1,128)}), f32[32,1,128]{2,1,0:T(1,128)S(1)}, u32[]{:S(2)}, u32[]{:S(2)}) async-start(f32[32,1,128]{2,1,0:T(1,128)} %bitcast.24), calls=%async_computation | async-start | bytes 32768 | tf_op jit(solution)/shard_map/all_to_all | solution.py:211
  15.9 0.0 copy-done.2
  15.9 1.9 %all-gather = bf16[1,256,256]{2,1,0:T(8,128)(2,1)S(1)} all-gather(bf16[1,128,256]{2,1,0:T(8,128)(2,1)S(1)} %copy-done.2), channel_id=2, replica_groups=mesh['t2'=2,'t1'=2,'t0'=2,'z'=8,'x'=4,'core'=2] {'core'}, dimensions={1}, use_global_device_ids=true | all-gather | bytes 196608 | tf_op jit(solution)/shard_map/all_gather | solution.py:236
  17.8 6.0 %all-to-all-done = f32[32,1,128]{2,1,0:T(1,128)S(1)} async-done(((f32[32,1,128]{2,1,0:T(1,128)}), f32[32,1,128]{2,1,0:T(1,128)S(1)}, u32[]{:S(2)}, u32[]{:S(2)}) %all-to-all-start) | async-done | bytes 16416 | tf_op jit(solution)/shard_map/all_to_all | solution.py:211
  23.7 1.3 %shard_map.114 = (bf16[1280,256]{1,0:T(8,128)(2,1)S(1)}, bf16[1280,256]{1,0:T(8,128)(2,1)}) custom-call(f32[32,128]{1,0:T(8,128)S(1)} %bitcast.20, bf16[256,256]{1,0:T(8,128)(2,1)S(1)} %bitcast.18), custom_call_target="tpu_custom_call" | custom-call | tf_op jit(solution)/shard_map/pallas_call | solution.py:197
  25.1 0.0 copy-start.5
  25.1 0.0 copy-start.6
  25.1 0.0 copy-start.8
  25.1 5.7 %all-to-all-start.1 = ((bf16[32,40,256]{2,1,0:T(8,128)(2,1)}), bf16[32,40,256]{2,1,0:T(8,128)(2,1)S(1)}, u32[]{:S(2)}, u32[]{:S(2)}) async-start(bf16[32,40,256]{2,1,0:T(8,128)(2,1)} %bitcast.7), calls=%async_computation.1 | async-start | bytes 1310720 | tf_op jit(solution)/shard_map/all_to_all | solution.py:211
  30.8 0.0 copy-done.5
  30.9 0.0 copy-done.6
  30.9 0.0 copy-done.8
  30.9 0.0 copy-start.9
  30.9 0.9 shard_map.115.refs_0_
  31.8 0.0 copy-done.9
  31.8 0.0 copy-start.3
  31.8 9.1 %all_gather.16 = bf16[2,128,256]{2,1,0:T(8,128)(2,1)S(1)} all-gather(bf16[1,128,256]{2,1,0:T(8,128)(2,1)S(1)} %copy-done.9), channel_id=1, replica_groups=mesh['t2'=2,'t1'=2,'t0'=2,'z'=8,'x'=4,'core'=2] {'t2'}, dimensions={0}, use_global_device_ids=true | all-gather | bytes 196608 | tf_op jit(solution)/shard_map/all_gather | solution.py:250
  40.9 8.5 %all-to-all-done.1 = bf16[32,40,256]{2,1,0:T(8,128)(2,1)S(1)} async-done(((bf16[32,40,256]{2,1,0:T(8,128)(2,1)}), bf16[32,40,256]{2,1,0:T(8,128)(2,1)S(1)}, u32[]{:S(2)}, u32[]{:S(2)}) %all-to-all-start.1) | async-done | bytes 655392 | tf_op jit(solution)/shard_map/all_to_all | solution.py:211
  49.4 0.0 copy-done.3
  49.4 0.4 shard_map.116.refs_2_
  49.8 1.9 %all_gather.17.x_ref = bf16[256,256]{1,0:T(8,128)(2,1)S(1)} all-gather(bf16[128,256]{1,0:T(8,128)(2,1)S(1)} %shard_map.116.refs_2_), channel_id=1, replica_groups=mesh['t2'=2,'t1'=2,'t0'=2,'z'=8,'x'=4,'core'=2] {'core'}, dimensions={0}, use_global_device_ids=true | all-gather | bytes 196608 | tf_op jit(solution)/shard_map/all_gather | solution.py:254
  51.7 1.1 %shard_map.117 = bf16[1280,256]{1,0:T(8,128)(2,1)} custom-call(bf16[1280,256]{1,0:T(8,128)(2,1)S(1)} %get-tuple-element.28.pick_ref, bf16[256,256]{1,0:T(8,128)(2,1)S(1)} %all_gather.17.x_ref), custom_call_target="tpu_custom_call" | custom-call | tf_op jit(solution)/shard_map/pallas_call | solution.py:197
  52.9 5.6 %all-to-all-start.2 = ((bf16[32,40,256]{2,1,0:T(8,128)(2,1)}), bf16[32,40,256]{2,1,0:T(8,128)(2,1)S(1)}, u32[]{:S(2)}, u32[]{:S(2)}) async-start(bf16[32,40,256]{2,1,0:T(8,128)(2,1)} %bitcast.10), calls=%async_computation.2 | async-start | bytes 1310720 | tf_op jit(solution)/shard_map/all_to_all | solution.py:211
  58.4 9.4 %all_gather.18 = bf16[4,128,256]{2,1,0:T(8,128)(2,1)S(1)} all-gather(bf16[2,128,256]{2,1,0:T(8,128)(2,1)S(1)} %all_gather.16), channel_id=1, replica_groups=mesh['t2'=2,'t1'=2,'t0'=2,'z'=8,'x'=4,'core'=2] {'t1'}, dimensions={0}, use_global_device_ids=true | all-gather | bytes 393216 | tf_op jit(solution)/shard_map/all_gather | solution.py:260
  67.8 0.0 copy-start.4
  67.8 8.0 %all_gather.19.cot_ref = bf16[8,128,256]{2,1,0:T(8,128)(2,1)S(1)} all-gather(bf16[4,128,256]{2,1,0:T(8,128)(2,1)S(1)} %all_gather.18), channel_id=1, replica_groups=mesh['t2'=2,'t1'=2,'t0'=2,'z'=8,'x'=4,'core'=2] {'t0'}, dimensions={0}, use_global_device_ids=true | all-gather | bytes 786432 | tf_op jit(solution)/shard_map/all_gather | solution.py:261
  75.8 2.6 %all-to-all-done.2 = bf16[32,40,256]{2,1,0:T(8,128)(2,1)S(1)} async-done(((bf16[32,40,256]{2,1,0:T(8,128)(2,1)}), bf16[32,40,256]{2,1,0:T(8,128)(2,1)S(1)}, u32[]{:S(2)}, u32[]{:S(2)}) %all-to-all-start.2) | async-done | bytes 655392 | tf_op jit(solution)/shard_map/all_to_all | solution.py:211
  78.4 0.0 copy-done.4
  78.4 0.0 copy-start.7
  78.4 0.4 shard_map.118
  78.8 0.0 copy-start
  78.8 0.0 copy-start.1
  78.8 23.4 %all_to_all.27.x_ref = bf16[8,128,256]{2,1,0:T(8,128)(2,1)S(1)} all-to-all(bf16[8,128,256]{2,1,0:T(8,128)(2,1)S(1)} %shard_map.118), channel_id=1, replica_groups=mesh['t2'=2,'t1'=2,'t0'=2,'z'=8,'x'=4,'core'=2] {'t2','t1','t0'}, dimensions={0} | all-to-all | bytes 1048576 | tf_op jit(solution)/shard_map/all_to_all | solution.py:211
  102.2 0.0 copy-done.7
  102.2 0.0 copy-done
  102.2 0.0 copy-done.1
  102.2 4.4 %shard_map.119 = (bf16[128,256]{1,0:T(8,128)(2,1)}, bf16[128,1024]{1,0:T(8,128)(2,1)}) custom-call(bf16[8,128,256]{2,1,0:T(8,128)(2,1)S(1)} %all_to_all.27.x_ref, bf16[8,128,256]{2,1,0:T(8,128)(2,1)S(1)} %all_gather.19.cot_ref, bf16[256,1024]{1,0:T(8,128)(2,1)S(1)} %copy-done, bf16[256,1024]{1,0:T(8,128)(2,1)S(1)} %copy-done.1, f32[1,1024]{1,0:T(1,128)S(1)} %bitcast.23, ...), custom_call_target="tpu_custom_call" | custom-call | tf_op jit(solution)/shard_map/pallas_call | solution.py:197
Async XLA Ops:
  0.6 15.2 %copy-start.2 = (bf16[1,128,256]{2,1,0:T(8,128)(2,1)S(1)}, bf16[1,128,256]{2,1,0:T(8,128)(2,1)}, u32[]{:S(2)}) copy-start(bf16[1,128,256]{2,1,0:T(8,128)(2,1)} %param.10) | copy-start | bytes 196612
  2.4 21.3 %all-to-all-start = ((f32[32,1,128]{2,1,0:T(1,128)}), f32[32,1,128]{2,1,0:T(1,128)S(1)}, u32[]{:S(2)}, u32[]{:S(2)}) async-start(f32[32,1,128]{2,1,0:T(1,128)} %bitcast.24), calls=%async_computation | async-start | bytes 32768 | tf_op jit(solution)/shard_map/all_to_all | solution.py:211
  25.1 5.8 %copy-start.5 = (s32[1,1024,1]{1,2,0:T(1,128)S(1)}, s32[1,1024,1]{1,2,0:T(1,128)}, u32[]{:S(2)}) copy-start(s32[1,1024,1]{1,2,0:T(1,128)} %param.11) | copy-start | bytes 12292
  25.1 5.8 %copy-start.6 = (s32[1,128]{1,0:T(1,128)S(1)}, s32[1,128]{1,0:T(1,128)}, u32[]{:S(2)}) copy-start(s32[1,128]{1,0:T(1,128)} %refs_3_.3) | copy-start | bytes 1540
  25.1 5.8 %copy-start.8 = (f32[8,128]{1,0:T(8,128)S(1)}, f32[8,128]{1,0:T(8,128)}, u32[]{:S(2)}) copy-start(f32[8,128]{1,0:T(8,128)} %get-tuple-element.25.rank_ref) | copy-start | bytes 12292
  25.1 24.3 %all-to-all-start.1 = ((bf16[32,40,256]{2,1,0:T(8,128)(2,1)}), bf16[32,40,256]{2,1,0:T(8,128)(2,1)S(1)}, u32[]{:S(2)}, u32[]{:S(2)}) async-start(bf16[32,40,256]{2,1,0:T(8,128)(2,1)} %bitcast.7), calls=%async_computation.1 | async-start | bytes 1310720 | tf_op jit(solution)/shard_map/all_to_all | solution.py:211
  30.9 0.9 copy-start.9
  31.8 17.6 %copy-start.3 = (bf16[256,256]{1,0:T(8,128)(2,1)S(1)}, bf16[256,256]{1,0:T(8,128)(2,1)}, u32[]{:S(2)}) copy-start(bf16[256,256]{1,0:T(8,128)(2,1)} %refs_4_.2) | copy-start | bytes 393220
  52.9 25.5 %all-to-all-start.2 = ((bf16[32,40,256]{2,1,0:T(8,128)(2,1)}), bf16[32,40,256]{2,1,0:T(8,128)(2,1)S(1)}, u32[]{:S(2)}, u32[]{:S(2)}) async-start(bf16[32,40,256]{2,1,0:T(8,128)(2,1)} %bitcast.10), calls=%async_computation.2 | async-start | bytes 1310720 | tf_op jit(solution)/shard_map/all_to_all | solution.py:211
  67.8 10.6 %copy-start.4 = (bf16[256,256]{1,0:T(8,128)(2,1)S(1)}, bf16[256,256]{1,0:T(8,128)(2,1)}, u32[]{:S(2)}) copy-start(bf16[256,256]{1,0:T(8,128)(2,1)} %refs_4_.3) | copy-start | bytes 393220
  78.4 23.8 %copy-start.7 = (f32[1024]{0:T(1024)S(1)}, f32[1024]{0:T(1024)}, u32[]{:S(2)}) copy-start(f32[1024]{0:T(1024)} %param.18) | copy-start | bytes 12292
  78.8 23.4 %copy-start = (bf16[256,1024]{1,0:T(8,128)(2,1)S(1)}, bf16[256,1024]{1,0:T(8,128)(2,1)}, u32[]{:S(2)}) copy-start(bf16[256,1024]{1,0:T(8,128)(2,1)} %w_in_ref.1) | copy-start | bytes 1572868
  78.8 23.4 %copy-start.1 = (bf16[256,1024]{1,0:T(8,128)(2,1)S(1)}, bf16[256,1024]{1,0:T(8,128)(2,1)}, u32[]{:S(2)}) copy-start(bf16[256,1024]{1,0:T(8,128)(2,1)} %w_rec_ref.1) | copy-start | bytes 1572868

commit v12 on v11

--- a/solution.py
+++ b/solution.py
@@ -139,6 +139,10 @@
     return i, f, g, o, c_new, jnp.tanh(c_new)
 
 
+def turned_bits(t):
+    return (t & 1) * 4 + (t & 2) + (t >> 2)
+
+
 def chain_kernel(
     x_ref,
     cot_ref,
@@ -159,7 +163,7 @@
     h = None
     c = jnp.zeros((NODE, H), F32)
     for t in range(SNAPS):
-        z = (matmul(x_ref[t], w_in_ref[...]) + bias_ref[...]).astype(BF16)
+        z = (matmul(x_ref[turned_bits(t)], w_in_ref[...]) + bias_ref[...]).astype(BF16)
         gates = z.astype(F32)
         if t > 0:
             gates = gates + matmul(h, w_rec_ref[...])
@@ -177,8 +181,7 @@
     dh = jnp.zeros((NODE, H), F32)
     dc = jnp.zeros((NODE, H), F32)
     for t in range(SNAPS - 1, -1, -1):
-        at = (t & 1) * 4 + (t & 2) + (t >> 2)
-        dh = dh + cot_ref[at].astype(F32)
+        dh = dh + cot_ref[turned_bits(t)].astype(F32)
         dc = dc + dh * saved_ref[t, 1]
         grad = jnp.concatenate(
             [dc * saved_ref[t, 2], dc * saved_ref[t, 3], dc * saved_ref[t, 4], dh * saved_ref[t, 5]],
@@ -263,7 +266,7 @@
     copies = call(
         second_kernel, shaped((SNAPS, NODE, H)), comb, arrived, x, counts, weight_two
     )
-    xs = exchange(copies, TM)
+    xs = exchange(copies, TM[::-1])
     hidden, grads = call(
         chain_kernel,
         (shaped((NODE, H)), shaped((NODE, 4 * H))),

time: 107 us -> 105 us (0.981)
  blocking collectives: 53.7 us -> 51.2 us
    all_to_all x1, blocking collectives: 23.4 us -> 20.9 us  [exchange(): return lax.all_to_all(array, axes, 0, 0, tiled=True)]
where the time goes in v12:
time: 105 us; the launch traced here: 104 us
  blocking collectives  51.2 us (49%)
  starting transfers between devices  24.7 us (24%)
  waiting for transfers between devices  17.1 us (16%)
  Pallas kernels  10.4 us (10%)
    all_to_all x3, starting transfers between devices, exchange(): return lax.all_to_all(array, axes, 0, 0, tiled=True)  24.7 us
    all_to_all x1, blocking collectives, exchange(): return lax.all_to_all(array, axes, 0, 0, tiled=True)  20.9 us
    all_to_all x3, waiting for transfers between devices, exchange(): return lax.all_to_all(array, axes, 0, 0, tiled=True)  17.1 us
    pallas_call x7, Pallas kernels, call(): pl.pallas_call(kernel, out_shape=out, scratch_shapes=list(scratch), compi...  10.4 us
    all_gather x1, blocking collectives, shards(): cot = lax.all_gather(cot, 't1', tiled=True)  9.38 us
    all_gather x1, blocking collectives, shards(): cot = lax.all_gather(cot, 't2', tiled=True)  9.13 us
    all_gather x1, blocking collectives, shards(): cot = lax.all_gather(cot, 't0', tiled=True)  7.96 us
    all_gather x2, blocking collectives, shards(): pair = lax.all_gather(x, 'core', tiled=True)  3.8 us
  transfers between devices with their start and end apart: 3, of which 3 were waited for; matrix products, arithmetic and copies ran while one was open for 0% of the time, Pallas kernels for 1%

profile of v12, /device:TPU:6, one launch (start us, length us, event | category | flops | bytes accessed | tf_op | source)
XLA Modules:
  0.0 104.2 jit_solution(6046385585292780033)
XLA Ops:
  0.6 0.0 copy-start.2
  0.6 1.8 %shard_map.113 = (f32[32,128]{1,0:T(8,128)}, f32[8,128]{1,0:T(8,128)}) custom-call(s32[8,128]{1,0:T(8,128)} %bitcast.21, s32[8,128]{1,0:T(8,128)} %bitcast.25), custom_call_target="tpu_custom_call" | custom-call | tf_op jit(solution)/shard_map/pallas_call | solution.py:200
  2.4 13.4 %all-to-all-start = ((f32[32,1,128]{2,1,0:T(1,128)}), f32[32,1,128]{2,1,0:T(1,128)S(1)}, u32[]{:S(2)}, u32[]{:S(2)}) async-start(f32[32,1,128]{2,1,0:T(1,128)} %bitcast.24), calls=%async_computation | async-start | bytes 32768 | tf_op jit(solution)/shard_map/all_to_all | solution.py:214
  15.9 0.0 copy-done.2
  15.9 1.9 %all-gather = bf16[1,256,256]{2,1,0:T(8,128)(2,1)S(1)} all-gather(bf16[1,128,256]{2,1,0:T(8,128)(2,1)S(1)} %copy-done.2), channel_id=2, replica_groups=mesh['t2'=2,'t1'=2,'t0'=2,'z'=8,'x'=4,'core'=2] {'core'}, dimensions={1}, use_global_device_ids=true | all-gather | bytes 196608 | tf_op jit(solution)/shard_map/all_gather | solution.py:239
  17.8 6.0 %all-to-all-done = f32[32,1,128]{2,1,0:T(1,128)S(1)} async-done(((f32[32,1,128]{2,1,0:T(1,128)}), f32[32,1,128]{2,1,0:T(1,128)S(1)}, u32[]{:S(2)}, u32[]{:S(2)}) %all-to-all-start) | async-done | bytes 16416 | tf_op jit(solution)/shard_map/all_to_all | solution.py:214
  23.7 1.3 %shard_map.114 = (bf16[1280,256]{1,0:T(8,128)(2,1)S(1)}, bf16[1280,256]{1,0:T(8,128)(2,1)}) custom-call(f32[32,128]{1,0:T(8,128)S(1)} %bitcast.20, bf16[256,256]{1,0:T(8,128)(2,1)S(1)} %bitcast.18), custom_call_target="tpu_custom_call" | custom-call | tf_op jit(solution)/shard_map/pallas_call | solution.py:200
  25.1 0.0 copy-start.5
  25.1 0.0 copy-start.6
  25.1 0.0 copy-start.8
  25.1 5.7 %all-to-all-start.1 = ((bf16[32,40,256]{2,1,0:T(8,128)(2,1)}), bf16[32,40,256]{2,1,0:T(8,128)(2,1)S(1)}, u32[]{:S(2)}, u32[]{:S(2)}) async-start(bf16[32,40,256]{2,1,0:T(8,128)(2,1)} %bitcast.7), calls=%async_computation.1 | async-start | bytes 1310720 | tf_op jit(solution)/shard_map/all_to_all | solution.py:214
  30.8 0.0 copy-done.5
  30.9 0.0 copy-done.6
  30.9 0.0 copy-done.8
  30.9 0.0 copy-start.9
  30.9 0.9 shard_map.115.refs_0_
  31.8 0.0 copy-done.9
  31.8 0.0 copy-start.3
  31.8 9.1 %all_gather.16 = bf16[2,128,256]{2,1,0:T(8,128)(2,1)S(1)} all-gather(bf16[1,128,256]{2,1,0:T(8,128)(2,1)S(1)} %copy-done.9), channel_id=1, replica_groups=mesh['t2'=2,'t1'=2,'t0'=2,'z'=8,'x'=4,'core'=2] {'t2'}, dimensions={0}, use_global_device_ids=true | all-gather | bytes 196608 | tf_op jit(solution)/shard_map/all_gather | solution.py:253
  40.9 8.5 %all-to-all-done.1 = bf16[32,40,256]{2,1,0:T(8,128)(2,1)S(1)} async-done(((bf16[32,40,256]{2,1,0:T(8,128)(2,1)}), bf16[32,40,256]{2,1,0:T(8,128)(2,1)S(1)}, u32[]{:S(2)}, u32[]{:S(2)}) %all-to-all-start.1) | async-done | bytes 655392 | tf_op jit(solution)/shard_map/all_to_all | solution.py:214
  49.4 0.0 copy-done.3
  49.4 0.4 shard_map.116.refs_2_
  49.8 1.9 %all_gather.17.x_ref = bf16[256,256]{1,0:T(8,128)(2,1)S(1)} all-gather(bf16[128,256]{1,0:T(8,128)(2,1)S(1)} %shard_map.116.refs_2_), channel_id=1, replica_groups=mesh['t2'=2,'t1'=2,'t0'=2,'z'=8,'x'=4,'core'=2] {'core'}, dimensions={0}, use_global_device_ids=true | all-gather | bytes 196608 | tf_op jit(solution)/shard_map/all_gather | solution.py:257
  51.7 1.1 %shard_map.117 = bf16[1280,256]{1,0:T(8,128)(2,1)} custom-call(bf16[1280,256]{1,0:T(8,128)(2,1)S(1)} %get-tuple-element.28.pick_ref, bf16[256,256]{1,0:T(8,128)(2,1)S(1)} %all_gather.17.x_ref), custom_call_target="tpu_custom_call" | custom-call | tf_op jit(solution)/shard_map/pallas_call | solution.py:200
  52.9 5.6 %all-to-all-start.2 = ((bf16[32,40,256]{2,1,0:T(8,128)(2,1)}), bf16[32,40,256]{2,1,0:T(8,128)(2,1)S(1)}, u32[]{:S(2)}, u32[]{:S(2)}) async-start(bf16[32,40,256]{2,1,0:T(8,128)(2,1)} %bitcast.10), calls=%async_computation.2 | async-start | bytes 1310720 | tf_op jit(solution)/shard_map/all_to_all | solution.py:214
  58.4 9.4 %all_gather.18 = bf16[4,128,256]{2,1,0:T(8,128)(2,1)S(1)} all-gather(bf16[2,128,256]{2,1,0:T(8,128)(2,1)S(1)} %all_gather.16), channel_id=1, replica_groups=mesh['t2'=2,'t1'=2,'t0'=2,'z'=8,'x'=4,'core'=2] {'t1'}, dimensions={0}, use_global_device_ids=true | all-gather | bytes 393216 | tf_op jit(solution)/shard_map/all_gather | solution.py:263
  67.8 0.0 copy-start.4
  67.8 8.0 %all_gather.19.cot_ref = bf16[8,128,256]{2,1,0:T(8,128)(2,1)S(1)} all-gather(bf16[4,128,256]{2,1,0:T(8,128)(2,1)S(1)} %all_gather.18), channel_id=1, replica_groups=mesh['t2'=2,'t1'=2,'t0'=2,'z'=8,'x'=4,'core'=2] {'t0'}, dimensions={0}, use_global_device_ids=true | all-gather | bytes 786432 | tf_op jit(solution)/shard_map/all_gather | solution.py:264
  75.8 2.6 %all-to-all-done.2 = bf16[32,40,256]{2,1,0:T(8,128)(2,1)S(1)} async-done(((bf16[32,40,256]{2,1,0:T(8,128)(2,1)}), bf16[32,40,256]{2,1,0:T(8,128)(2,1)S(1)}, u32[]{:S(2)}, u32[]{:S(2)}) %all-to-all-start.2) | async-done | bytes 655392 | tf_op jit(solution)/shard_map/all_to_all | solution.py:214
  78.4 0.0 copy-done.4
  78.4 0.0 copy-start.7
  78.4 0.4 shard_map.118
  78.8 0.0 copy-start
  78.8 0.0 copy-start.1
  78.8 20.9 %all_to_all.27.x_ref = bf16[8,128,256]{2,1,0:T(8,128)(2,1)S(1)} all-to-all(bf16[8,128,256]{2,1,0:T(8,128)(2,1)S(1)} %shard_map.118), channel_id=1, replica_groups=mesh['t2'=2,'t1'=2,'t0'=2,'z'=8,'x'=4,'core'=2] {'t0','t1','t2'}, dimensions={0} | all-to-all | bytes 1048576 | tf_op jit(solution)/shard_map/all_to_all | solution.py:214
  99.7 0.0 copy-done.7
  99.7 0.0 copy-done
  99.7 0.0 copy-done.1
  99.7 4.4 %shard_map.119 = (bf16[128,256]{1,0:T(8,128)(2,1)}, bf16[128,1024]{1,0:T(8,128)(2,1)}) custom-call(bf16[8,128,256]{2,1,0:T(8,128)(2,1)S(1)} %all_to_all.27.x_ref, bf16[8,128,256]{2,1,0:T(8,128)(2,1)S(1)} %all_gather.19.cot_ref, bf16[256,1024]{1,0:T(8,128)(2,1)S(1)} %copy-done, bf16[256,1024]{1,0:T(8,128)(2,1)S(1)} %copy-done.1, f32[1,1024]{1,0:T(1,128)S(1)} %bitcast.23, ...), custom_call_target="tpu_custom_call" | custom-call | tf_op jit(solution)/shard_map/pallas_call | solution.py:200
Async XLA Ops:
  0.6 15.2 %copy-start.2 = (bf16[1,128,256]{2,1,0:T(8,128)(2,1)S(1)}, bf16[1,128,256]{2,1,0:T(8,128)(2,1)}, u32[]{:S(2)}) copy-start(bf16[1,128,256]{2,1,0:T(8,128)(2,1)} %param.10) | copy-start | bytes 196612
  2.4 21.3 %all-to-all-start = ((f32[32,1,128]{2,1,0:T(1,128)}), f32[32,1,128]{2,1,0:T(1,128)S(1)}, u32[]{:S(2)}, u32[]{:S(2)}) async-start(f32[32,1,128]{2,1,0:T(1,128)} %bitcast.24), calls=%async_computation | async-start | bytes 32768 | tf_op jit(solution)/shard_map/all_to_all | solution.py:214
  25.1 5.8 %copy-start.5 = (s32[1,1024,1]{1,2,0:T(1,128)S(1)}, s32[1,1024,1]{1,2,0:T(1,128)}, u32[]{:S(2)}) copy-start(s32[1,1024,1]{1,2,0:T(1,128)} %param.11) | copy-start | bytes 12292
  25.1 5.8 %copy-start.6 = (s32[1,128]{1,0:T(1,128)S(1)}, s32[1,128]{1,0:T(1,128)}, u32[]{:S(2)}) copy-start(s32[1,128]{1,0:T(1,128)} %refs_3_.3) | copy-start | bytes 1540
  25.1 5.8 %copy-start.8 = (f32[8,128]{1,0:T(8,128)S(1)}, f32[8,128]{1,0:T(8,128)}, u32[]{:S(2)}) copy-start(f32[8,128]{1,0:T(8,128)} %get-tuple-element.25.rank_ref) | copy-start | bytes 12292
  25.1 24.3 %all-to-all-start.1 = ((bf16[32,40,256]{2,1,0:T(8,128)(2,1)}), bf16[32,40,256]{2,1,0:T(8,128)(2,1)S(1)}, u32[]{:S(2)}, u32[]{:S(2)}) async-start(bf16[32,40,256]{2,1,0:T(8,128)(2,1)} %bitcast.7), calls=%async_computation.1 | async-start | bytes 1310720 | tf_op jit(solution)/shard_map/all_to_all | solution.py:214
  30.9 0.9 copy-start.9
  31.8 17.6 %copy-start.3 = (bf16[256,256]{1,0:T(8,128)(2,1)S(1)}, bf16[256,256]{1,0:T(8,128)(2,1)}, u32[]{:S(2)}) copy-start(bf16[256,256]{1,0:T(8,128)(2,1)} %refs_4_.2) | copy-start | bytes 393220
  52.9 25.5 %all-to-all-start.2 = ((bf16[32,40,256]{2,1,0:T(8,128)(2,1)}), bf16[32,40,256]{2,1,0:T(8,128)(2,1)S(1)}, u32[]{:S(2)}, u32[]{:S(2)}) async-start(bf16[32,40,256]{2,1,0:T(8,128)(2,1)} %bitcast.10), calls=%async_computation.2 | async-start | bytes 1310720 | tf_op jit(solution)/shard_map/all_to_all | solution.py:214
  67.8 10.6 %copy-start.4 = (bf16[256,256]{1,0:T(8,128)(2,1)S(1)}, bf16[256,256]{1,0:T(8,128)(2,1)}, u32[]{:S(2)}) copy-start(bf16[256,256]{1,0:T(8,128)(2,1)} %refs_4_.3) | copy-start | bytes 393220
  78.4 21.3 %copy-start.7 = (f32[1024]{0:T(1024)S(1)}, f32[1024]{0:T(1024)}, u32[]{:S(2)}) copy-start(f32[1024]{0:T(1024)} %param.18) | copy-start | bytes 12292
  78.8 20.9 %copy-start = (bf16[256,1024]{1,0:T(8,128)(2,1)S(1)}, bf16[256,1024]{1,0:T(8,128)(2,1)}, u32[]{:S(2)}) copy-start(bf16[256,1024]{1,0:T(8,128)(2,1)} %w_in_ref.1) | copy-start | bytes 1572868
  78.8 20.9 %copy-start.1 = (bf16[256,1024]{1,0:T(8,128)(2,1)S(1)}, bf16[256,1024]{1,0:T(8,128)(2,1)}, u32[]{:S(2)}) copy-start(bf16[256,1024]{1,0:T(8,128)(2,1)} %w_rec_ref.1) | copy-start | bytes 1572868

commit v13 on v12

--- a/solution.py
+++ b/solution.py
@@ -36,12 +36,16 @@
     return copies
 
 
+def chip_of(owner):
+    return owner // 2 % 4 * 8 + owner // 8
+
+
 def plan_kernel(owner_hbm, row_hbm, wanted_ref, rank_ref, owner_ref, row_ref, sems):
     for copy in fetch(((owner_hbm, owner_ref), (row_hbm, row_ref)), sems):
         copy.wait()
     owner = owner_ref[...]
     value = ((owner % 2) * NODE + row_ref[...]).astype(F32)
-    chip = owner // 2
+    chip = chip_of(owner)
     upper = jnp.where(iota((LANES, LANES), 0) < iota((LANES, LANES), 1), 1.0, 0.0).astype(BF16)
     named = [
         jnp.where(iota((CHIPS, LANES), 0) == chip[i : i + 1, :], 1.0, 0.0) for i in range(KNB)
@@ -68,7 +72,7 @@
     count = column(cnt_ref[...].astype(F32))
     lane = iota((1, LANES), 1)
     sub = iota((2 * KNB, LANES), 0)
-    chip = (owner_ref[...] // 2).astype(F32)
+    chip = chip_of(owner_ref[...]).astype(F32)
     place = jnp.zeros((NODE, 2 * KNB), F32)
     for i in range(KNB):
         group = jnp.where(iota((NODE, LANES), 0) == i * (LANES // KNB) + lane // KNB, 1.0, 0.0)
@@ -217,7 +221,7 @@
 def shards(
     features, nbr_owner, nbr_row, counts, weight_one, weight_two, w_in, w_rec, gate_bias, cotangent
 ):
-    chips = ("z", "x")
+    chips = ("x", "z")
     hbm = pl.BlockSpec(memory_space=pltpu.HBM)
     vmem = pl.BlockSpec(memory_space=pltpu.VMEM)
     x = features[0]

time: 105 us -> 105 us (level); the launches traced: 104 us -> 103 us
  waiting for transfers between devices: 17.1 us -> 13 us
  starting transfers between devices: 24.7 us -> 26.7 us
    all_to_all x3, waiting for transfers between devices: 17.1 us -> 13 us  [exchange(): return lax.all_to_all(array, axes, 0, 0, tiled=True)]
    all_to_all x3, starting transfers between devices: 24.7 us -> 26.7 us  [exchange(): return lax.all_to_all(array, axes, 0, 0, tiled=True)]
where the time goes in v13:
time: 105 us; the launch traced here: 103 us
  blocking collectives  52 us (50%)
  starting transfers between devices  26.7 us (25%)
  waiting for transfers between devices  13 us (12%)
  Pallas kernels  10.3 us (10%)
    all_to_all x3, starting transfers between devices, exchange(): return lax.all_to_all(array, axes, 0, 0, tiled=True)  26.7 us
    all_to_all x1, blocking collectives, exchange(): return lax.all_to_all(array, axes, 0, 0, tiled=True)  21.8 us
    all_to_all x3, waiting for transfers between devices, exchange(): return lax.all_to_all(array, axes, 0, 0, tiled=True)  13 us
    pallas_call x7, Pallas kernels, call(): pl.pallas_call(kernel, out_shape=out, scratch_shapes=list(scratch), compi...  10.3 us
    all_gather x1, blocking collectives, shards(): cot = lax.all_gather(cot, 't1', tiled=True)  9.38 us
    all_gather x1, blocking collectives, shards(): cot = lax.all_gather(cot, 't2', tiled=True)  9.13 us
    all_gather x1, blocking collectives, shards(): cot = lax.all_gather(cot, 't0', tiled=True)  7.96 us
    all_gather x2, blocking collectives, shards(): pair = lax.all_gather(x, 'core', tiled=True)  3.8 us
  transfers between devices with their start and end apart: 3, of which 3 were waited for; matrix products, arithmetic and copies ran while one was open for 0% of the time, Pallas kernels for 1%

profile of v13, /device:TPU:6, one launch (start us, length us, event | category | flops | bytes accessed | tf_op | source)
XLA Modules:
  0.0 103.0 jit_solution(16755487338113708592)
XLA Ops:
  0.6 0.0 copy-start.2
  0.6 1.8 %shard_map.113 = (f32[32,128]{1,0:T(8,128)}, f32[8,128]{1,0:T(8,128)}) custom-call(s32[8,128]{1,0:T(8,128)} %bitcast.21, s32[8,128]{1,0:T(8,128)} %bitcast.25), custom_call_target="tpu_custom_call" | custom-call | tf_op jit(solution)/shard_map/pallas_call | solution.py:204
  2.4 13.5 %all-to-all-start = ((f32[32,1,128]{2,1,0:T(1,128)}), f32[32,1,128]{2,1,0:T(1,128)S(1)}, u32[]{:S(2)}, u32[]{:S(2)}) async-start(f32[32,1,128]{2,1,0:T(1,128)} %bitcast.24), calls=%async_computation | async-start | bytes 32768 | tf_op jit(solution)/shard_map/all_to_all | solution.py:218
  15.9 0.0 copy-done.2
  15.9 1.9 %all-gather = bf16[1,256,256]{2,1,0:T(8,128)(2,1)S(1)} all-gather(bf16[1,128,256]{2,1,0:T(8,128)(2,1)S(1)} %copy-done.2), channel_id=2, replica_groups=mesh['t2'=2,'t1'=2,'t0'=2,'z'=8,'x'=4,'core'=2] {'core'}, dimensions={1}, use_global_device_ids=true | all-gather | bytes 196608 | tf_op jit(solution)/shard_map/all_gather | solution.py:243
  17.8 5.9 %all-to-all-done = f32[32,1,128]{2,1,0:T(1,128)S(1)} async-done(((f32[32,1,128]{2,1,0:T(1,128)}), f32[32,1,128]{2,1,0:T(1,128)S(1)}, u32[]{:S(2)}, u32[]{:S(2)}) %all-to-all-start) | async-done | bytes 16416 | tf_op jit(solution)/shard_map/all_to_all | solution.py:218
  23.7 1.3 %shard_map.114 = (bf16[1280,256]{1,0:T(8,128)(2,1)S(1)}, bf16[1280,256]{1,0:T(8,128)(2,1)}) custom-call(f32[32,128]{1,0:T(8,128)S(1)} %bitcast.20, bf16[256,256]{1,0:T(8,128)(2,1)S(1)} %bitcast.18), custom_call_target="tpu_custom_call" | custom-call | tf_op jit(solution)/shard_map/pallas_call | solution.py:204
  25.1 0.0 copy-start.5
  25.1 0.0 copy-start.6
  25.1 0.0 copy-start.8
  25.1 5.9 %all-to-all-start.1 = ((bf16[32,40,256]{2,1,0:T(8,128)(2,1)}), bf16[32,40,256]{2,1,0:T(8,128)(2,1)S(1)}, u32[]{:S(2)}, u32[]{:S(2)}) async-start(bf16[32,40,256]{2,1,0:T(8,128)(2,1)} %bitcast.7), calls=%async_computation.1 | async-start | bytes 1310720 | tf_op jit(solution)/shard_map/all_to_all | solution.py:218
  31.0 0.0 copy-done.5
  31.1 0.0 copy-done.6
  31.1 0.0 copy-done.8
  31.1 0.0 copy-start.9
  31.1 0.9 shard_map.115.refs_0_
  32.0 0.0 copy-done.9
  32.0 0.0 copy-start.3
  32.0 9.1 %all_gather.16 = bf16[2,128,256]{2,1,0:T(8,128)(2,1)S(1)} all-gather(bf16[1,128,256]{2,1,0:T(8,128)(2,1)S(1)} %copy-done.9), channel_id=1, replica_groups=mesh['t2'=2,'t1'=2,'t0'=2,'z'=8,'x'=4,'core'=2] {'t2'}, dimensions={0}, use_global_device_ids=true | all-gather | bytes 196608 | tf_op jit(solution)/shard_map/all_gather | solution.py:257
  41.1 6.8 %all-to-all-done.1 = bf16[32,40,256]{2,1,0:T(8,128)(2,1)S(1)} async-done(((bf16[32,40,256]{2,1,0:T(8,128)(2,1)}), bf16[32,40,256]{2,1,0:T(8,128)(2,1)S(1)}, u32[]{:S(2)}, u32[]{:S(2)}) %all-to-all-start.1) | async-done | bytes 655392 | tf_op jit(solution)/shard_map/all_to_all | solution.py:218
  47.9 0.0 copy-done.3
  47.9 0.4 shard_map.116.refs_2_
  48.3 1.9 %all_gather.17.x_ref = bf16[256,256]{1,0:T(8,128)(2,1)S(1)} all-gather(bf16[128,256]{1,0:T(8,128)(2,1)S(1)} %shard_map.116.refs_2_), channel_id=1, replica_groups=mesh['t2'=2,'t1'=2,'t0'=2,'z'=8,'x'=4,'core'=2] {'core'}, dimensions={0}, use_global_device_ids=true | all-gather | bytes 196608 | tf_op jit(solution)/shard_map/all_gather | solution.py:261
  50.2 1.1 %shard_map.117 = bf16[1280,256]{1,0:T(8,128)(2,1)} custom-call(bf16[1280,256]{1,0:T(8,128)(2,1)S(1)} %get-tuple-element.28.pick_ref, bf16[256,256]{1,0:T(8,128)(2,1)S(1)} %all_gather.17.x_ref), custom_call_target="tpu_custom_call" | custom-call | tf_op jit(solution)/shard_map/pallas_call | solution.py:204
  51.3 7.3 %all-to-all-start.2 = ((bf16[32,40,256]{2,1,0:T(8,128)(2,1)}), bf16[32,40,256]{2,1,0:T(8,128)(2,1)S(1)}, u32[]{:S(2)}, u32[]{:S(2)}) async-start(bf16[32,40,256]{2,1,0:T(8,128)(2,1)} %bitcast.10), calls=%async_computation.2 | async-start | bytes 1310720 | tf_op jit(solution)/shard_map/all_to_all | solution.py:218
  58.6 9.4 %all_gather.18 = bf16[4,128,256]{2,1,0:T(8,128)(2,1)S(1)} all-gather(bf16[2,128,256]{2,1,0:T(8,128)(2,1)S(1)} %all_gather.16), channel_id=1, replica_groups=mesh['t2'=2,'t1'=2,'t0'=2,'z'=8,'x'=4,'core'=2] {'t1'}, dimensions={0}, use_global_device_ids=true | all-gather | bytes 393216 | tf_op jit(solution)/shard_map/all_gather | solution.py:267
  68.0 0.0 copy-start.4
  68.0 8.0 %all_gather.19.cot_ref = bf16[8,128,256]{2,1,0:T(8,128)(2,1)S(1)} all-gather(bf16[4,128,256]{2,1,0:T(8,128)(2,1)S(1)} %all_gather.18), channel_id=1, replica_groups=mesh['t2'=2,'t1'=2,'t0'=2,'z'=8,'x'=4,'core'=2] {'t0'}, dimensions={0}, use_global_device_ids=true | all-gather | bytes 786432 | tf_op jit(solution)/shard_map/all_gather | solution.py:268
  76.0 0.3 all-to-all-done.2
  76.3 0.0 copy-done.4
  76.3 0.0 copy-start.7
  76.3 0.4 shard_map.118
  76.7 0.0 copy-start
  76.7 0.0 copy-start.1
  76.8 21.8 %all_to_all.27.x_ref = bf16[8,128,256]{2,1,0:T(8,128)(2,1)S(1)} all-to-all(bf16[8,128,256]{2,1,0:T(8,128)(2,1)S(1)} %shard_map.118), channel_id=1, replica_groups=mesh['t2'=2,'t1'=2,'t0'=2,'z'=8,'x'=4,'core'=2] {'t0','t1','t2'}, dimensions={0} | all-to-all | bytes 1048576 | tf_op jit(solution)/shard_map/all_to_all | solution.py:218
  98.5 0.0 copy-done.7
  98.5 0.0 copy-done
  98.5 0.0 copy-done.1
  98.5 4.4 %shard_map.119 = (bf16[128,256]{1,0:T(8,128)(2,1)}, bf16[128,1024]{1,0:T(8,128)(2,1)}) custom-call(bf16[8,128,256]{2,1,0:T(8,128)(2,1)S(1)} %all_to_all.27.x_ref, bf16[8,128,256]{2,1,0:T(8,128)(2,1)S(1)} %all_gather.19.cot_ref, bf16[256,1024]{1,0:T(8,128)(2,1)S(1)} %copy-done, bf16[256,1024]{1,0:T(8,128)(2,1)S(1)} %copy-done.1, f32[1,1024]{1,0:T(1,128)S(1)} %bitcast.23, ...), custom_call_target="tpu_custom_call" | custom-call | tf_op jit(solution)/shard_map/pallas_call | solution.py:204
Async XLA Ops:
  0.6 15.3 %copy-start.2 = (bf16[1,128,256]{2,1,0:T(8,128)(2,1)S(1)}, bf16[1,128,256]{2,1,0:T(8,128)(2,1)}, u32[]{:S(2)}) copy-start(bf16[1,128,256]{2,1,0:T(8,128)(2,1)} %param.10) | copy-start | bytes 196612
  2.4 21.3 %all-to-all-start = ((f32[32,1,128]{2,1,0:T(1,128)}), f32[32,1,128]{2,1,0:T(1,128)S(1)}, u32[]{:S(2)}, u32[]{:S(2)}) async-start(f32[32,1,128]{2,1,0:T(1,128)} %bitcast.24), calls=%async_computation | async-start | bytes 32768 | tf_op jit(solution)/shard_map/all_to_all | solution.py:218
  25.1 6.0 %copy-start.5 = (s32[1,1024,1]{1,2,0:T(1,128)S(1)}, s32[1,1024,1]{1,2,0:T(1,128)}, u32[]{:S(2)}) copy-start(s32[1,1024,1]{1,2,0:T(1,128)} %param.11) | copy-start | bytes 12292
  25.1 6.0 %copy-start.6 = (s32[1,128]{1,0:T(1,128)S(1)}, s32[1,128]{1,0:T(1,128)}, u32[]{:S(2)}) copy-start(s32[1,128]{1,0:T(1,128)} %refs_3_.3) | copy-start | bytes 1540
  25.1 6.0 %copy-start.8 = (f32[8,128]{1,0:T(8,128)S(1)}, f32[8,128]{1,0:T(8,128)}, u32[]{:S(2)}) copy-start(f32[8,128]{1,0:T(8,128)} %get-tuple-element.25.rank_ref) | copy-start | bytes 12292
  25.1 22.8 %all-to-all-start.1 = ((bf16[32,40,256]{2,1,0:T(8,128)(2,1)}), bf16[32,40,256]{2,1,0:T(8,128)(2,1)S(1)}, u32[]{:S(2)}, u32[]{:S(2)}) async-start(bf16[32,40,256]{2,1,0:T(8,128)(2,1)} %bitcast.7), calls=%async_computation.1 | async-start | bytes 1310720 | tf_op jit(solution)/shard_map/all_to_all | solution.py:218
  31.1 0.9 copy-start.9
  32.0 15.9 %copy-start.3 = (bf16[256,256]{1,0:T(8,128)(2,1)S(1)}, bf16[256,256]{1,0:T(8,128)(2,1)}, u32[]{:S(2)}) copy-start(bf16[256,256]{1,0:T(8,128)(2,1)} %refs_4_.2) | copy-start | bytes 393220
  51.3 25.0 %all-to-all-start.2 = ((bf16[32,40,256]{2,1,0:T(8,128)(2,1)}), bf16[32,40,256]{2,1,0:T(8,128)(2,1)S(1)}, u32[]{:S(2)}, u32[]{:S(2)}) async-start(bf16[32,40,256]{2,1,0:T(8,128)(2,1)} %bitcast.10), calls=%async_computation.2 | async-start | bytes 1310720 | tf_op jit(solution)/shard_map/all_to_all | solution.py:218
  68.0 8.3 %copy-start.4 = (bf16[256,256]{1,0:T(8,128)(2,1)S(1)}, bf16[256,256]{1,0:T(8,128)(2,1)}, u32[]{:S(2)}) copy-start(bf16[256,256]{1,0:T(8,128)(2,1)} %refs_4_.3) | copy-start | bytes 393220
  76.3 22.2 %copy-start.7 = (f32[1024]{0:T(1024)S(1)}, f32[1024]{0:T(1024)}, u32[]{:S(2)}) copy-start(f32[1024]{0:T(1024)} %param.18) | copy-start | bytes 12292
  76.7 21.8 %copy-start = (bf16[256,1024]{1,0:T(8,128)(2,1)S(1)}, bf16[256,1024]{1,0:T(8,128)(2,1)}, u32[]{:S(2)}) copy-start(bf16[256,1024]{1,0:T(8,128)(2,1)} %w_in_ref.1) | copy-start | bytes 1572868
  76.7 21.8 %copy-start.1 = (bf16[256,1024]{1,0:T(8,128)(2,1)S(1)}, bf16[256,1024]{1,0:T(8,128)(2,1)}, u32[]{:S(2)}) copy-start(bf16[256,1024]{1,0:T(8,128)(2,1)} %w_rec_ref.1) | copy-start | bytes 1572868

commit v14 on v13

--- a/solution.py
+++ b/solution.py
@@ -16,6 +16,7 @@
 BLOCKS = 8
 TM = ("t2", "t1", "t0")
 LANES = 128
+RANKS = 64
 BF16 = jnp.bfloat16
 F32 = jnp.float32
 NT = ((1,), (1,))
@@ -52,13 +53,13 @@
     ]
     before = matmul(jnp.concatenate(named, 0).astype(BF16), upper)
     base = jnp.zeros((CHIPS, 1), F32)
-    wanted = jnp.zeros((CHIPS, LANES), F32)
+    wanted = jnp.zeros((CHIPS, RANKS), F32)
     for i in range(KNB):
         earlier = before[i * CHIPS : (i + 1) * CHIPS] + base
         base = base + jnp.sum(named[i], 1, keepdims=True)
         rank = jnp.sum(named[i] * earlier, 0, keepdims=True)
         rank_ref[i : i + 1, :] = rank
-        ranks = jnp.where(iota((LANES, LANES), 0).astype(F32) == rank, 1.0, 0.0).astype(BF16)
+        ranks = jnp.where(iota((RANKS, LANES), 0).astype(F32) == rank, 1.0, 0.0).astype(BF16)
         wanted = wanted + matmul((named[i] * value[i : i + 1, :]).astype(BF16), ranks, NT)
     wanted_ref[...] = wanted
 
@@ -89,7 +90,7 @@
 
 
 def pick_kernel(asked_ref, x_ref, pick_ref, out_hbm, out_ref, sems):
-    eye = jnp.where(iota((LANES, LANES), 0) == iota((LANES, LANES), 1), 1.0, 0.0).astype(BF16)
+    eye = jnp.where(iota((RANKS, RANKS), 0) == iota((RANKS, RANKS), 1), 1.0, 0.0).astype(BF16)
     turned = matmul(eye, asked_ref[...].astype(BF16), NT)
     col = iota((CAP, H), 1).astype(F32)
     x = x_ref[...]
@@ -228,7 +229,7 @@
     owner = nbr_owner.reshape(KNB, LANES)
     wanted, rank = call(
         plan_kernel,
-        (shaped((CHIPS, LANES), F32), shaped((KNB, LANES), F32)),
+        (shaped((CHIPS, RANKS), F32), shaped((KNB, LANES), F32)),
         owner,
         nbr_row.reshape(KNB, LANES),
         in_specs=[hbm] * 2,

time: 105 us -> 104 us (level)
  no operation moved by 1% of the time
where the time goes in v14:
time: 104 us; the launch traced here: 103 us
  blocking collectives  52.2 us (50%)
  starting transfers between devices  26.7 us (26%)
  waiting for transfers between devices  12.8 us (12%)
  Pallas kernels  10.3 us (10%)
    all_to_all x3, starting transfers between devices, exchange(): return lax.all_to_all(array, axes, 0, 0, tiled=True)  26.7 us
    all_to_all x1, blocking collectives, exchange(): return lax.all_to_all(array, axes, 0, 0, tiled=True)  21.8 us
    all_to_all x3, waiting for transfers between devices, exchange(): return lax.all_to_all(array, axes, 0, 0, tiled=True)  12.8 us
    pallas_call x7, Pallas kernels, call(): pl.pallas_call(kernel, out_shape=out, scratch_shapes=list(scratch), compi...  10.3 us
    all_gather x1, blocking collectives, shards(): cot = lax.all_gather(cot, 't1', tiled=True)  9.38 us
    all_gather x1, blocking collectives, shards(): cot = lax.all_gather(cot, 't2', tiled=True)  9.13 us
    all_gather x1, blocking collectives, shards(): cot = lax.all_gather(cot, 't0', tiled=True)  7.96 us
    all_gather x2, blocking collectives, shards(): pair = lax.all_gather(x, 'core', tiled=True)  4.01 us
  transfers between devices with their start and end apart: 3, of which 3 were waited for; matrix products, arithmetic and copies ran while one was open for 0% of the time, Pallas kernels for 1%

profile of v14, /device:TPU:6, one launch (start us, length us, event | category | flops | bytes accessed | tf_op | source)
XLA Modules:
  0.0 102.9 jit_solution(15645546373242604662)
XLA Ops:
  0.6 1.7 %shard_map.113 = (f32[32,64]{1,0:T(8,128)}, f32[8,128]{1,0:T(8,128)}) custom-call(s32[8,128]{1,0:T(8,128)} %bitcast.21, s32[8,128]{1,0:T(8,128)} %bitcast.25), custom_call_target="tpu_custom_call" | custom-call | tf_op jit(solution)/shard_map/pallas_call | solution.py:205
  2.3 13.5 %all-to-all-start = ((f32[32,1,64]{2,1,0:T(1,128)}), f32[32,1,64]{2,1,0:T(1,128)S(1)}, u32[]{:S(2)}, u32[]{:S(2)}) async-start(f32[32,1,64]{2,1,0:T(1,128)} %bitcast.24), calls=%async_computation | async-start | bytes 32768 | tf_op jit(solution)/shard_map/all_to_all | solution.py:219
  15.8 2.1 %all-gather = bf16[1,256,256]{2,1,0:T(8,128)(2,1)S(1)} all-gather(bf16[1,128,256]{2,1,0:T(8,128)(2,1)} %param.10), channel_id=2, replica_groups=mesh['t2'=2,'t1'=2,'t0'=2,'z'=8,'x'=4,'core'=2] {'core'}, dimensions={1}, use_global_device_ids=true | all-gather | bytes 196608 | tf_op jit(solution)/shard_map/all_gather | solution.py:244
  17.9 5.7 %all-to-all-done = f32[32,1,64]{2,1,0:T(1,128)S(1)} async-done(((f32[32,1,64]{2,1,0:T(1,128)}), f32[32,1,64]{2,1,0:T(1,128)S(1)}, u32[]{:S(2)}, u32[]{:S(2)}) %all-to-all-start) | async-done | bytes 8224 | tf_op jit(solution)/shard_map/all_to_all | solution.py:219
  23.6 1.3 %shard_map.114 = (bf16[1280,256]{1,0:T(8,128)(2,1)S(1)}, bf16[1280,256]{1,0:T(8,128)(2,1)}) custom-call(f32[32,64]{1,0:T(8,128)S(1)} %bitcast.20, bf16[256,256]{1,0:T(8,128)(2,1)S(1)} %bitcast.18), custom_call_target="tpu_custom_call" | custom-call | tf_op jit(solution)/shard_map/pallas_call | solution.py:205
  25.0 0.0 copy-start.5
  25.0 0.0 copy-start.6
  25.0 0.0 copy-start.8
  25.0 5.9 %all-to-all-start.1 = ((bf16[32,40,256]{2,1,0:T(8,128)(2,1)}), bf16[32,40,256]{2,1,0:T(8,128)(2,1)S(1)}, u32[]{:S(2)}, u32[]{:S(2)}) async-start(bf16[32,40,256]{2,1,0:T(8,128)(2,1)} %bitcast.7), calls=%async_computation.1 | async-start | bytes 1310720 | tf_op jit(solution)/shard_map/all_to_all | solution.py:219
  30.9 0.0 copy-done.5
  31.0 0.0 copy-done.6
  31.0 0.0 copy-done.8
  31.0 0.0 copy-start.9
  31.0 0.9 shard_map.115.refs_0_
  31.9 0.0 copy-done.9
  31.9 0.0 copy-start.2
  31.9 0.0 copy-start.3
  31.9 9.1 %all_gather.16 = bf16[2,128,256]{2,1,0:T(8,128)(2,1)S(1)} all-gather(bf16[1,128,256]{2,1,0:T(8,128)(2,1)S(1)} %copy-done.9), channel_id=1, replica_groups=mesh['t2'=2,'t1'=2,'t0'=2,'z'=8,'x'=4,'core'=2] {'t2'}, dimensions={0}, use_global_device_ids=true | all-gather | bytes 196608 | tf_op jit(solution)/shard_map/all_gather | solution.py:258
  41.0 6.8 %all-to-all-done.1 = bf16[32,40,256]{2,1,0:T(8,128)(2,1)S(1)} async-done(((bf16[32,40,256]{2,1,0:T(8,128)(2,1)}), bf16[32,40,256]{2,1,0:T(8,128)(2,1)S(1)}, u32[]{:S(2)}, u32[]{:S(2)}) %all-to-all-start.1) | async-done | bytes 655392 | tf_op jit(solution)/shard_map/all_to_all | solution.py:219
  47.8 0.0 copy-done.2
  47.8 0.0 copy-done.3
  47.8 0.4 shard_map.116.refs_2_
  48.2 1.9 %all_gather.17.x_ref = bf16[256,256]{1,0:T(8,128)(2,1)S(1)} all-gather(bf16[128,256]{1,0:T(8,128)(2,1)S(1)} %shard_map.116.refs_2_), channel_id=1, replica_groups=mesh['t2'=2,'t1'=2,'t0'=2,'z'=8,'x'=4,'core'=2] {'core'}, dimensions={0}, use_global_device_ids=true | all-gather | bytes 196608 | tf_op jit(solution)/shard_map/all_gather | solution.py:262
  50.1 1.1 %shard_map.117 = bf16[1280,256]{1,0:T(8,128)(2,1)} custom-call(bf16[1280,256]{1,0:T(8,128)(2,1)S(1)} %get-tuple-element.28.pick_ref, bf16[256,256]{1,0:T(8,128)(2,1)S(1)} %all_gather.17.x_ref), custom_call_target="tpu_custom_call" | custom-call | tf_op jit(solution)/shard_map/pallas_call | solution.py:205
  51.2 7.3 %all-to-all-start.2 = ((bf16[32,40,256]{2,1,0:T(8,128)(2,1)}), bf16[32,40,256]{2,1,0:T(8,128)(2,1)S(1)}, u32[]{:S(2)}, u32[]{:S(2)}) async-start(bf16[32,40,256]{2,1,0:T(8,128)(2,1)} %bitcast.10), calls=%async_computation.2 | async-start | bytes 1310720 | tf_op jit(solution)/shard_map/all_to_all | solution.py:219
  58.5 9.4 %all_gather.18 = bf16[4,128,256]{2,1,0:T(8,128)(2,1)S(1)} all-gather(bf16[2,128,256]{2,1,0:T(8,128)(2,1)S(1)} %all_gather.16), channel_id=1, replica_groups=mesh['t2'=2,'t1'=2,'t0'=2,'z'=8,'x'=4,'core'=2] {'t1'}, dimensions={0}, use_global_device_ids=true | all-gather | bytes 393216 | tf_op jit(solution)/shard_map/all_gather | solution.py:268
  67.9 0.0 copy-start.4
  67.9 8.0 %all_gather.19.cot_ref = bf16[8,128,256]{2,1,0:T(8,128)(2,1)S(1)} all-gather(bf16[4,128,256]{2,1,0:T(8,128)(2,1)S(1)} %all_gather.18), channel_id=1, replica_groups=mesh['t2'=2,'t1'=2,'t0'=2,'z'=8,'x'=4,'core'=2] {'t0'}, dimensions={0}, use_global_device_ids=true | all-gather | bytes 786432 | tf_op jit(solution)/shard_map/all_gather | solution.py:269
  75.9 0.3 all-to-all-done.2
  76.2 0.0 copy-done.4
  76.2 0.0 copy-start.7
  76.2 0.4 shard_map.118
  76.6 0.0 copy-start
  76.6 0.0 copy-start.1
  76.7 21.8 %all_to_all.27.x_ref = bf16[8,128,256]{2,1,0:T(8,128)(2,1)S(1)} all-to-all(bf16[8,128,256]{2,1,0:T(8,128)(2,1)S(1)} %shard_map.118), channel_id=1, replica_groups=mesh['t2'=2,'t1'=2,'t0'=2,'z'=8,'x'=4,'core'=2] {'t0','t1','t2'}, dimensions={0} | all-to-all | bytes 1048576 | tf_op jit(solution)/shard_map/all_to_all | solution.py:219
  98.4 0.0 copy-done.7
  98.4 0.0 copy-done
  98.4 0.0 copy-done.1
  98.4 4.4 %shard_map.119 = (bf16[128,256]{1,0:T(8,128)(2,1)}, bf16[128,1024]{1,0:T(8,128)(2,1)}) custom-call(bf16[8,128,256]{2,1,0:T(8,128)(2,1)S(1)} %all_to_all.27.x_ref, bf16[8,128,256]{2,1,0:T(8,128)(2,1)S(1)} %all_gather.19.cot_ref, bf16[256,1024]{1,0:T(8,128)(2,1)S(1)} %copy-done, bf16[256,1024]{1,0:T(8,128)(2,1)S(1)} %copy-done.1, f32[1,1024]{1,0:T(1,128)S(1)} %bitcast.23, ...), custom_call_target="tpu_custom_call" | custom-call | tf_op jit(solution)/shard_map/pallas_call | solution.py:205
Async XLA Ops:
  2.3 21.3 %all-to-all-start = ((f32[32,1,64]{2,1,0:T(1,128)}), f32[32,1,64]{2,1,0:T(1,128)S(1)}, u32[]{:S(2)}, u32[]{:S(2)}) async-start(f32[32,1,64]{2,1,0:T(1,128)} %bitcast.24), calls=%async_computation | async-start | bytes 32768 | tf_op jit(solution)/shard_map/all_to_all | solution.py:219
  25.0 6.0 %copy-start.5 = (s32[1,1024,1]{1,2,0:T(1,128)S(1)}, s32[1,1024,1]{1,2,0:T(1,128)}, u32[]{:S(2)}) copy-start(s32[1,1024,1]{1,2,0:T(1,128)} %param.11) | copy-start | bytes 12292
  25.0 6.0 %copy-start.6 = (s32[1,128]{1,0:T(1,128)S(1)}, s32[1,128]{1,0:T(1,128)}, u32[]{:S(2)}) copy-start(s32[1,128]{1,0:T(1,128)} %refs_3_.3) | copy-start | bytes 1540
  25.0 6.0 %copy-start.8 = (f32[8,128]{1,0:T(8,128)S(1)}, f32[8,128]{1,0:T(8,128)}, u32[]{:S(2)}) copy-start(f32[8,128]{1,0:T(8,128)} %get-tuple-element.25.rank_ref) | copy-start | bytes 12292
  25.0 22.8 %all-to-all-start.1 = ((bf16[32,40,256]{2,1,0:T(8,128)(2,1)}), bf16[32,40,256]{2,1,0:T(8,128)(2,1)S(1)}, u32[]{:S(2)}, u32[]{:S(2)}) async-start(bf16[32,40,256]{2,1,0:T(8,128)(2,1)} %bitcast.7), calls=%async_computation.1 | async-start | bytes 1310720 | tf_op jit(solution)/shard_map/all_to_all | solution.py:219
  31.0 0.9 copy-start.9
  31.9 15.9 %copy-start.2 = (bf16[1,128,256]{2,1,0:T(8,128)(2,1)S(1)}, bf16[1,128,256]{2,1,0:T(8,128)(2,1)}, u32[]{:S(2)}) copy-start(bf16[1,128,256]{2,1,0:T(8,128)(2,1)} %param.10) | copy-start | bytes 196612
  31.9 15.9 %copy-start.3 = (bf16[256,256]{1,0:T(8,128)(2,1)S(1)}, bf16[256,256]{1,0:T(8,128)(2,1)}, u32[]{:S(2)}) copy-start(bf16[256,256]{1,0:T(8,128)(2,1)} %refs_4_.2) | copy-start | bytes 393220
  51.2 25.0 %all-to-all-start.2 = ((bf16[32,40,256]{2,1,0:T(8,128)(2,1)}), bf16[32,40,256]{2,1,0:T(8,128)(2,1)S(1)}, u32[]{:S(2)}, u32[]{:S(2)}) async-start(bf16[32,40,256]{2,1,0:T(8,128)(2,1)} %bitcast.10), calls=%async_computation.2 | async-start | bytes 1310720 | tf_op jit(solution)/shard_map/all_to_all | solution.py:219
  67.9 8.3 %copy-start.4 = (bf16[256,256]{1,0:T(8,128)(2,1)S(1)}, bf16[256,256]{1,0:T(8,128)(2,1)}, u32[]{:S(2)}) copy-start(bf16[256,256]{1,0:T(8,128)(2,1)} %refs_4_.3) | copy-start | bytes 393220
  76.2 22.2 %copy-start.7 = (f32[1024]{0:T(1024)S(1)}, f32[1024]{0:T(1024)}, u32[]{:S(2)}) copy-start(f32[1024]{0:T(1024)} %param.18) | copy-start | bytes 12292
  76.6 21.8 %copy-start = (bf16[256,1024]{1,0:T(8,128)(2,1)S(1)}, bf16[256,1024]{1,0:T(8,128)(2,1)}, u32[]{:S(2)}) copy-start(bf16[256,1024]{1,0:T(8,128)(2,1)} %w_in_ref.1) | copy-start | bytes 1572868
  76.6 21.8 %copy-start.1 = (bf16[256,1024]{1,0:T(8,128)(2,1)S(1)}, bf16[256,1024]{1,0:T(8,128)(2,1)}, u32[]{:S(2)}) copy-start(bf16[256,1024]{1,0:T(8,128)(2,1)} %w_rec_ref.1) | copy-start | bytes 1572868
